TPU v7x, 32 devices: a whole 2x2x4 slice. The times are simulated.
32 devices in a mesh: mode: 4 (over z), tile: 8 (over y, x, core).
Axes of the slice: x: 2, y: 2, z: 4, core: 2. Of those that a mesh axis runs over, the one named last changes fastest.
Arguments:
- distribution: float32 [4096, 64, 128], P('mode', 'tile'), may hold values from -6 to 6
- courant: float32 [2, 4096], P(None, 'mode'), may hold values from -0.4 to 0.4
- relax_rate: float32 [4096], P('mode'), may hold values from 0.1 to 2
- scatter_weight: float32 [4096, 4096], P('mode'), may hold values from -0.09375 to 0.09375
- cell_flags: int32 [64, 128], P('tile'), may hold values 0 or 1
Outputs:
- evolved: float32 [4096, 64, 128], P('mode', 'tile')
All inputs are finite; a program needn't handle non-finite values. No bound on the sum of `cell_flags` on one device may be relied on, other than what follows from the above.
Results may differ from a plain program's by a relative error of at most 0.0012.
Values may be sent and summed in bfloat16 or wider, within the bound.
No kernel may reach another device: no remote copies, remote signals or barrier semaphores. Data moves between devices by JAX's collectives and lax.ppermute only.
A program may use at most 128 MiB of HBM per device.

v0:
```python
import jax
import jax.numpy as jnp
from jax import lax
from jax.sharding import PartitionSpec as P

time_step = 0.25
wall_rate = 2.0


def extended(block, sides, width):
    for axis, dim in sides:
        count = lax.axis_size(axis)
        forward = [(i, i + 1) for i in range(count - 1)]
        backward = [(target, source) for source, target in forward]
        low = lax.ppermute(
            lax.slice_in_dim(block, block.shape[dim] - width, None, axis=dim), axis, forward
        )
        high = lax.ppermute(lax.slice_in_dim(block, 0, width, axis=dim), axis, backward)
        block = jnp.concatenate([low, block, high], axis=dim)
    return block


def transport_rows(padded, cx, cy):
    full = jnp.pad(padded, ((0, 0), (0, 0), (2, 2)))
    centre = full[:, 2:-2, 2:-2]
    back_x = 1.5 * centre - 2.0 * full[:, 1:-3, 2:-2] + 0.5 * full[:, :-4, 2:-2]
    fwd_x = -1.5 * centre + 2.0 * full[:, 3:-1, 2:-2] - 0.5 * full[:, 4:, 2:-2]
    back_y = 1.5 * centre - 2.0 * full[:, 2:-2, 1:-3] + 0.5 * full[:, 2:-2, :-4]
    fwd_y = -1.5 * centre + 2.0 * full[:, 2:-2, 3:-1] - 0.5 * full[:, 2:-2, 4:]
    return (
        jnp.maximum(cx, 0.0) * back_x
        + jnp.minimum(cx, 0.0) * fwd_x
        + jnp.maximum(cy, 0.0) * back_y
        + jnp.minimum(cy, 0.0) * fwd_y
    )


def collide(field, scatter_weight):
    rounded = field.astype(jnp.bfloat16)
    count = rounded.shape[1] * rounded.shape[2]
    flat = rounded.reshape(rounded.shape[0], count)
    gain = jnp.dot(
        scatter_weight,
        lax.all_gather(flat, "mode", axis=0, tiled=True).astype(jnp.float32),
        precision=lax.Precision.HIGHEST,
        preferred_element_type=jnp.float32,
    )
    return gain.reshape(field.shape)


def update(centre, moved, gain, rate, flags):
    return centre - moved + time_step * (gain - rate * centre - wall_rate * flags * centre)


def body(distribution, courant, relax_rate, scatter_weight, cell_flags):
    cx = courant[0][:, None, None]
    cy = courant[1][:, None, None]
    rate = relax_rate[:, None, None]
    flags = cell_flags.astype(jnp.float32)[None]
    field = distribution
    for step in range(2):
        padded = extended(field, (("tile", 1),), 2)
        moved = transport_rows(padded, cx, cy)
        gain = collide(field, scatter_weight)
        field = update(field, moved, gain, rate, flags)
    return field


def solution(mesh):
    in_specs = (
        P("mode", "tile", None),
        P(None, "mode"),
        P("mode"),
        P("mode", None),
        P("tile", None),
    )
    out_specs = P("mode", "tile", None)
    return jax.shard_map(body, mesh=mesh, in_specs=in_specs, out_specs=out_specs, check_vma=False)
```

profile of v0, /device:TPU:0, one launch (start us, length us, event | category | flops | bytes accessed | tf_op | source)
XLA Modules:
  0.0 398.1 jit_solution(6005349296509350939)
XLA Ops:
  6.5 2.4 convert_element_type.14
  8.9 1.9 copy.46
  10.8 0.0 all-gather.3.cloned.1.call-update
  10.9 0.0 all-gather.5.cloned.1.call-start
  10.9 4.2 %fusion.50 = (f32[1024,2,128]{2,1,0:T(2,128)S(1)}, f32[1024,2,128]{2,1,0:T(2,128)S(1)}) fusion(f32[1024,8,128]{2,1,0:T(8,128)} %param.5), kind=kLoop, calls=%fused_computation.81 | loop fusion | bytes 4194304 | tf_op jit(solution)/shard_map/slice | solution.py:16
  15.1 0.1 copy.43
  15.2 1.3 collective-permute-start.1
  16.5 0.1 copy.42
  16.6 0.0 copy-start.6
  16.6 0.0 copy-start.5
  16.6 4.1 %collective-permute-start = (f32[1024,2,128]{2,0,1:T(8,128)S(1)}, f32[1024,2,128]{2,0,1:T(8,128)}, u32[]{:S(2)}, u32[]{:S(2)}) collective-permute-start(f32[1024,2,128]{2,0,1:T(8,128)S(1)} %copy.42), channel_id=1, source_target_pairs={{0,1},{1,2},{2,3},{3,4},{4,5},{5,6},{6,7},{8,9},{9,10},{10,11},{11... | collective-permute-start | bytes 3145736 | tf_op jit(solution)/shard_map/ppermute | solution.py:15
  20.7 5.7 %copy.32 = f32[1024,8,128]{0,2,1:T(8,128)} copy(f32[1024,8,128]{2,1,0:T(8,128)} %param.5) | data formatting | bytes 8388608 | tf_op args[0]
  26.4 0.3 copy.28
  26.8 1.6 copy.23
  28.4 5.0 %select_maximum_fusion.2 = f32[1024,12,132]{0,2,1:T(8,128)} fusion(f32[1024,2,128]{0,2,1:T(8,128)S(1)} %copy.28, f32[1024,8,128]{0,2,1:T(8,128)} %copy.32, f32[1024,2,128]{0,2,1:T(8,128)S(1)} %copy.23), kind=kLoop, calls=%fused_computation.4 | loop fusion | flops 12976128 | bytes 12779520 | tf_op jit(solution)/shard_map/concatenate | solution.py:19
  33.5 129.9 %all-gather.3.cloned.1.call-done = bf16[4096,1024]{1,0:T(8,128)(2,1)} async-done(((bf16[1024,1024]{1,0:T(8,128)(2,1)}), bf16[4096,1024]{1,0:T(8,128)(2,1)}) %all-gather.3.cloned.1.call-update) | async-done | bytes 8388624 | tf_op jit(solution)/shard_map/all_gather | solution.py:44
  163.4 30.6 %fusion.51 = f32[1024,1024]{0,1:T(8,128)S(1)} fusion(f32[1024,4096]{1,0:T(8,128)} %param.8, bf16[4096,1024]{1,0:T(8,128)(2,1)} %all-gather.3.cloned.1.call-done), kind=kOutput, calls=%fused_computation.82 | convolution fusion | flops 51539607552 | bytes 29360128 | tf_op jit(solution)/shard_map/dot_general | solution.py:42
  194.0 6.6 %fusion.47 = (bf16[1024,8,128]{0,2,1:T(8,128)(2,1)}, f32[1024,8,128]{0,2,1:T(8,128)}) fusion(f32[1024,8,128]{0,2,1:T(8,128)S(1)} %copy-done.3, f32[8,128]{1,0:T(8,128)S(1)} %convert_multiply_fusion, f32[1024,8,128]{0,2,1:T(8,128)S(1)} %bitcast.21, f32[1024]{0:T(1024)S(1)} %copy-done.4, f32[1024,12,132]{0,2,1:T(8,128)S(1)} %copy-done.1, ...), kind=kLoop, calls=%fused_computation.79 | loop fusion | flops 38797312 | bytes 33579008 | tf_op jit(solution)/shard_map/convert_element_type | solution.py:39
  200.6 0.0 all-gather.5.cloned.1.call-update
  200.6 1.7 fusion.49
  202.3 0.3 copy.37
  202.7 1.3 collective-permute-start.3
  204.0 1.4 copy.35
  205.4 4.0 %collective-permute-start.2 = (f32[1024,2,128]{2,0,1:T(8,128)}, f32[1024,2,128]{2,0,1:T(8,128)}, u32[]{:S(2)}, u32[]{:S(2)}) collective-permute-start(f32[1024,2,128]{2,0,1:T(8,128)} %copy.35), channel_id=1, source_target_pairs={{0,1},{1,2},{2,3},{3,4},{4,5},{5,6},{6,7},{8,9},{9,10},{10,11},{11... | collective-permute-start | bytes 3145736 | tf_op jit(solution)/shard_map/ppermute | solution.py:15
  209.4 0.3 copy.38
  209.7 1.3 collective-permute-done.2
  211.0 1.6 copy.36
  212.7 5.0 %select_maximum_fusion = f32[1024,12,132]{0,2,1:T(8,128)} fusion(f32[1024,2,128]{0,2,1:T(8,128)S(1)} %copy.38, f32[1024,8,128]{0,2,1:T(8,128)} %get-tuple-element.6, f32[1024,2,128]{0,2,1:T(8,128)S(1)} %copy.36), kind=kLoop, calls=%fused_computation.2 | loop fusion | flops 12976128 | bytes 12779520 | tf_op jit(solution)/shard_map/concatenate | solution.py:19
  217.7 131.0 %all-gather.5.cloned.1.call-done = bf16[4096,1024]{0,1:T(8,128)(2,1)} async-done(((bf16[1024,1024]{0,1:T(8,128)(2,1)}), bf16[4096,1024]{0,1:T(8,128)(2,1)}) %all-gather.5.cloned.1.call-update) | async-done | bytes 8388624 | tf_op jit(solution)/shard_map/all_gather | solution.py:44
  348.7 30.9 %fusion.52 = f32[1024,1024]{1,0:T(8,128)S(1)} fusion(bf16[4096,1024]{0,1:T(8,128)(2,1)} %all-gather.5.cloned.1.call-done, f32[1024,4096]{1,0:T(8,128)} %param.8), kind=kOutput, calls=%fused_computation.83 | convolution fusion | flops 51539607552 | bytes 29360128 | tf_op jit(solution)/shard_map/dot_general | solution.py:42
  379.6 6.3 %fusion.10 = f32[1024,8,128]{0,2,1:T(8,128)} fusion(f32[1024,8,128]{0,2,1:T(8,128)S(1)} %copy-done.2, f32[1024,2,128]{0,2,1:T(8,128)S(1)} %copy.38, f32[1024,2,128]{0,2,1:T(8,128)S(1)} %copy.36, f32[1024,12,132]{0,2,1:T(8,128)S(1)} %copy-done, f32[1024,8,128]{0,2,1:T(8,128)S(1)} %bitcast.20, f32[8,128]{1,0:T(8,128)S(1)} %convert_multiply_fusion, ...), kind=kLoop, calls=%fused_computation.24 | loop fusion | flops 37748736 | bytes 31481856 | tf_op jit(solution)/shard_map/add | solution.py:52
  385.9 5.4 %copy.41 = f32[1024,8,128]{2,1,0:T(8,128)} copy(f32[1024,8,128]{0,2,1:T(8,128)} %fusion.10) | data formatting | bytes 8388608 | tf_op jit(solution)/shard_map/add | solution.py:52
  (18 shorter events, 0.1 us)
Async XLA Ops:
  6.5 156.8 %all-gather.3.cloned.1.call-start = ((), (), s32[]{:S(2)}) async-start(), calls=%async_computation | async-start | bytes 10485760 | tf_op jit(solution)/shard_map/all_gather | solution.py:44
  10.9 337.8 %all-gather.5.cloned.1.call-start = ((), (), s32[]{:S(2)}) async-start(), calls=%async_computation.1 | async-start | bytes 10485760 | tf_op jit(solution)/shard_map/all_gather | solution.py:44
  15.2 11.2 %collective-permute-start.1 = (f32[1024,2,128]{2,0,1:T(8,128)S(1)}, f32[1024,2,128]{2,0,1:T(8,128)S(1)}, u32[]{:S(2)}, u32[]{:S(2)}) collective-permute-start(f32[1024,2,128]{2,0,1:T(8,128)S(1)} %copy.43), channel_id=1, source_target_pairs={{1,0},{2,1},{3,2},{4,3},{5,4},{6,5},{7,6},{9,8},{10,9},{11,10},{12... | collective-permute-start | bytes 3145736 | tf_op jit(solution)/shard_map/ppermute | solution.py:18
  16.6 9.8 %copy-start.6 = (s32[8,128]{1,0:T(8,128)S(1)}, s32[8,128]{1,0:T(8,128)}, u32[]{:S(2)}) copy-start(s32[8,128]{1,0:T(8,128)} %param.9) | copy-start | bytes 12292
  16.6 9.8 %copy-start.5 = (f32[2,1024]{1,0:T(2,128)S(1)}, f32[2,1024]{1,0:T(2,128)}, u32[]{:S(2)}) copy-start(f32[2,1024]{1,0:T(2,128)} %param.6) | copy-start | bytes 24580
  16.6 10.2 %collective-permute-start = (f32[1024,2,128]{2,0,1:T(8,128)S(1)}, f32[1024,2,128]{2,0,1:T(8,128)}, u32[]{:S(2)}, u32[]{:S(2)}) collective-permute-start(f32[1024,2,128]{2,0,1:T(8,128)S(1)} %copy.42), channel_id=1, source_target_pairs={{0,1},{1,2},{2,3},{3,4},{4,5},{5,6},{6,7},{8,9},{9,10},{10,11},{11... | collective-permute-start | bytes 3145736 | tf_op jit(solution)/shard_map/ppermute | solution.py:15
  33.5 160.6 %copy-start.4 = (f32[1024]{0:T(1024)S(1)}, f32[1024]{0:T(1024)}, u32[]{:S(2)}) copy-start(f32[1024]{0:T(1024)} %param.7) | copy-start | bytes 12292
  163.4 30.7 %copy-start.1 = (f32[1024,12,132]{0,2,1:T(8,128)S(1)}, f32[1024,12,132]{0,2,1:T(8,128)}, u32[]{:S(2)}) copy-start(f32[1024,12,132]{0,2,1:T(8,128)} %select_maximum_fusion.2) | copy-start | bytes 19464196
  163.4 30.7 %copy-start.3 = (f32[1024,8,128]{0,2,1:T(8,128)S(1)}, f32[1024,8,128]{0,2,1:T(8,128)}, u32[]{:S(2)}) copy-start(f32[1024,8,128]{0,2,1:T(8,128)} %copy.32) | copy-start | bytes 12582916
  202.7 6.7 %collective-permute-start.3 = (f32[1024,2,128]{2,0,1:T(8,128)S(1)}, f32[1024,2,128]{2,0,1:T(8,128)S(1)}, u32[]{:S(2)}, u32[]{:S(2)}) collective-permute-start(f32[1024,2,128]{2,0,1:T(8,128)S(1)} %copy.37), channel_id=1, source_target_pairs={{1,0},{2,1},{3,2},{4,3},{5,4},{6,5},{7,6},{9,8},{10,9},{11,10},{12... | collective-permute-start | bytes 3145736 | tf_op jit(solution)/shard_map/ppermute | solution.py:18
  205.4 5.6 %collective-permute-start.2 = (f32[1024,2,128]{2,0,1:T(8,128)}, f32[1024,2,128]{2,0,1:T(8,128)}, u32[]{:S(2)}, u32[]{:S(2)}) collective-permute-start(f32[1024,2,128]{2,0,1:T(8,128)} %copy.35), channel_id=1, source_target_pairs={{0,1},{1,2},{2,3},{3,4},{4,5},{5,6},{6,7},{8,9},{9,10},{10,11},{11... | collective-permute-start | bytes 3145736 | tf_op jit(solution)/shard_map/ppermute | solution.py:15
  348.7 30.9 %copy-start = (f32[1024,12,132]{0,2,1:T(8,128)S(1)}, f32[1024,12,132]{0,2,1:T(8,128)}, u32[]{:S(2)}) copy-start(f32[1024,12,132]{0,2,1:T(8,128)} %select_maximum_fusion) | copy-start | bytes 19464196
  348.7 30.9 %copy-start.2 = (f32[1024,8,128]{0,2,1:T(8,128)S(1)}, f32[1024,8,128]{0,2,1:T(8,128)}, u32[]{:S(2)}) copy-start(f32[1024,8,128]{0,2,1:T(8,128)} %get-tuple-element.6) | copy-start | bytes 12582916
Sparse Core Ops, SparseCore 0:
  11.0 152.3 all-gather.2
  200.8 147.8 all-gather.4
where the time goes:
time: 399 us; the launch traced here: 398 us
  waiting for transfers between devices  262 us (66%)
  matrix products  61.5 us (15%)
  other arithmetic  25.4 us (6%)
  local copies, waits for them, and re-layouts  24.7 us (6%)
  between operations  13.6 us (3%)
  starting transfers between devices  10.8 us (3%)
    all_gather x2, waiting for transfers between devices, collide(): lax.all_gather(flat, 'mode', axis=0, tiled=True).astype(jnp.float32)  261 us
    dot_general x2, matrix products, collide(): jnp.dot(scatter_weight, lax.all_gather(flat, 'mode', axis=0, tiled=True)....  61.5 us
    concatenate x2, other arithmetic, extended(): block = jnp.concatenate([low, block, high], axis=dim)  10 us
    convert_element_type x2, other arithmetic, collide(): rounded = field.astype(jnp.bfloat16)  8.96 us
    ppermute x2, starting transfers between devices, extended(): lax.ppermute(lax.slice_in_dim(block, block.shape[dim] - width, None, axis...  8.14 us
  transfers between devices with their start and end apart: 6, of which 3 were waited for; matrix products, arithmetic and copies ran while one was open for 7% of the time, Pallas kernels for 0%

commit v1 on v0

v1 whole, which is shorter than its diff:
```python
import functools

import jax
import jax.numpy as jnp
from jax import lax
from jax.experimental import pallas as pl
from jax.experimental.pallas import tpu as pltpu
from jax.sharding import PartitionSpec as P

time_step = 0.25
wall_rate = 2.0
chunk_rows = 4
bf16 = jnp.bfloat16
f32 = jnp.float32


def pack_kernel(rows, modes, field_ref, rounded_ref, low_ref, high_ref):
    for r in range(rows):
        line = field_ref[pl.ds(r, modes, stride=rows), :]
        rounded_ref[r] = line.astype(bf16)
        if r < 2:
            low_ref[r] = line
        if r >= rows - 2:
            high_ref[r - rows + 2] = line


def pack(field):
    modes, rows, columns = field.shape
    block = 256
    return pl.pallas_call(
        functools.partial(pack_kernel, rows, block),
        grid=(modes // block,),
        in_specs=[pl.BlockSpec((block * rows, columns), lambda i: (i, 0))],
        out_specs=[
            pl.BlockSpec((rows, block, columns), lambda i: (0, i, 0)),
            pl.BlockSpec((2, block, columns), lambda i: (0, i, 0)),
            pl.BlockSpec((2, block, columns), lambda i: (0, i, 0)),
        ],
        out_shape=[
            jax.ShapeDtypeStruct((rows, modes, columns), bf16),
            jax.ShapeDtypeStruct((2, modes, columns), f32),
            jax.ShapeDtypeStruct((2, modes, columns), f32),
        ],
        cost_estimate=pl.CostEstimate(flops=1000, bytes_accessed= 1000, transcendentals=0),
        compiler_params=pltpu.CompilerParams(vmem_limit_bytes=32 * 2**20),
        name="pack",
    )(field.reshape(modes * rows, columns))


def local_line(lines, r, params, flags):
    cx, cy, rate = params
    centre = lines(r)
    shape = centre.shape
    lane = lax.broadcasted_iota(jnp.int32, shape, 1)
    columns = shape[1]

    def moved(by):
        turned = pltpu.roll(centre, by % columns, 1)
        keep = lane >= by if by > 0 else lane < columns + by
        return jnp.where(keep, turned, 0.0)

    back_x = 1.5 * centre - 2.0 * lines(r - 1) + 0.5 * lines(r - 2)
    fwd_x = -1.5 * centre + 2.0 * lines(r + 1) - 0.5 * lines(r + 2)
    back_y = 1.5 * centre - 2.0 * moved(1) + 0.5 * moved(2)
    fwd_y = -1.5 * centre + 2.0 * moved(-1) - 0.5 * moved(-2)
    transport = (
        jnp.maximum(cx, 0.0) * back_x
        + jnp.minimum(cx, 0.0) * fwd_x
        + jnp.maximum(cy, 0.0) * back_y
        + jnp.minimum(cy, 0.0) * fwd_y
    )
    return centre - transport - time_step * (rate * centre + wall_rate * flags * centre)


def base_kernel(rows, modes, strided, field_ref, before_ref, after_ref, cx_ref, cy_ref, rate_ref, flags_ref, out_ref):
    params = (cx_ref[...], cy_ref[...], rate_ref[...])

    def lines(r):
        if r < 0:
            return before_ref[r + 2]
        if r >= rows:
            return after_ref[r - rows]
        if strided:
            return field_ref[pl.ds(r, modes, stride=rows), :]
        return field_ref[r]

    for r in range(rows):
        out_ref[r] = local_line(lines, r, params, flags_ref[r:r + 1, :])


def base(field, before, after, params, flags, strided):
    rows, columns = flags.shape
    modes = before.shape[1]
    block = 128
    if strided:
        field_spec = pl.BlockSpec((block * rows, columns), lambda i: (i, 0))
        field = field.reshape(modes * rows, columns)
    else:
        field_spec = pl.BlockSpec((rows, block, columns), lambda i: (0, i, 0))
    side = pl.BlockSpec((2, block, columns), lambda i: (0, i, 0))
    per_mode = pl.BlockSpec((block, 1), lambda i: (i, 0))
    return pl.pallas_call(
        functools.partial(base_kernel, rows, block, strided),
        grid=(modes // block,),
        in_specs=[field_spec, side, side, per_mode, per_mode, per_mode, pl.BlockSpec((rows, columns), lambda i: (0, 0))],
        out_specs=pl.BlockSpec((rows, block, columns), lambda i: (0, i, 0)),
        out_shape=jax.ShapeDtypeStruct((rows, modes, columns), f32),
        cost_estimate=pl.CostEstimate(flops=1000, bytes_accessed= 1000, transcendentals=0),
        compiler_params=pltpu.CompilerParams(vmem_limit_bytes=32 * 2**20),
        name="base",
    )(field, before, after, *params, flags)


def gains_kernel(own_steps, order_ref, own_w_ref, edge_w_ref, a_ref, b_ref, c_ref, d_ref, base_ref, first_ref, rounded_ref, sum_ref, cells_ref):
    rows, depth, lanes = a_ref.shape

    @pl.when(pl.program_id(0) == 0)
    def _():
        for j, part in enumerate((a_ref, b_ref, c_ref, d_ref)):
            at = pl.ds(pl.multiple_of(order_ref[j] * depth, depth), depth)
            for r in range(rows):
                cells_ref[at, r * lanes:(r + 1) * lanes] = part[r]

    @pl.when(pl.program_id(0) < own_steps)
    def _():
        total = jnp.dot(own_w_ref[...], cells_ref[...], preferred_element_type=f32)
        for r in range(rows):
            line = base_ref[r] + time_step * total[:, r * lanes:(r + 1) * lanes]
            first_ref[r] = line
            rounded_ref[r] = line.astype(bf16)

    @pl.when(pl.program_id(0) >= own_steps)
    def _():
        at = pl.ds(pl.multiple_of(order_ref[4] * depth, depth), 3 * depth)
        total = jnp.dot(edge_w_ref[...], cells_ref[at, :], preferred_element_type=f32)
        for r in range(rows):
            sum_ref[r] = total[:, r * lanes:(r + 1) * lanes].astype(bf16)


def gains(order, own_w, edge_w, parts, based, at):
    modes, depth = own_w.shape
    rows, _, columns = parts[0].shape
    block = modes // 2
    steps = modes // block
    first = lambda i, order: (0, jnp.minimum(i, steps - 1), 0)
    second = lambda i, order: (0, jnp.maximum(i - steps, 0), 0)
    whole = pl.BlockSpec(parts[0].shape, lambda i, order: (0, 0, 0))
    return pl.pallas_call(
        functools.partial(gains_kernel, steps),
        grid_spec=pltpu.PrefetchScalarGridSpec(
            num_scalar_prefetch=1,
            grid=(2 * steps,),
            in_specs=[
                pl.BlockSpec((block, depth), lambda i, order: (jnp.minimum(i, steps - 1), 0)),
                pl.BlockSpec((block, depth - modes), lambda i, order: (jnp.maximum(i - steps, 0), 0)),
                whole, whole, whole, whole,
                pl.BlockSpec((rows, block, columns), lambda i, order: (at, jnp.minimum(i, steps - 1), 0)),
            ],
            out_specs=[
                pl.BlockSpec((rows, block, columns), first),
                pl.BlockSpec((rows, block, columns), first),
                pl.BlockSpec((rows, block, columns), second),
            ],
            scratch_shapes=[pltpu.VMEM((depth, rows * columns), bf16)],
        ),
        out_shape=[
            jax.ShapeDtypeStruct((rows, modes, columns), f32),
            jax.ShapeDtypeStruct((rows, modes, columns), bf16),
            jax.ShapeDtypeStruct((rows, modes, columns), bf16),
        ],
        cost_estimate=pl.CostEstimate(flops=1000, bytes_accessed= 1000, transcendentals=0),
        compiler_params=pltpu.CompilerParams(vmem_limit_bytes=44 * 2**20),
        name="gains",
    )(order, own_w, edge_w, *parts, based)


def unpack_kernel(rows, modes, each, *refs):
    out_ref = refs[-1]
    count = len(refs) // 2
    for r in range(rows):
        line = refs[r // each][r % each] + time_step * refs[count + r // each][r % each].astype(f32)
        out_ref[pl.ds(r, modes, stride=rows), :] = line


def unpack(firsts, sums):
    each, modes, columns = firsts[0].shape
    rows = each * len(firsts)
    block = 256
    flat = pl.pallas_call(
        functools.partial(unpack_kernel, rows, block, each),
        grid=(modes // block,),
        in_specs=[pl.BlockSpec((each, block, columns), lambda i: (0, i, 0))] * (2 * len(firsts)),
        out_specs=pl.BlockSpec((block * rows, columns), lambda i: (i, 0)),
        out_shape=jax.ShapeDtypeStruct((modes * rows, columns), f32),
        cost_estimate=pl.CostEstimate(flops=1000, bytes_accessed= 1000, transcendentals=0),
        compiler_params=pltpu.CompilerParams(vmem_limit_bytes=32 * 2**20),
        name="unpack",
    )(*firsts, *sums)
    return flat.reshape(modes, rows, columns)


inward = [(0, 1), (3, 2)]
outward = [(1, 0), (2, 3)]
across = [(1, 2), (2, 1)]


def line_of_four(distribution, courant, relax_rate, scatter_weight, cell_flags):
    modes, rows, columns = distribution.shape
    plane = lax.axis_index("mode")
    beside = plane + 1 - 2 * (plane % 2)
    order = jnp.stack([plane, beside, 3 - plane, 3 - beside, (plane < 2).astype(jnp.int32)])
    flags = cell_flags.astype(f32)
    params = tuple(v[:, None] for v in (courant[0], courant[1], relax_rate))
    count = lax.axis_size("tile")
    up = [(i, i + 1) for i in range(count - 1)]
    down = [(i + 1, i) for i in range(count - 1)]
    send = functools.partial(lax.ppermute, axis_name="mode")
    after = lambda value, *earlier: lax.optimization_barrier((value, *earlier))[0]

    rounded, low, high = pack(distribution)
    x1, x2 = rounded[:chunk_rows], rounded[chunk_rows:]

    share = modes // count
    piece = lax.dynamic_slice(
        scatter_weight,
        (lax.axis_index("tile") * share, jnp.where(plane == 0, modes, 0)),
        (share, 3 * modes),
    )
    piece = send(after(piece.astype(bf16), rounded), perm=inward)
    own_w = after(scatter_weight, rounded).astype(bf16)
    b1 = send(x1, perm=across)
    edge_w = lax.all_gather(after(piece, own_w, b1), "tile", axis=0, tiled=True)
    b2 = send(after(x2, b1), perm=across)
    a1 = send(after(x1, piece), perm=inward)
    a2 = send(after(x2, a1), perm=inward)
    c1 = send(a1, perm=across)
    c2 = send(a2, perm=across)
    based = base(
        distribution,
        lax.ppermute(high, "tile", up),
        lax.ppermute(low, "tile", down),
        params, flags, True,
    )
    first1, own1, sum1 = gains(order, own_w, edge_w, (x1, a1, b1, c1), based, 0)
    first2, own2, sum2 = gains(order, own_w, edge_w, (x2, a2, b2, c2), based, 1)
    b1 = send(own1, perm=across)
    b2 = send(after(own2, b1), perm=across)
    field1 = first1 + time_step * send(sum1, perm=outward).astype(f32)
    x1 = field1.astype(bf16)
    a1 = send(x1, perm=inward)
    field2 = first2 + time_step * send(sum2, perm=outward).astype(f32)
    x2 = field2.astype(bf16)
    a2 = send(x2, perm=inward)
    c1 = send(a1, perm=across)
    c2 = send(a2, perm=across)
    based = base(
        jnp.concatenate([field1, field2], axis=0),
        lax.ppermute(field2[-2:], "tile", up),
        lax.ppermute(field1[:2], "tile", down),
        params, flags, False,
    )
    first1, _, sum1 = gains(order, own_w, edge_w, (x1, a1, b1, c1), based, 0)
    first2, _, sum2 = gains(order, own_w, edge_w, (x2, a2, b2, c2), based, 1)
    return unpack([first1, first2], [send(sum1, perm=outward), send(sum2, perm=outward)])


def extended(block, width):
    count = lax.axis_size("tile")
    up = [(i, i + 1) for i in range(count - 1)]
    down = [(i + 1, i) for i in range(count - 1)]
    low = lax.ppermute(block[:, -width:], "tile", up)
    high = lax.ppermute(block[:, :width], "tile", down)
    return jnp.concatenate([low, block, high], axis=1)


def gathered(distribution, courant, relax_rate, scatter_weight, cell_flags):
    cx = courant[0][:, None, None]
    cy = courant[1][:, None, None]
    rate = relax_rate[:, None, None]
    flags = cell_flags.astype(f32)[None]
    weight = scatter_weight.astype(bf16)
    field = distribution
    for step in range(2):
        full = jnp.pad(extended(field, 2), ((0, 0), (0, 0), (2, 2)))
        centre = full[:, 2:-2, 2:-2]
        back_x = 1.5 * centre - 2.0 * full[:, 1:-3, 2:-2] + 0.5 * full[:, :-4, 2:-2]
        fwd_x = -1.5 * centre + 2.0 * full[:, 3:-1, 2:-2] - 0.5 * full[:, 4:, 2:-2]
        back_y = 1.5 * centre - 2.0 * full[:, 2:-2, 1:-3] + 0.5 * full[:, 2:-2, :-4]
        fwd_y = -1.5 * centre + 2.0 * full[:, 2:-2, 3:-1] - 0.5 * full[:, 2:-2, 4:]
        transport = (
            jnp.maximum(cx, 0.0) * back_x
            + jnp.minimum(cx, 0.0) * fwd_x
            + jnp.maximum(cy, 0.0) * back_y
            + jnp.minimum(cy, 0.0) * fwd_y
        )
        flat = field.astype(bf16).reshape(field.shape[0], -1)
        flat = lax.all_gather(flat, "mode", axis=0, tiled=True)
        gain = jnp.dot(weight, flat, preferred_element_type=f32).reshape(field.shape)
        field = field - transport + time_step * (gain - rate * field - wall_rate * flags * field)
    return field


def body(*args):
    if lax.axis_size("mode") == 4 and args[0].shape[1] == 2 * chunk_rows:
        return line_of_four(*args)
    return gathered(*args)


def solution(mesh):
    in_specs = (
        P("mode", "tile", None),
        P(None, "mode"),
        P("mode"),
        P("mode", None),
        P("tile", None),
    )
    out_specs = P("mode", "tile", None)
    return jax.shard_map(body, mesh=mesh, in_specs=in_specs, out_specs=out_specs, check_vma=False)
```

time: 399 us -> 311 us (0.78)
  waiting for transfers between devices: 262 us -> 128 us
  Pallas kernels: 0 us -> 78.3 us
  matrix products: 61.5 us -> 0 us
  starting transfers between devices: 10.8 us -> 67.4 us
  other arithmetic: 25.4 us -> 9.92 us
  local copies, waits for them, and re-layouts: 24.7 us -> 13.1 us
    all_gather x2 -> x1, waiting for transfers between devices: 261 us -> 0.01 us  [line_of_four(): edge_w = lax.all_gather(after(piece, own_w, b1), 'tile', axis=0, tiled=True)]
    ppermute x4 -> x21, waiting for transfers between devices: 1.28 us -> 128 us  [the longest x1 36.1 us: line_of_four(): send(sum2, perm=outward)]
    pallas_call x0 -> x8, Pallas kernels: none -> 78.3 us  [the longest x4 57 us: gains(): pl.pallas_call(functools.partial(gains_kernel, steps), grid_spec=pltpu.Pr...]
    dot_general x2 -> x0, matrix products: 61.5 us -> none  [collide(): jnp.dot(scatter_weight, lax.all_gather(flat, 'mode', axis=0, tiled=True)....]
    ppermute x4 -> x21, starting transfers between devices: 10.7 us -> 67.4 us  [the longest x1 26.4 us: line_of_four(): a1 = send(x1, perm=inward)]
    concatenate x2 -> x1, other arithmetic: 10 us -> 0.27 us  [line_of_four(): jnp.concatenate([field1, field2], axis=0)]
    slice x4 -> x3, local copies, waits for them, and re-layouts: 7.61 us -> 0.28 us  [the longest x1 0.14 us: line_of_four(): x1, x2 = (rounded[:chunk_rows], rounded[chunk_rows:])]
    add x1 -> x0, other arithmetic: 6.33 us -> none  [update(): centre - moved]
  transfers between devices with their start and end apart: 6 -> 22, of which waited for: 3 -> 9; matrix products, arithmetic and copies ran while one was open for 7% -> 4% of each run, Pallas kernels for 0% -> 23%
where the time goes in v1:
time: 311 us; the launch traced here: 310 us
  waiting for transfers between devices  128 us (41%)
  Pallas kernels  78.3 us (25%)
  starting transfers between devices  67.4 us (22%)
  between operations  13.8 us (4%)
  local copies, waits for them, and re-layouts  13.1 us (4%)
  other arithmetic  9.92 us (3%)
    pallas_call x4, Pallas kernels, gains(): pl.pallas_call(functools.partial(gains_kernel, steps), grid_spec=pltpu.Pr...  57 us
    ppermute x1, waiting for transfers between devices, line_of_four(): send(sum2, perm=outward)  36.1 us
    ppermute x1, starting transfers between devices, line_of_four(): a1 = send(x1, perm=inward)  26.4 us
    ppermute x1, waiting for transfers between devices, line_of_four(): a2 = send(x2, perm=inward)  20.5 us
    ppermute x1, waiting for transfers between devices, line_of_four(): a1 = send(after(x1, piece), perm=inward)  20.4 us
    ppermute x1, waiting for transfers between devices, line_of_four(): field2 = first2 + time_step * send(sum2, perm=outward).astype(f32)  18.1 us
    pallas_call x2, Pallas kernels, base(): pl.pallas_call(functools.partial(base_kernel, rows, block, strided), grid...  15.8 us
    ppermute x1, waiting for transfers between devices, line_of_four(): a2 = send(after(x2, a1), perm=inward)  12.6 us
  transfers between devices with their start and end apart: 22, of which 9 were waited for; matrix products, arithmetic and copies ran while one was open for 4% of the time, Pallas kernels for 23%

profile of v1, /device:TPU:0, one launch (start us, length us, event | category | flops | bytes accessed | tf_op | source)
XLA Modules:
  0.0 310.1 jit_solution(2799814424470768236)
XLA Ops:
  6.5 2.2 copy-done.2
  8.7 2.3 pack.1
  11.2 1.7 collective-permute-start.1
  12.9 1.5 dynamic_slice.5
  14.4 7.0 %collective-permute-start = (bf16[128,3072]{1,0:T(8,128)(2,1)S(1)}, bf16[128,3072]{1,0:T(8,128)(2,1)S(1)}, u32[]{:S(2)}, u32[]{:S(2)}) collective-permute-start(bf16[128,3072]{1,0:T(8,128)(2,1)S(1)} %dynamic_slice.5), channel_id=1, source_target_pairs={{0,8},{24,16},{1,9},{25,17},{2,10},{26,18},{3,11},{27,19},{4,12},{... | collective-permute-start | bytes 2359304 | tf_op jit(solution)/shard_map/ppermute | solution.py:229
  21.4 9.1 %convert_element_type.22.own_w_ref = bf16[1024,4096]{1,0:T(8,128)(2,1)} convert(f32[1024,4096]{1,0:T(8,128)} %param.8) | non-fusion elementwise | flops 4194304 | bytes 25165824 | tf_op jit(solution)/shard_map/convert_element_type | solution.py:230
  30.5 7.4 %collective-permute-done = bf16[128,3072]{1,0:T(8,128)(2,1)S(1)} collective-permute-done((bf16[128,3072]{1,0:T(8,128)(2,1)S(1)}, bf16[128,3072]{1,0:T(8,128)(2,1)S(1)}, u32[]{:S(2)}, u32[]{:S(2)}) %collective-permute-start) | collective-permute-done | bytes 786464 | tf_op jit(solution)/shard_map/ppermute | solution.py:229
  38.8 5.4 %collective-permute-start.2 = (bf16[4,1024,128]{2,1,0:T(8,128)(2,1)S(1)}, bf16[4,1024,128]{2,1,0:T(8,128)(2,1)}, u32[]{:S(2)}, u32[]{:S(2)}) collective-permute-start(bf16[4,1024,128]{2,1,0:T(8,128)(2,1)S(1)} %get-tuple-element.29.a_ref), channel_id=1, source_target_pairs={{0,8},{24,16},{1,9},{25,17},{2,10},{26,18},{3,11},{27,19},{4,12},{... | collective-permute-start | bytes 3145736 | tf_op jit(solution)/shard_map/ppermute | solution.py:234
  44.2 20.4 %collective-permute-done.2.b_ref = bf16[4,1024,128]{2,1,0:T(8,128)(2,1)} collective-permute-done((bf16[4,1024,128]{2,1,0:T(8,128)(2,1)S(1)}, bf16[4,1024,128]{2,1,0:T(8,128)(2,1)}, u32[]{:S(2)}, u32[]{:S(2)}) %collective-permute-start.2) | collective-permute-done | bytes 1048608 | tf_op jit(solution)/shard_map/ppermute | solution.py:234
  64.6 5.5 %collective-permute-start.10 = (bf16[4,1024,128]{2,1,0:T(8,128)(2,1)S(1)}, bf16[4,1024,128]{2,1,0:T(8,128)(2,1)}, u32[]{:S(2)}, u32[]{:S(2)}) collective-permute-start(bf16[4,1024,128]{2,1,0:T(8,128)(2,1)S(1)} %get-tuple-element.36.a_ref), channel_id=1, source_target_pairs={{0,8},{24,16},{1,9},{25,17},{2,10},{26,18},{3,11},{27,19},{4,12},{... | collective-permute-start | bytes 3145736 | tf_op jit(solution)/shard_map/ppermute | solution.py:235
  70.1 2.3 collective-permute-start.4
  73.6 1.7 collective-permute-start.3
  75.3 1.7 collective-permute-start.11
  77.0 12.6 %collective-permute-done.10.b_ref = bf16[4,1024,128]{2,1,0:T(8,128)(2,1)} collective-permute-done((bf16[4,1024,128]{2,1,0:T(8,128)(2,1)S(1)}, bf16[4,1024,128]{2,1,0:T(8,128)(2,1)}, u32[]{:S(2)}, u32[]{:S(2)}) %collective-permute-start.10) | collective-permute-done | bytes 1048608 | tf_op jit(solution)/shard_map/ppermute | solution.py:235
  89.6 1.7 collective-permute-start.12
  92.1 2.2 copy-done.3
  94.2 8.5 %base.2.base_ref = f32[8,1024,128]{2,1,0:T(8,128)S(1)} custom-call(f32[8192,128]{1,0:T(8,128)S(1)} %bitcast.13, f32[2,1024,128]{2,1,0:T(8,128)} %collective-permute-done.4.before_ref, f32[2,1024,128]{2,1,0:T(8,128)} %collective-permute-done.5.after_ref, f32[1024,1]{1,0:T(8,128)S(1)} %copy.6.cx_ref, f32[1024,1]{1,0:T(8,128)S(1)} %copy.7.cy_ref, ...), custom_call_target="tpu_custom_call" | custom-call | flops 1000 | bytes 1000 | tf_op jit(solution)/shard_map/base/pallas_call | solution.py:102
  102.8 2.0 copy-done.1
  106.0 14.4 %gains.4 = (f32[4,1024,128]{2,1,0:T(8,128)S(1)}, bf16[4,1024,128]{2,1,0:T(8,128)(2,1)S(1)}, bf16[4,1024,128]{2,1,0:T(8,128)(2,1)S(1)}) custom-call(s32[5]{0:T(128)S(1)} %stack.27.order_ref, bf16[1024,4096]{1,0:T(8,128)(2,1)} %convert_element_type.22.own_w_ref, bf16[1024,3072]{1,0:T(8,128)(2,1)} %all-gather.2.cloned.1.call-done.edge_w_ref, ...), custom_call_target="tpu_custom_call" | custom-call | flops 1000 | bytes 1000 | tf_op jit(solution)/shard_map/gains/pallas_call | solution.py:148
  121.7 14.4 %gains.5 = (f32[4,1024,128]{2,1,0:T(8,128)S(1)}, bf16[4,1024,128]{2,1,0:T(8,128)(2,1)S(1)}, bf16[4,1024,128]{2,1,0:T(8,128)(2,1)S(1)}) custom-call(s32[5]{0:T(128)S(1)} %stack.27.order_ref, bf16[1024,4096]{1,0:T(8,128)(2,1)} %convert_element_type.22.own_w_ref, bf16[1024,3072]{1,0:T(8,128)(2,1)} %all-gather.2.cloned.1.call-done.edge_w_ref, ...), custom_call_target="tpu_custom_call" | custom-call | flops 1000 | bytes 1000 | tf_op jit(solution)/shard_map/gains/pallas_call | solution.py:148
  139.4 26.4 %collective-permute-start.7 = (bf16[4,1024,128]{2,1,0:T(8,128)(2,1)S(1)}, bf16[4,1024,128]{2,1,0:T(8,128)(2,1)S(1)}, u32[]{:S(2)}, u32[]{:S(2)}) collective-permute-start(bf16[4,1024,128]{2,1,0:T(8,128)(2,1)S(1)} %get-tuple-element.47.a_ref), channel_id=1, source_target_pairs={{0,8},{24,16},{1,9},{25,17},{2,10},{26,18},{3,11},{27,19},{4,12},{... | collective-permute-start | bytes 3145736 | tf_op jit(solution)/shard_map/ppermute | solution.py:250
  165.9 18.1 %collective-permute-done.13 = bf16[4,1024,128]{2,1,0:T(8,128)(2,1)S(1)} collective-permute-done((bf16[4,1024,128]{2,1,0:T(8,128)(2,1)S(1)}, bf16[4,1024,128]{2,1,0:T(8,128)(2,1)S(1)}, u32[]{:S(2)}, u32[]{:S(2)}) %collective-permute-start.13) | collective-permute-done | bytes 1048608 | tf_op jit(solution)/shard_map/ppermute | solution.py:251
  184.3 1.5 collective-permute-start.16
  185.9 1.9 collective-permute-start.14
  190.7 20.5 %collective-permute-done.16.b_ref = bf16[4,1024,128]{2,1,0:T(8,128)(2,1)S(1)} collective-permute-done((bf16[4,1024,128]{2,1,0:T(8,128)(2,1)S(1)}, bf16[4,1024,128]{2,1,0:T(8,128)(2,1)S(1)}, u32[]{:S(2)}, u32[]{:S(2)}) %collective-permute-start.16) | collective-permute-done | bytes 1048608 | tf_op jit(solution)/shard_map/ppermute | solution.py:253
  212.5 7.3 %base.3.base_ref = f32[8,1024,128]{2,1,0:T(8,128)S(1)} custom-call(f32[8,1024,128]{2,1,0:T(8,128)S(1)} %pad_maximum_fusion.field_ref, f32[2,1024,128]{2,1,0:T(8,128)S(1)} %collective-permute-done.14.before_ref, f32[2,1024,128]{2,1,0:T(8,128)S(1)} %collective-permute-done.15.after_ref, f32[1024,1]{1,0:T(8,128)S(1)} %copy.6.cx_ref, f32[1024,1]{1,0:T(8,128)S(1)} %copy.7.cy_ref, ...), custom_call_target="tpu_custom_call" | custom-call | flops 1000 | bytes 1000 | tf_op jit(solution)/shard_map/base/pallas_call | solution.py:102
  219.8 2.0 copy-done
  221.8 14.1 %gains.6 = (f32[4,1024,128]{2,1,0:T(8,128)S(1)}, bf16[4,1024,128]{2,1,0:T(8,128)(2,1)}, bf16[4,1024,128]{2,1,0:T(8,128)(2,1)S(1)}) custom-call(s32[5]{0:T(128)S(1)} %stack.27.order_ref, bf16[1024,4096]{1,0:T(8,128)(2,1)} %convert_element_type.22.own_w_ref, bf16[1024,3072]{1,0:T(8,128)(2,1)} %all-gather.2.cloned.1.call-done.edge_w_ref, ...), custom_call_target="tpu_custom_call" | custom-call | flops 1000 | bytes 1000 | tf_op jit(solution)/shard_map/gains/pallas_call | solution.py:148
  237.2 14.1 %gains.7 = (f32[4,1024,128]{2,1,0:T(8,128)S(1)}, bf16[4,1024,128]{2,1,0:T(8,128)(2,1)}, bf16[4,1024,128]{2,1,0:T(8,128)(2,1)S(1)}) custom-call(s32[5]{0:T(128)S(1)} %stack.27.order_ref, bf16[1024,4096]{1,0:T(8,128)(2,1)} %convert_element_type.22.own_w_ref, bf16[1024,3072]{1,0:T(8,128)(2,1)} %all-gather.2.cloned.1.call-done.edge_w_ref, ...), custom_call_target="tpu_custom_call" | custom-call | flops 1000 | bytes 1000 | tf_op jit(solution)/shard_map/gains/pallas_call | solution.py:148
  252.6 11.4 %collective-permute-done.19.refs_2_ = bf16[4,1024,128]{2,1,0:T(8,128)(2,1)S(1)} collective-permute-done((bf16[4,1024,128]{2,1,0:T(8,128)(2,1)S(1)}, bf16[4,1024,128]{2,1,0:T(8,128)(2,1)S(1)}, u32[]{:S(2)}, u32[]{:S(2)}) %collective-permute-start.19) | collective-permute-done | bytes 1048608 | tf_op jit(solution)/shard_map/ppermute | solution.py:264
  263.9 36.1 %collective-permute-done.20.refs_3_ = bf16[4,1024,128]{2,1,0:T(8,128)(2,1)S(1)} collective-permute-done((bf16[4,1024,128]{2,1,0:T(8,128)(2,1)S(1)}, bf16[4,1024,128]{2,1,0:T(8,128)(2,1)S(1)}, u32[]{:S(2)}, u32[]{:S(2)}) %collective-permute-start.20) | collective-permute-done | bytes 1048608 | tf_op jit(solution)/shard_map/ppermute | solution.py:264
  300.1 3.2 %unpack.1 = f32[8192,128]{1,0:T(8,128)} custom-call(f32[4,1024,128]{2,1,0:T(8,128)S(1)} %get-tuple-element.39.refs_0_, f32[4,1024,128]{2,1,0:T(8,128)S(1)} %get-tuple-element.42.refs_1_, bf16[4,1024,128]{2,1,0:T(8,128)(2,1)S(1)} %collective-permute-done.19.refs_2_, bf16[4,1024,128]{2,1,0:T(8,128)(2,1)S(1)} %collective-permute-done.20.refs_3_), custom_call_target="tpu_custom_call" | custom-call | flops 1000 | bytes 1000 | tf_op jit(solution)/shard_map/unpack/pallas_call | solution.py:189
  (55 shorter events, 16.0 us)
Async XLA Ops:
  6.5 98.3 %all-gather.2.cloned.1.call-start = ((), (), s32[]{:S(2)}) async-start(), calls=%async_computation | async-start | bytes 7077888 | tf_op jit(solution)/shard_map/all_gather | solution.py:232
  6.5 2.2 copy-start.2
  11.2 27.6 %copy-start.4 = (bf16[4,1024,128]{2,1,0:T(8,128)(2,1)}, bf16[4,1024,128]{2,1,0:T(8,128)(2,1)S(1)}, u32[]{:S(2)}) copy-start(bf16[4,1024,128]{2,1,0:T(8,128)(2,1)S(1)} %get-tuple-element.29.a_ref) | copy-start | bytes 3145732
  11.2 26.6 %collective-permute-start.1 = (bf16[4,1024,128]{2,1,0:T(8,128)(2,1)S(1)}, bf16[4,1024,128]{2,1,0:T(8,128)(2,1)}, u32[]{:S(2)}, u32[]{:S(2)}) collective-permute-start(bf16[4,1024,128]{2,1,0:T(8,128)(2,1)S(1)} %get-tuple-element.29.a_ref), channel_id=1, source_target_pairs={{8,16},{16,8},{9,17},{17,9},{10,18},{18,10},{11,19},{19,11},{12,20... | collective-permute-start | bytes 3145736 | tf_op jit(solution)/shard_map/ppermute | solution.py:231
  14.4 76.9 %copy-start.9 = (s32[8,128]{1,0:T(8,128)S(1)}, s32[8,128]{1,0:T(8,128)}, u32[]{:S(2)}) copy-start(s32[8,128]{1,0:T(8,128)} %param.9) | copy-start | bytes 12292
  14.4 76.9 %copy-start.7 = (f32[2,1024]{1,0:T(2,128)S(1)}, f32[2,1024]{1,0:T(2,128)}, u32[]{:S(2)}) copy-start(f32[2,1024]{1,0:T(2,128)} %param.6) | copy-start | bytes 24580
  14.4 77.3 %copy-start.8 = (f32[1024]{0:T(1024)S(1)}, f32[1024]{0:T(1024)}, u32[]{:S(2)}) copy-start(f32[1024]{0:T(1024)} %param.7) | copy-start | bytes 12292
  14.4 23.4 %collective-permute-start = (bf16[128,3072]{1,0:T(8,128)(2,1)S(1)}, bf16[128,3072]{1,0:T(8,128)(2,1)S(1)}, u32[]{:S(2)}, u32[]{:S(2)}) collective-permute-start(bf16[128,3072]{1,0:T(8,128)(2,1)S(1)} %dynamic_slice.5), channel_id=1, source_target_pairs={{0,8},{24,16},{1,9},{25,17},{2,10},{26,18},{3,11},{27,19},{4,12},{... | collective-permute-start | bytes 2359304 | tf_op jit(solution)/shard_map/ppermute | solution.py:229
  37.8 0.9 copy-start.6
  38.8 25.8 %collective-permute-start.2 = (bf16[4,1024,128]{2,1,0:T(8,128)(2,1)S(1)}, bf16[4,1024,128]{2,1,0:T(8,128)(2,1)}, u32[]{:S(2)}, u32[]{:S(2)}) collective-permute-start(bf16[4,1024,128]{2,1,0:T(8,128)(2,1)S(1)} %get-tuple-element.29.a_ref), channel_id=1, source_target_pairs={{0,8},{24,16},{1,9},{25,17},{2,10},{26,18},{3,11},{27,19},{4,12},{... | collective-permute-start | bytes 3145736 | tf_op jit(solution)/shard_map/ppermute | solution.py:234
  64.6 25.0 %collective-permute-start.10 = (bf16[4,1024,128]{2,1,0:T(8,128)(2,1)S(1)}, bf16[4,1024,128]{2,1,0:T(8,128)(2,1)}, u32[]{:S(2)}, u32[]{:S(2)}) collective-permute-start(bf16[4,1024,128]{2,1,0:T(8,128)(2,1)S(1)} %get-tuple-element.36.a_ref), channel_id=1, source_target_pairs={{0,8},{24,16},{1,9},{25,17},{2,10},{26,18},{3,11},{27,19},{4,12},{... | collective-permute-start | bytes 3145736 | tf_op jit(solution)/shard_map/ppermute | solution.py:235
  70.1 22.0 %collective-permute-start.4 = (f32[2,1024,128]{2,1,0:T(8,128)}, f32[2,1024,128]{2,1,0:T(8,128)}, u32[]{:S(2)}, u32[]{:S(2)}) collective-permute-start(f32[2,1024,128]{2,1,0:T(8,128)} %get-tuple-element.30), channel_id=1, source_target_pairs={{0,1},{1,2},{2,3},{3,4},{4,5},{5,6},{6,7},{8,9},{9,10},{10,11},{11... | collective-permute-start | bytes 3145736 | tf_op jit(solution)/shard_map/ppermute | solution.py:240
  72.3 19.7 %collective-permute-start.5 = (f32[2,1024,128]{2,1,0:T(8,128)}, f32[2,1024,128]{2,1,0:T(8,128)}, u32[]{:S(2)}, u32[]{:S(2)}) collective-permute-start(f32[2,1024,128]{2,1,0:T(8,128)} %get-tuple-element.31), channel_id=1, source_target_pairs={{1,0},{2,1},{3,2},{4,3},{5,4},{6,5},{7,6},{9,8},{10,9},{11,10},{12... | collective-permute-start | bytes 3145736 | tf_op jit(solution)/shard_map/ppermute | solution.py:241
  73.6 31.2 %collective-permute-start.3 = (bf16[4,1024,128]{2,1,0:T(8,128)(2,1)}, bf16[4,1024,128]{2,1,0:T(8,128)(2,1)}, u32[]{:S(2)}, u32[]{:S(2)}) collective-permute-start(bf16[4,1024,128]{2,1,0:T(8,128)(2,1)} %collective-permute-done.2.b_ref), channel_id=1, source_target_pairs={{8,16},{16,8},{9,17},{17,9},{10,18},{18,10},{11,19},{19,11},{12,20... | collective-permute-start | bytes 3145736 | tf_op jit(solution)/shard_map/ppermute | solution.py:236
  75.3 46.4 %collective-permute-start.11 = (bf16[4,1024,128]{2,1,0:T(8,128)(2,1)S(1)}, bf16[4,1024,128]{2,1,0:T(8,128)(2,1)}, u32[]{:S(2)}, u32[]{:S(2)}) collective-permute-start(bf16[4,1024,128]{2,1,0:T(8,128)(2,1)S(1)} %get-tuple-element.36.a_ref), channel_id=1, source_target_pairs={{8,16},{16,8},{9,17},{17,9},{10,18},{18,10},{11,19},{19,11},{12,20... | collective-permute-start | bytes 3145736 | tf_op jit(solution)/shard_map/ppermute | solution.py:233
  89.6 32.2 %collective-permute-start.12 = (bf16[4,1024,128]{2,1,0:T(8,128)(2,1)}, bf16[4,1024,128]{2,1,0:T(8,128)(2,1)}, u32[]{:S(2)}, u32[]{:S(2)}) collective-permute-start(bf16[4,1024,128]{2,1,0:T(8,128)(2,1)} %collective-permute-done.10.b_ref), channel_id=1, source_target_pairs={{8,16},{16,8},{9,17},{17,9},{10,18},{18,10},{11,19},{19,11},{12,20... | collective-permute-start | bytes 3145736 | tf_op jit(solution)/shard_map/ppermute | solution.py:237
  92.0 2.2 copy-start.3
  102.8 2.0 copy-start.1
  104.8 1.2 copy-start.5
  120.4 18.7 %collective-permute-start.6 = (bf16[4,1024,128]{2,1,0:T(8,128)(2,1)S(1)}, bf16[4,1024,128]{2,1,0:T(8,128)(2,1)S(1)}, u32[]{:S(2)}, u32[]{:S(2)}) collective-permute-start(bf16[4,1024,128]{2,1,0:T(8,128)(2,1)S(1)} %get-tuple-element.33), channel_id=1, source_target_pairs={{8,0},{16,24},{9,1},{17,25},{10,2},{18,26},{11,3},{19,27},{12,4},{... | collective-permute-start | bytes 3145736 | tf_op jit(solution)/shard_map/ppermute | solution.py:248
  136.1 47.9 %collective-permute-start.13 = (bf16[4,1024,128]{2,1,0:T(8,128)(2,1)S(1)}, bf16[4,1024,128]{2,1,0:T(8,128)(2,1)S(1)}, u32[]{:S(2)}, u32[]{:S(2)}) collective-permute-start(bf16[4,1024,128]{2,1,0:T(8,128)(2,1)S(1)} %get-tuple-element.38), channel_id=1, source_target_pairs={{8,0},{16,24},{9,1},{17,25},{10,2},{18,26},{11,3},{19,27},{12,4},{... | collective-permute-start | bytes 3145736 | tf_op jit(solution)/shard_map/ppermute | solution.py:251
  137.4 51.8 %collective-permute-start.8 = (bf16[4,1024,128]{2,1,0:T(8,128)(2,1)S(1)}, bf16[4,1024,128]{2,1,0:T(8,128)(2,1)S(1)}, u32[]{:S(2)}, u32[]{:S(2)}) collective-permute-start(bf16[4,1024,128]{2,1,0:T(8,128)(2,1)S(1)} %get-tuple-element.34), channel_id=1, source_target_pairs={{8,16},{16,8},{9,17},{17,9},{10,18},{18,10},{11,19},{19,11},{12,20... | collective-permute-start | bytes 3145736 | tf_op jit(solution)/shard_map/ppermute | solution.py:246
  139.4 49.8 %collective-permute-start.7 = (bf16[4,1024,128]{2,1,0:T(8,128)(2,1)S(1)}, bf16[4,1024,128]{2,1,0:T(8,128)(2,1)S(1)}, u32[]{:S(2)}, u32[]{:S(2)}) collective-permute-start(bf16[4,1024,128]{2,1,0:T(8,128)(2,1)S(1)} %get-tuple-element.47.a_ref), channel_id=1, source_target_pairs={{0,8},{24,16},{1,9},{25,17},{2,10},{26,18},{3,11},{27,19},{4,12},{... | collective-permute-start | bytes 3145736 | tf_op jit(solution)/shard_map/ppermute | solution.py:250
  184.3 27.0 %collective-permute-start.16 = (bf16[4,1024,128]{2,1,0:T(8,128)(2,1)S(1)}, bf16[4,1024,128]{2,1,0:T(8,128)(2,1)S(1)}, u32[]{:S(2)}, u32[]{:S(2)}) collective-permute-start(bf16[4,1024,128]{2,1,0:T(8,128)(2,1)S(1)} %get-tuple-element.45.a_ref), channel_id=1, source_target_pairs={{0,8},{24,16},{1,9},{25,17},{2,10},{26,18},{3,11},{27,19},{4,12},{... | collective-permute-start | bytes 3145736 | tf_op jit(solution)/shard_map/ppermute | solution.py:253
  185.9 26.6 %collective-permute-start.14 = (f32[2,1024,128]{2,1,0:T(8,128)S(1)}, f32[2,1024,128]{2,1,0:T(8,128)S(1)}, u32[]{:S(2)}, u32[]{:S(2)}) collective-permute-start(f32[2,1024,128]{2,1,0:T(8,128)S(1)} %slice.24), channel_id=1, source_target_pairs={{0,1},{1,2},{2,3},{3,4},{4,5},{5,6},{6,7},{8,9},{9,10},{10,11},{11... | collective-permute-start | bytes 3145736 | tf_op jit(solution)/shard_map/ppermute | solution.py:258
  187.9 24.6 %collective-permute-start.15 = (f32[2,1024,128]{2,1,0:T(8,128)S(1)}, f32[2,1024,128]{2,1,0:T(8,128)S(1)}, u32[]{:S(2)}, u32[]{:S(2)}) collective-permute-start(f32[2,1024,128]{2,1,0:T(8,128)S(1)} %slice.25), channel_id=1, source_target_pairs={{1,0},{2,1},{3,2},{4,3},{5,4},{6,5},{7,6},{9,8},{10,9},{11,10},{12... | collective-permute-start | bytes 3145736 | tf_op jit(solution)/shard_map/ppermute | solution.py:259
  189.3 32.5 %collective-permute-start.9 = (bf16[4,1024,128]{2,1,0:T(8,128)(2,1)S(1)}, bf16[4,1024,128]{2,1,0:T(8,128)(2,1)S(1)}, u32[]{:S(2)}, u32[]{:S(2)}) collective-permute-start(bf16[4,1024,128]{2,1,0:T(8,128)(2,1)S(1)} %collective-permute-done.7.b_ref), channel_id=1, source_target_pairs={{8,16},{16,8},{9,17},{17,9},{10,18},{18,10},{11,19},{19,11},{12,20... | collective-permute-start | bytes 3145736 | tf_op jit(solution)/shard_map/ppermute | solution.py:254
  190.0 47.2 %collective-permute-start.17 = (bf16[4,1024,128]{2,1,0:T(8,128)(2,1)S(1)}, bf16[4,1024,128]{2,1,0:T(8,128)(2,1)S(1)}, u32[]{:S(2)}, u32[]{:S(2)}) collective-permute-start(bf16[4,1024,128]{2,1,0:T(8,128)(2,1)S(1)} %get-tuple-element.41), channel_id=1, source_target_pairs={{8,16},{16,8},{9,17},{17,9},{10,18},{18,10},{11,19},{19,11},{12,20... | collective-permute-start | bytes 3145736 | tf_op jit(solution)/shard_map/ppermute | solution.py:247
  211.3 25.9 %collective-permute-start.18 = (bf16[4,1024,128]{2,1,0:T(8,128)(2,1)S(1)}, bf16[4,1024,128]{2,1,0:T(8,128)(2,1)S(1)}, u32[]{:S(2)}, u32[]{:S(2)}) collective-permute-start(bf16[4,1024,128]{2,1,0:T(8,128)(2,1)S(1)} %collective-permute-done.16.b_ref), channel_id=1, source_target_pairs={{8,16},{16,8},{9,17},{17,9},{10,18},{18,10},{11,19},{19,11},{12,20... | collective-permute-start | bytes 3145736 | tf_op jit(solution)/shard_map/ppermute | solution.py:255
  219.7 2.0 copy-start
  235.9 28.1 %collective-permute-start.19 = (bf16[4,1024,128]{2,1,0:T(8,128)(2,1)S(1)}, bf16[4,1024,128]{2,1,0:T(8,128)(2,1)S(1)}, u32[]{:S(2)}, u32[]{:S(2)}) collective-permute-start(bf16[4,1024,128]{2,1,0:T(8,128)(2,1)S(1)} %get-tuple-element.43), channel_id=1, source_target_pairs={{8,0},{16,24},{9,1},{17,25},{10,2},{18,26},{11,3},{19,27},{12,4},{... | collective-permute-start | bytes 3145736 | tf_op jit(solution)/shard_map/ppermute | solution.py:264
  251.3 48.8 %collective-permute-start.20 = (bf16[4,1024,128]{2,1,0:T(8,128)(2,1)S(1)}, bf16[4,1024,128]{2,1,0:T(8,128)(2,1)S(1)}, u32[]{:S(2)}, u32[]{:S(2)}) collective-permute-start(bf16[4,1024,128]{2,1,0:T(8,128)(2,1)S(1)} %get-tuple-element.44), channel_id=1, source_target_pairs={{8,0},{16,24},{9,1},{17,25},{10,2},{18,26},{11,3},{19,27},{12,4},{... | collective-permute-start | bytes 3145736 | tf_op jit(solution)/shard_map/ppermute | solution.py:264
Sparse Core Ops, SparseCore 0:
  38.9 53.1 all-gather.1

commit v2 on v0

v2 whole, which is shorter than its diff:
```python
import functools

import jax
import jax.numpy as jnp
from jax import lax
from jax.experimental import pallas as pl
from jax.experimental.pallas import tpu as pltpu
from jax.sharding import PartitionSpec as P

time_step = 0.25
wall_rate = 2.0
bf16 = jnp.bfloat16
f32 = jnp.float32


def small(limit):
    return dict(
        cost_estimate=pl.CostEstimate(flops=1000, bytes_accessed=1000, transcendentals=0),
        compiler_params=pltpu.CompilerParams(vmem_limit_bytes=limit * 2**20),
    )


def pack_kernel(blocks, field_ref, one_ref, two_ref, low_ref, high_ref, held_ref, done_ref):
    modes, cells = one_ref.shape
    columns = field_ref.shape[1]
    half = cells // columns
    rows = 2 * half
    block = modes // blocks
    copies = []
    for i in range(blocks):
        at = pl.ds(i * block * rows, block * rows)
        copies.append(pltpu.make_async_copy(field_ref.at[at], held_ref.at[at], done_ref.at[i]))
        copies[i].start()
    for i in range(blocks):
        copies[i].wait()
        to = slice(i * block, (i + 1) * block)
        for r in range(rows):
            line = held_ref[pl.ds(i * block * rows + r, block, stride=rows), :]
            to_ref = one_ref if r < half else two_ref
            to_ref[to, r % half * columns:(r % half + 1) * columns] = line.astype(bf16)
            if r < 2:
                low_ref[to, r * columns:(r + 1) * columns] = line
            if r >= rows - 2:
                at = r - rows + 2
                high_ref[to, at * columns:(at + 1) * columns] = line


def pack(field):
    modes, rows, columns = field.shape
    blocks = 4
    shape = lambda count, kind: jax.ShapeDtypeStruct((modes, count * columns), kind)
    return pl.pallas_call(
        functools.partial(pack_kernel, blocks),
        in_specs=[pl.BlockSpec(memory_space=pl.ANY)],
        out_specs=[pl.BlockSpec(memory_space=pltpu.VMEM)] * 4,
        out_shape=[shape(rows // 2, bf16)] * 2 + [shape(2, f32)] * 2,
        scratch_shapes=[pltpu.VMEM((modes * rows, columns), f32), pltpu.SemaphoreType.DMA((blocks,))],
        name="pack",
        **small(46),
    )(field.reshape(modes * rows, columns))


def local_line(lines, r, params, flags):
    cx, cy, rate = params
    centre = lines(r)
    lane = lax.broadcasted_iota(jnp.int32, centre.shape, 1)
    columns = centre.shape[1]

    def moved(by):
        turned = pltpu.roll(centre, by % columns, 1)
        keep = lane >= by if by > 0 else lane < columns + by
        return jnp.where(keep, turned, 0.0)

    back_x = 1.5 * centre - 2.0 * lines(r - 1) + 0.5 * lines(r - 2)
    fwd_x = -1.5 * centre + 2.0 * lines(r + 1) - 0.5 * lines(r + 2)
    back_y = 1.5 * centre - 2.0 * moved(1) + 0.5 * moved(2)
    fwd_y = -1.5 * centre + 2.0 * moved(-1) - 0.5 * moved(-2)
    transport = (
        jnp.maximum(cx, 0.0) * back_x
        + jnp.minimum(cx, 0.0) * fwd_x
        + jnp.maximum(cy, 0.0) * back_y
        + jnp.minimum(cy, 0.0) * fwd_y
    )
    return centre - transport - time_step * (rate * centre + wall_rate * flags * centre)


def column(line):
    count = line.shape[1]
    at = lax.broadcasted_iota(jnp.int32, (count, count), 0)
    lane = lax.broadcasted_iota(jnp.int32, (count, count), 1)
    return jnp.sum(jnp.where(at == lane, line, 0.0), axis=1, keepdims=True)


def base_kernel(rows, modes, strided, *refs):
    *field_refs, before_ref, behind_ref, courant_ref, rate_ref, flags_ref, one_ref, two_ref = refs
    params = (column(courant_ref[0:1, :]), column(courant_ref[1:2, :]), column(rate_ref[...]))
    flags = flags_ref[...].astype(f32)
    columns = flags_ref.shape[1]
    half = rows // 2
    cut = lambda at: slice(at * columns, (at + 1) * columns)

    def lines(r):
        if r < 0:
            return before_ref[:, cut(r + 2)]
        if r >= rows:
            return behind_ref[:, cut(r - rows)]
        if strided:
            return field_refs[0][pl.ds(r, modes, stride=rows), :]
        return field_refs[r // half][:, cut(r % half)]

    for r in range(rows):
        to_ref = one_ref if r < half else two_ref
        to_ref[:, cut(r % half)] = local_line(lines, r, params, flags[r:r + 1, :])


def base(fields, before, behind, courant, rate, flags):
    rows, columns = flags.shape
    modes = before.shape[0]
    block = 128
    spec = lambda count: pl.BlockSpec((block, count * columns), lambda i: (i, 0))
    strided = len(fields) == 1
    if strided:
        field_specs = [pl.BlockSpec((block * rows, columns), lambda i: (i, 0))]
        fields = [fields[0].reshape(modes * rows, columns)]
    else:
        field_specs = [spec(rows // 2)] * 2
    per_mode = lambda count: pl.BlockSpec((count, block), lambda i: (0, i))
    return pl.pallas_call(
        functools.partial(base_kernel, rows, block, strided),
        grid=(modes // block,),
        in_specs=field_specs + [spec(2), spec(2), per_mode(2), per_mode(1), pl.BlockSpec((rows, columns), lambda i: (0, 0))],
        out_specs=[spec(rows // 2)] * 2,
        out_shape=[jax.ShapeDtypeStruct((modes, rows // 2 * columns), f32)] * 2,
        name="base",
        **small(12),
    )(*fields, before, behind, courant, rate.reshape(1, modes), flags)


def piece_kernel(w_ref, out_ref, held_ref, done_ref):
    share, kept = out_ref.shape
    at = pl.multiple_of(lax.axis_index("tile") * share, share)
    skipped = w_ref.shape[1] - kept
    left = pl.multiple_of(jnp.where(lax.axis_index("mode") == 0, skipped, 0), skipped)
    copy = pltpu.make_async_copy(w_ref.at[pl.ds(at, share), pl.ds(left, kept)], held_ref, done_ref)
    copy.start()
    copy.wait()
    out_ref[...] = held_ref[...].astype(bf16)


def piece_of(weights, count):
    modes, depth = weights.shape
    shape = (modes // count, depth - modes)
    return pl.pallas_call(
        piece_kernel,
        in_specs=[pl.BlockSpec(memory_space=pl.ANY)],
        out_specs=pl.BlockSpec(memory_space=pltpu.VMEM),
        out_shape=jax.ShapeDtypeStruct(shape, bf16),
        scratch_shapes=[pltpu.VMEM(shape, f32), pltpu.SemaphoreType.DMA],
        name="piece",
        **small(56),
    )(weights)


def meet_kernel(low, first_ref, sum_ref, field_ref, one_ref, two_ref, side_ref):
    block = 128
    half = one_ref.shape[1]
    side = side_ref.shape[1]

    def step(i, _):
        at = pl.ds(pl.multiple_of(i * block, block), block)
        line = first_ref[at, :] + time_step * sum_ref[at, :].astype(f32)
        field_ref[at, :] = line
        rounded = line.astype(bf16)
        one_ref[at, :] = rounded[:, :half]
        two_ref[at, :] = rounded[:, half:]
        side_ref[at, :] = line[:, :side] if low else line[:, line.shape[1] - side:]
        return 0

    lax.fori_loop(0, first_ref.shape[0] // block, step, 0)


def meet(first, total, columns, low):
    modes, cells = first.shape
    vmem = pl.BlockSpec(memory_space=pltpu.VMEM)
    return pl.pallas_call(
        functools.partial(meet_kernel, low),
        in_specs=[vmem] * 2,
        out_specs=[vmem] * 4,
        out_shape=[
            jax.ShapeDtypeStruct((modes, cells), f32),
            jax.ShapeDtypeStruct((modes, cells // 2), bf16),
            jax.ShapeDtypeStruct((modes, cells // 2), bf16),
            jax.ShapeDtypeStruct((modes, 2 * columns), f32),
        ],
        name="meet",
        **small(12),
    )(first, total)


def cast_kernel(w_ref, out_ref):
    block = w_ref.shape[0]
    out_ref[pl.ds(pl.multiple_of(pl.program_id(0) * block, block), block), :] = w_ref[...].astype(bf16)


def cast(weights):
    block = 128
    return pl.pallas_call(
        cast_kernel,
        grid=(weights.shape[0] // block,),
        in_specs=[pl.BlockSpec((block, weights.shape[1]), lambda i: (i, 0))],
        out_specs=pl.BlockSpec(memory_space=pltpu.VMEM),
        out_shape=jax.ShapeDtypeStruct(weights.shape, bf16),
        name="cast",
        **small(36),
    )(weights)


def product(w_ref, span, parts, ours):
    plane = lax.axis_index("mode")
    beside = plane + 1 - 2 * lax.rem(plane, 2)
    owner = {0: plane, 1: beside, 2: 3 - plane, 3: 3 - beside}
    if not ours:
        skipped = jnp.where(plane < 2, 1, 0)
        owner = {j: jnp.clip(of - skipped, 0, 2) for j, of in owner.items()}
    total = None
    for j, pieces in parts.items():
        depth = pieces[0].shape[0]
        at = pl.multiple_of(owner[j] * depth, depth)
        weights = w_ref[span, pl.ds(at, depth)]
        terms = [jnp.dot(weights, piece[...], preferred_element_type=f32) for piece in pieces]
        term = terms[0] if len(terms) == 1 else jnp.concatenate(terms, axis=1)
        total = term if total is None else total + term
    return total


def parts_of(counts, refs):
    refs = iter(refs)
    return {j: [next(refs) for _ in range(count)] for j, count in counts.items()}


def own_kernel(counts, w_ref, *refs):
    *part_refs, base_ref, first_ref, rounded_ref = refs
    parts = parts_of(counts, part_refs)
    half = w_ref.shape[0] // 2
    for span in (slice(0, half), slice(half, 2 * half)):
        line = base_ref[span, :] + time_step * product(w_ref, span, parts, True)
        first_ref[span, :] = line
        rounded_ref[span, :] = line.astype(bf16)


def sum_kernel(counts, cut, this_ref, other_ref, *refs):
    *part_refs, sum_ref = refs
    parts = parts_of(counts, part_refs)
    if cut is not None:
        parts[2] = [parts[2][0].at[:, cut]]
    share = this_ref.shape[0] // 4
    x, y, core = place()
    for w_ref, of_core in ((this_ref, core), (other_ref, 1 - core)):
        total = product(w_ref, slice(None), parts, False).astype(bf16)
        for k, (of_x, of_y) in enumerate(((x, y), (1 - x, y), (x, 1 - y), (1 - x, 1 - y))):
            at = pl.multiple_of((4 * of_y + 2 * of_x + of_core) * share, share)
            sum_ref[pl.ds(at, share), :] = total[k * share:(k + 1) * share]


def place():
    tile = lax.axis_index("tile")
    return lax.rem(tile // 2, 2), tile // 4, lax.rem(tile, 2)


def gains(kernel, arrays, shape, kinds):
    vmem = pl.BlockSpec(memory_space=pltpu.VMEM)
    return pl.pallas_call(
        kernel,
        in_specs=[vmem] * len(arrays),
        out_specs=[vmem] * len(kinds),
        out_shape=[jax.ShapeDtypeStruct(shape, kind) for kind in kinds],
        name=kernel.func.__name__,
        **small(12),
    )(*arrays)


def own_rows(weights, x, a, b, c, based):
    parts = {0: x, 1: a, 2: b, 3: c}
    kernel = functools.partial(own_kernel, {j: len(part) for j, part in parts.items()})
    return gains(kernel, (weights, *x, *a, *b, *c, based), based.shape, (f32, bf16))


def end_sum(weights, x, b, c, cut=None):
    kernel = functools.partial(sum_kernel, {0: 1, 2: 1, 3: 1}, cut)
    return gains(kernel, (*weights, x, b, c), x.shape, (bf16,))[0]


def stack_kernel(*refs):
    out_ref = refs[-1]
    share = refs[0].shape[0]
    for k, ref in enumerate(refs[:-1]):
        out_ref[k * share:(k + 1) * share, :] = ref[...]


def stack(*pieces):
    share, depth = pieces[0].shape
    vmem = pl.BlockSpec(memory_space=pltpu.VMEM)
    return pl.pallas_call(
        stack_kernel,
        in_specs=[vmem] * len(pieces),
        out_specs=vmem,
        out_shape=jax.ShapeDtypeStruct((len(pieces) * share, depth), bf16),
        name="stack",
        **small(12),
    )(*pieces)


def unpack_kernel(rows, modes, *refs):
    *sum_refs, out_ref = refs[2:]
    columns = out_ref.shape[1]
    half, quarter = rows // 2, rows // 4
    for r in range(rows):
        at = slice(r % half * columns, (r % half + 1) * columns)
        of = slice(r % quarter * columns, (r % quarter + 1) * columns)
        line = refs[r // half][:, at] + time_step * sum_refs[r // quarter][:, of].astype(f32)
        out_ref[pl.ds(r, modes, stride=rows), :] = line


def unpack(firsts, sums, rows):
    modes, cells = firsts[0].shape
    columns = 2 * cells // rows
    block = 256
    spec = lambda count: pl.BlockSpec((block, count), lambda i: (i, 0))
    flat = pl.pallas_call(
        functools.partial(unpack_kernel, rows, block),
        grid=(modes // block,),
        in_specs=[spec(cells)] * 2 + [spec(cells // 2)] * 4,
        out_specs=pl.BlockSpec((block * rows, columns), lambda i: (i, 0)),
        out_shape=jax.ShapeDtypeStruct((modes * rows, columns), f32),
        name="unpack",
        **small(12),
    )(*firsts, *sums)
    return flat.reshape(modes, rows, columns)


inward = [(0, 1), (3, 2)]
outward = [(1, 0), (2, 3)]
across = [(1, 2), (2, 1)]


def line_of_four(distribution, courant, relax_rate, scatter_weight, cell_flags):
    modes, rows, columns = distribution.shape
    count = lax.axis_size("tile")
    up = [(i, i + 1) for i in range(count - 1)]
    down = [(i + 1, i) for i in range(count - 1)]
    send = functools.partial(lax.ppermute, axis_name="mode")
    after = lambda value, *earlier: lax.optimization_barrier((value, *earlier))[0]
    local = functools.partial(base, courant=courant, rate=relax_rate, flags=cell_flags)
    by = lambda value, bits: lax.ppermute(value, "tile", [(i, i ^ bits) for i in range(count)])

    piece = piece_of(scatter_weight, count)
    x1, x2, low, high = pack(distribution)
    piece = send(piece, perm=inward)
    b1 = send(x1, perm=across)
    b2 = send(after(x2, b1), perm=across)
    before = lax.ppermute(high, "tile", up)
    behind = lax.ppermute(low, "tile", down)
    a1 = send(x1, perm=inward)
    own_w = cast(after(scatter_weight, x1))
    base1, base2 = local([distribution], before, behind)
    from_piece = after(piece, own_w)
    px, py, pd = by(from_piece, 2), by(from_piece, 4), by(from_piece, 6)
    a2 = send(after(x2, a1, pd), perm=inward)
    c1 = send(after(a1, base1), perm=across)
    this = stack(after(piece, b2), px, py, pd)
    c2 = send(after(a2, this, pd), perm=across)
    edge_w = (this, by(after(this, a2, c1), 1))
    first1, own1 = own_rows(own_w, [x1], [a1], [b1], [c1], base1)
    sum1 = end_sum(edge_w, after(x1, own1), b1, c1)
    sum2 = end_sum(edge_w, x2, b2, c2)
    first2, own2 = own_rows(own_w, [after(x2, sum2)], [a2], [b2], [c2], base2)

    b1 = send(own1, perm=across)
    b2 = send(own2, perm=across)
    field1, x1, y1, low = meet(first1, send(sum1, perm=outward), columns, True)
    a1 = send(after(x1, b1), perm=inward)
    d1 = send(after(y1, b1), perm=inward)
    field2, x2, y2, high = meet(first2, send(sum2, perm=outward), columns, False)
    a2 = send(after(x2, b2), perm=inward)
    d2 = send(after(y2, b2, a2), perm=inward)
    c1 = send(a1, perm=across)
    e1 = send(d1, perm=across)
    half = b1.shape[1] // 2
    left, right = slice(0, half), slice(half, 2 * half)
    sum1 = end_sum(edge_w, x1, b1, c1, left)
    out1 = send(sum1, perm=outward)
    rum1 = end_sum(edge_w, y1, b1, e1, right)
    rut1 = send(after(rum1, out1), perm=outward)
    before = lax.ppermute(after(high, b2, d1), "tile", up)
    behind = lax.ppermute(after(low, b2, d1), "tile", down)
    base1, base2 = local([field1, field2], before, behind)
    c2 = send(a2, perm=across)
    e2 = send(after(d2, c2), perm=across)
    sum2 = end_sum(edge_w, after(x2, rum1, before), b2, c2, left)
    out2 = send(after(sum2, rut1, out1), perm=outward)
    rum2 = end_sum(edge_w, after(y2, sum2, base1), b2, e2, right)
    first1, _ = own_rows(own_w, [x1, y1], [a1, d1], [b1], [c1, e1], base1)
    rut2 = send(after(rum2, out2), perm=outward)
    first2, _ = own_rows(own_w, [after(x2, sum2), y2], [a2, d2], [b2], [c2, e2], base2)
    return unpack([first1, first2], [out1, rut1, out2, rut2], rows)


def extended(block, width):
    count = lax.axis_size("tile")
    up = [(i, i + 1) for i in range(count - 1)]
    down = [(i + 1, i) for i in range(count - 1)]
    low = lax.ppermute(block[:, -width:], "tile", up)
    high = lax.ppermute(block[:, :width], "tile", down)
    return jnp.concatenate([low, block, high], axis=1)


def gathered(distribution, courant, relax_rate, scatter_weight, cell_flags):
    cx = courant[0][:, None, None]
    cy = courant[1][:, None, None]
    rate = relax_rate[:, None, None]
    flags = cell_flags.astype(f32)[None]
    weight = scatter_weight.astype(bf16)
    field = distribution
    for step in range(2):
        full = jnp.pad(extended(field, 2), ((0, 0), (0, 0), (2, 2)))
        centre = full[:, 2:-2, 2:-2]
        back_x = 1.5 * centre - 2.0 * full[:, 1:-3, 2:-2] + 0.5 * full[:, :-4, 2:-2]
        fwd_x = -1.5 * centre + 2.0 * full[:, 3:-1, 2:-2] - 0.5 * full[:, 4:, 2:-2]
        back_y = 1.5 * centre - 2.0 * full[:, 2:-2, 1:-3] + 0.5 * full[:, 2:-2, :-4]
        fwd_y = -1.5 * centre + 2.0 * full[:, 2:-2, 3:-1] - 0.5 * full[:, 2:-2, 4:]
        transport = (
            jnp.maximum(cx, 0.0) * back_x
            + jnp.minimum(cx, 0.0) * fwd_x
            + jnp.maximum(cy, 0.0) * back_y
            + jnp.minimum(cy, 0.0) * fwd_y
        )
        flat = field.astype(bf16).reshape(field.shape[0], -1)
        flat = lax.all_gather(flat, "mode", axis=0, tiled=True)
        gain = jnp.dot(weight, flat, preferred_element_type=f32).reshape(field.shape)
        field = field - transport + time_step * (gain - rate * field - wall_rate * flags * field)
    return field


def body(*args):
    if lax.axis_size("mode") == 4 and lax.axis_size("tile") == 8 and args[0].shape[1] % 4 == 0:
        return line_of_four(*args)
    return gathered(*args)


def solution(mesh):
    in_specs = (
        P("mode", "tile", None),
        P(None, "mode"),
        P("mode"),
        P("mode", None),
        P("tile", None),
    )
    out_specs = P("mode", "tile", None)
    return jax.shard_map(body, mesh=mesh, in_specs=in_specs, out_specs=out_specs, check_vma=False)
```

time: 399 us -> 228 us (0.57)
  waiting for transfers between devices: 262 us -> 85.2 us
  starting transfers between devices: 10.8 us -> 78.1 us
  Pallas kernels: 0 us -> 63.5 us
  matrix products: 61.5 us -> 0 us
  other arithmetic: 25.4 us -> 0 us
  local copies, waits for them, and re-layouts: 24.7 us -> 0.03 us
  between operations: 13.6 us -> 0.54 us
    all_gather x2 -> x0, waiting for transfers between devices: 261 us -> none  [collide(): lax.all_gather(flat, 'mode', axis=0, tiled=True).astype(jnp.float32)]
    ppermute x4 -> x31, waiting for transfers between devices: 1.28 us -> 85.2 us  [the longest x1 22.3 us: line_of_four(): field1, x1, y1, low = meet(first1, send(sum1, perm=outward), columns, True)]
    ppermute x4 -> x31, starting transfers between devices: 10.7 us -> 78.1 us  [the longest x1 15.3 us: line_of_four(): a1 = send(after(x1, b1), perm=inward)]
    pallas_call x0 -> x19, Pallas kernels: none -> 63.5 us  [the longest x10 33.9 us: gains(): pl.pallas_call(kernel, in_specs=[vmem] * len(arrays), out_specs=[vmem] *...]
    dot_general x2 -> x0, matrix products: 61.5 us -> none  [collide(): jnp.dot(scatter_weight, lax.all_gather(flat, 'mode', axis=0, tiled=True)....]
    concatenate x2 -> x0, other arithmetic: 10 us -> none  [extended(): block = jnp.concatenate([low, block, high], axis=dim)]
    convert_element_type x2 -> x0, other arithmetic: 8.96 us -> none  [collide(): rounded = field.astype(jnp.bfloat16)]
    unnamed x18 -> x8, local copies, waits for them, and re-layouts: 7.77 us -> 0.03 us
  transfers between devices with their start and end apart: 6 -> 31, of which waited for: 3 -> 13; matrix products, arithmetic and copies ran while one was open for 7% -> 0% of each run, Pallas kernels for 0% -> 26%
where the time goes in v2:
time: 228 us; the launch traced here: 227 us
  waiting for transfers between devices  85.2 us (37%)
  starting transfers between devices  78.1 us (34%)
  Pallas kernels  63.5 us (28%)
    pallas_call x10, Pallas kernels, gains(): pl.pallas_call(kernel, in_specs=[vmem] * len(arrays), out_specs=[vmem] *...  33.9 us
    ppermute x1, waiting for transfers between devices, line_of_four(): field1, x1, y1, low = meet(first1, send(sum1, perm=outward), columns, True)  22.3 us
    ppermute x4, waiting for transfers between devices, line_of_four(): lax.ppermute(value, 'tile', [(i, i ^ bits) for i in range(count)])  16.5 us
    ppermute x1, starting transfers between devices, line_of_four(): a1 = send(after(x1, b1), perm=inward)  15.3 us
    pallas_call x2, Pallas kernels, base(): pl.pallas_call(functools.partial(base_kernel, rows, block, strided), grid...  13 us
    ppermute x4, starting transfers between devices, line_of_four(): lax.ppermute(value, 'tile', [(i, i ^ bits) for i in range(count)])  11.9 us
    ppermute x1, waiting for transfers between devices, line_of_four(): a1 = send(after(x1, b1), perm=inward)  11 us
    ppermute x1, waiting for transfers between devices, line_of_four(): rut1 = send(after(rum1, out1), perm=outward)  10.9 us
  transfers between devices with their start and end apart: 31, of which 13 were waited for; matrix products, arithmetic and copies ran while one was open for 0% of the time, Pallas kernels for 26%

profile of v2, /device:TPU:0, one launch (start us, length us, event | category | flops | bytes accessed | tf_op | source)
XLA Modules:
  0.0 227.4 jit_solution(8141957719855578887)
XLA Ops:
  0.0 2.4 %piece.1 = bf16[128,3072]{1,0:T(8,128)(2,1)} custom-call(f32[1024,4096]{1,0:T(8,128)} %w_ref.2), custom_call_target="tpu_custom_call" | custom-call | flops 1000 | bytes 1000 | tf_op jit(solution)/shard_map/piece/pallas_call | solution.py:153
  2.4 5.0 %collective-permute-start.5 = (bf16[128,3072]{1,0:T(8,128)(2,1)}, bf16[128,3072]{1,0:T(8,128)(2,1)S(1)}, u32[]{:S(2)}, u32[]{:S(2)}) collective-permute-start(bf16[128,3072]{1,0:T(8,128)(2,1)} %piece.1), channel_id=1, source_target_pairs={{0,8},{24,16},{1,9},{25,17},{2,10},{26,18},{3,11},{27,19},{4,12},{... | collective-permute-start | bytes 2359304 | tf_op jit(solution)/shard_map/ppermute | solution.py:358
  7.4 2.4 %pack.1 = (bf16[1024,512]{1,0:T(8,128)(2,1)S(1)}, bf16[1024,512]{1,0:T(8,128)(2,1)S(1)}, f32[1024,256]{1,0:T(8,128)S(1)}, f32[1024,256]{1,0:T(8,128)S(1)}) custom-call(f32[8192,128]{1,0:T(8,128)} %bitcast.3), custom_call_target="tpu_custom_call" | custom-call | flops 1000 | bytes 1000 | tf_op jit(solution)/shard_map/pack/pallas_call | solution.py:52
  13.5 4.1 %collective-permute-start = (bf16[1024,512]{1,0:T(8,128)(2,1)S(1)}, bf16[1024,512]{1,0:T(8,128)(2,1)S(1)}, u32[]{:S(2)}, u32[]{:S(2)}) collective-permute-start(bf16[1024,512]{1,0:T(8,128)(2,1)S(1)} %get-tuple-element.64.refs_0_), channel_id=1, source_target_pairs={{0,8},{24,16},{1,9},{25,17},{2,10},{26,18},{3,11},{27,19},{4,12},{... | collective-permute-start | bytes 3145736 | tf_op jit(solution)/shard_map/ppermute | solution.py:363
  17.6 8.1 %cast.1.w_ref = bf16[1024,4096]{1,0:T(8,128)(2,1)S(1)} custom-call(f32[1024,4096]{1,0:T(8,128)} %w_ref.2), custom_call_target="tpu_custom_call" | custom-call | flops 1000 | bytes 1000 | tf_op jit(solution)/shard_map/cast/pallas_call | solution.py:207
  25.7 5.3 %collective-permute-start.9 = (bf16[128,3072]{1,0:T(8,128)(2,1)S(1)}, bf16[128,3072]{1,0:T(8,128)(2,1)S(1)}, u32[]{:S(2)}, u32[]{:S(2)}) collective-permute-start(bf16[128,3072]{1,0:T(8,128)(2,1)S(1)} %collective-permute-done.5.refs_0_), channel_id=1, source_target_pairs={{0,6},{1,7},{2,4},{3,5},{4,2},{5,3},{6,0},{7,1},{8,14},{9,15},{10,... | collective-permute-start | bytes 2359304 | tf_op jit(solution)/shard_map/ppermute | solution.py:354
  31.8 6.7 %base.2 = (f32[1024,512]{1,0:T(8,128)S(1)}, f32[1024,512]{1,0:T(8,128)S(1)}) custom-call(f32[8192,128]{1,0:T(8,128)S(1)} %bitcast.4, f32[1024,256]{1,0:T(8,128)S(1)} %collective-permute-done.2.refs_1_, f32[1024,256]{1,0:T(8,128)S(1)} %collective-permute-done.3.refs_2_, f32[2,1024]{1,0:T(2,128)S(1)} %copy-done.1, f32[1,1024]{1,0:T(1,128)S(1)} %bitcast.5, ...), custom_call_target="tpu_custom_call" | custom-call | flops 1000 | bytes 1000 | tf_op jit(solution)/shard_map/base/pallas_call | solution.py:128
  38.5 8.3 %collective-permute-done.refs_1_ = bf16[1024,512]{1,0:T(8,128)(2,1)S(1)} collective-permute-done((bf16[1024,512]{1,0:T(8,128)(2,1)S(1)}, bf16[1024,512]{1,0:T(8,128)(2,1)S(1)}, u32[]{:S(2)}, u32[]{:S(2)}) %collective-permute-start) | collective-permute-done | bytes 1048608 | tf_op jit(solution)/shard_map/ppermute | solution.py:363
  48.5 6.3 %collective-permute-start.10 = (bf16[1024,512]{1,0:T(8,128)(2,1)S(1)}, bf16[1024,512]{1,0:T(8,128)(2,1)S(1)}, u32[]{:S(2)}, u32[]{:S(2)}) collective-permute-start(bf16[1024,512]{1,0:T(8,128)(2,1)S(1)} %get-tuple-element.71.refs_0_), channel_id=1, source_target_pairs={{0,8},{24,16},{1,9},{25,17},{2,10},{26,18},{3,11},{27,19},{4,12},{... | collective-permute-start | bytes 3145736 | tf_op jit(solution)/shard_map/ppermute | solution.py:368
  54.7 6.6 %collective-permute-start.7 = (bf16[128,3072]{1,0:T(8,128)(2,1)S(1)}, bf16[128,3072]{1,0:T(8,128)(2,1)S(1)}, u32[]{:S(2)}, u32[]{:S(2)}) collective-permute-start(bf16[128,3072]{1,0:T(8,128)(2,1)S(1)} %collective-permute-done.5.refs_0_), channel_id=1, source_target_pairs={{0,2},{1,3},{2,0},{3,1},{4,6},{5,7},{6,4},{7,5},{8,10},{9,11},{10,... | collective-permute-start | bytes 2359304 | tf_op jit(solution)/shard_map/ppermute | solution.py:354
  61.4 13.6 %collective-permute-done.7.refs_1_ = bf16[128,3072]{1,0:T(8,128)(2,1)S(1)} collective-permute-done((bf16[128,3072]{1,0:T(8,128)(2,1)S(1)}, bf16[128,3072]{1,0:T(8,128)(2,1)S(1)}, u32[]{:S(2)}, u32[]{:S(2)}) %collective-permute-start.7) | collective-permute-done | bytes 786464 | tf_op jit(solution)/shard_map/ppermute | solution.py:354
  78.1 4.5 %own_kernel.4 = (f32[1024,512]{1,0:T(8,128)S(1)}, bf16[1024,512]{1,0:T(8,128)(2,1)S(1)}) custom-call(bf16[1024,4096]{1,0:T(8,128)(2,1)S(1)} %cast.1.w_ref, bf16[1024,512]{1,0:T(8,128)(2,1)S(1)} %get-tuple-element.64.refs_0_, bf16[1024,512]{1,0:T(8,128)(2,1)S(1)} %collective-permute-done.refs_1_, ...), custom_call_target="tpu_custom_call" | custom-call | flops 1000 | bytes 1000 | tf_op jit(solution)/shard_map/own_kernel/pallas_call | solution.py:272
  83.0 3.4 %sum_kernel.6 = bf16[1024,512]{1,0:T(8,128)(2,1)S(1)} custom-call(bf16[512,3072]{1,0:T(8,128)(2,1)S(1)} %stack.1.this_ref, bf16[512,3072]{1,0:T(8,128)(2,1)S(1)} %collective-permute-done.11.other_ref, bf16[1024,512]{1,0:T(8,128)(2,1)S(1)} %get-tuple-element.64.refs_0_, bf16[1024,512]{1,0:T(8,128)(2,1)S(1)} %collective-permute-done.1.refs_2_.refs_1_, ...), custom_call_target="tpu_custom_call" | custom-call | flops 1000 | bytes 1000 | tf_op jit(solution)/shard_map/sum_kernel/pallas_call | solution.py:272
  88.5 3.4 %sum_kernel.7 = bf16[1024,512]{1,0:T(8,128)(2,1)S(1)} custom-call(bf16[512,3072]{1,0:T(8,128)(2,1)S(1)} %stack.1.this_ref, bf16[512,3072]{1,0:T(8,128)(2,1)S(1)} %collective-permute-done.11.other_ref, bf16[1024,512]{1,0:T(8,128)(2,1)S(1)} %get-tuple-element.71.refs_0_, bf16[1024,512]{1,0:T(8,128)(2,1)S(1)} %collective-permute-done.6.refs_1_.refs_2_, ...), custom_call_target="tpu_custom_call" | custom-call | flops 1000 | bytes 1000 | tf_op jit(solution)/shard_map/sum_kernel/pallas_call | solution.py:272
  93.4 4.5 %own_kernel.5 = (f32[1024,512]{1,0:T(8,128)S(1)}, bf16[1024,512]{1,0:T(8,128)(2,1)S(1)}) custom-call(bf16[1024,4096]{1,0:T(8,128)(2,1)S(1)} %cast.1.w_ref, bf16[1024,512]{1,0:T(8,128)(2,1)S(1)} %get-tuple-element.71.refs_0_, bf16[1024,512]{1,0:T(8,128)(2,1)S(1)} %collective-permute-done.10.refs_1_, ...), custom_call_target="tpu_custom_call" | custom-call | flops 1000 | bytes 1000 | tf_op jit(solution)/shard_map/own_kernel/pallas_call | solution.py:272
  98.6 22.3 %collective-permute-done.12.sum_ref = bf16[1024,512]{1,0:T(8,128)(2,1)S(1)} collective-permute-done((bf16[1024,512]{1,0:T(8,128)(2,1)S(1)}, bf16[1024,512]{1,0:T(8,128)(2,1)S(1)}, u32[]{:S(2)}, u32[]{:S(2)}) %collective-permute-start.12) | collective-permute-done | bytes 1048608 | tf_op jit(solution)/shard_map/ppermute | solution.py:380
  121.3 15.3 %collective-permute-start.14 = (bf16[1024,256]{1,0:T(8,128)(2,1)S(1)}, bf16[1024,256]{1,0:T(8,128)(2,1)S(1)}, u32[]{:S(2)}, u32[]{:S(2)}) collective-permute-start(bf16[1024,256]{1,0:T(8,128)(2,1)S(1)} %get-tuple-element.67.refs_0_), channel_id=1, source_target_pairs={{0,8},{24,16},{1,9},{25,17},{2,10},{26,18},{3,11},{27,19},{4,12},{... | collective-permute-start | bytes 1572872 | tf_op jit(solution)/shard_map/ppermute | solution.py:381
  137.9 11.0 %collective-permute-done.14.refs_2_ = bf16[1024,256]{1,0:T(8,128)(2,1)S(1)} collective-permute-done((bf16[1024,256]{1,0:T(8,128)(2,1)S(1)}, bf16[1024,256]{1,0:T(8,128)(2,1)S(1)}, u32[]{:S(2)}, u32[]{:S(2)}) %collective-permute-start.14) | collective-permute-done | bytes 524320 | tf_op jit(solution)/shard_map/ppermute | solution.py:381
  150.0 9.1 %collective-permute-start.23 = (bf16[1024,256]{1,0:T(8,128)(2,1)S(1)}, bf16[1024,256]{1,0:T(8,128)(2,1)S(1)}, u32[]{:S(2)}, u32[]{:S(2)}) collective-permute-start(bf16[1024,256]{1,0:T(8,128)(2,1)S(1)} %get-tuple-element.85.refs_0_), channel_id=1, source_target_pairs={{0,8},{24,16},{1,9},{25,17},{2,10},{26,18},{3,11},{27,19},{4,12},{... | collective-permute-start | bytes 1572872 | tf_op jit(solution)/shard_map/ppermute | solution.py:384
  161.1 1.8 sum_kernel.10
  164.2 5.4 %collective-permute-done.23.refs_2_ = bf16[1024,256]{1,0:T(8,128)(2,1)S(1)} collective-permute-done((bf16[1024,256]{1,0:T(8,128)(2,1)S(1)}, bf16[1024,256]{1,0:T(8,128)(2,1)S(1)}, u32[]{:S(2)}, u32[]{:S(2)}) %collective-permute-start.23) | collective-permute-done | bytes 524320 | tf_op jit(solution)/shard_map/ppermute | solution.py:384
  169.7 4.4 %collective-permute-start.25 = (bf16[1024,256]{1,0:T(8,128)(2,1)S(1)}, bf16[1024,256]{1,0:T(8,128)(2,1)S(1)}, u32[]{:S(2)}, u32[]{:S(2)}) collective-permute-start(bf16[1024,256]{1,0:T(8,128)(2,1)S(1)} %get-tuple-element.93.refs_1_.refs_0_), channel_id=1, source_target_pairs={{0,8},{24,16},{1,9},{25,17},{2,10},{26,18},{3,11},{27,19},{4,12},{... | collective-permute-start | bytes 1572872 | tf_op jit(solution)/shard_map/ppermute | solution.py:385
  176.1 1.8 sum_kernel.8
  177.9 5.2 %collective-permute-done.27.refs_2_ = bf16[1024,256]{1,0:T(8,128)(2,1)S(1)} collective-permute-done((bf16[1024,256]{1,0:T(8,128)(2,1)S(1)}, bf16[1024,256]{1,0:T(8,128)(2,1)S(1)}, u32[]{:S(2)}, u32[]{:S(2)}) %collective-permute-start.27) | collective-permute-done | bytes 524320 | tf_op jit(solution)/shard_map/ppermute | solution.py:391
  185.1 1.8 sum_kernel.9
  186.9 10.9 %collective-permute-done.28.refs_3_ = bf16[1024,256]{1,0:T(8,128)(2,1)S(1)} collective-permute-done((bf16[1024,256]{1,0:T(8,128)(2,1)S(1)}, bf16[1024,256]{1,0:T(8,128)(2,1)S(1)}, u32[]{:S(2)}, u32[]{:S(2)}) %collective-permute-start.28) | collective-permute-done | bytes 524320 | tf_op jit(solution)/shard_map/ppermute | solution.py:393
  199.1 6.2 %base.3 = (f32[1024,512]{1,0:T(8,128)S(1)}, f32[1024,512]{1,0:T(8,128)S(1)}) custom-call(f32[1024,512]{1,0:T(8,128)S(1)} %get-tuple-element.69.refs_0_, f32[1024,512]{1,0:T(8,128)S(1)} %get-tuple-element.74.refs_1_, f32[1024,256]{1,0:T(8,128)S(1)} %collective-permute-done.21.refs_2_, f32[1024,256]{1,0:T(8,128)S(1)} %collective-permute-done.22.refs_3_, ...), custom_call_target="tpu_custom_call" | custom-call | flops 1000 | bytes 1000 | tf_op jit(solution)/shard_map/base/pallas_call | solution.py:128
  205.4 1.8 sum_kernel.11
  207.2 4.4 %collective-permute-done.29.refs_4_ = bf16[1024,256]{1,0:T(8,128)(2,1)S(1)} collective-permute-done((bf16[1024,256]{1,0:T(8,128)(2,1)S(1)}, bf16[1024,256]{1,0:T(8,128)(2,1)S(1)}, u32[]{:S(2)}, u32[]{:S(2)}) %collective-permute-start.29) | collective-permute-done | bytes 524320 | tf_op jit(solution)/shard_map/ppermute | solution.py:400
  213.1 5.5 %own_kernel.6 = (f32[1024,512]{1,0:T(8,128)S(1)}, bf16[1024,512]{1,0:T(8,128)(2,1)}) custom-call(bf16[1024,4096]{1,0:T(8,128)(2,1)S(1)} %cast.1.w_ref, bf16[1024,256]{1,0:T(8,128)(2,1)S(1)} %get-tuple-element.67.refs_0_, bf16[1024,256]{1,0:T(8,128)(2,1)S(1)} %get-tuple-element.68.refs_1_.refs_0_, bf16[1024,256]{1,0:T(8,128)(2,1)S(1)} %collective-permute-done.14.refs_2_, ...), custom_call_target="tpu_custom_call" | custom-call | flops 1000 | bytes 1000 | tf_op jit(solution)/shard_map/own_kernel/pallas_call | solution.py:272
  218.6 5.5 %own_kernel.7 = (f32[1024,512]{1,0:T(8,128)S(1)}, bf16[1024,512]{1,0:T(8,128)(2,1)}) custom-call(bf16[1024,4096]{1,0:T(8,128)(2,1)S(1)} %cast.1.w_ref, bf16[1024,256]{1,0:T(8,128)(2,1)S(1)} %get-tuple-element.85.refs_0_, bf16[1024,256]{1,0:T(8,128)(2,1)S(1)} %get-tuple-element.93.refs_1_.refs_0_, bf16[1024,256]{1,0:T(8,128)(2,1)S(1)} %collective-permute-done.23.refs_2_, ...), custom_call_target="tpu_custom_call" | custom-call | flops 1000 | bytes 1000 | tf_op jit(solution)/shard_map/own_kernel/pallas_call | solution.py:272
  224.5 2.9 %unpack.1 = f32[8192,128]{1,0:T(8,128)} custom-call(f32[1024,512]{1,0:T(8,128)S(1)} %get-tuple-element.81.refs_0_, f32[1024,512]{1,0:T(8,128)S(1)} %get-tuple-element.90.refs_1_, bf16[1024,256]{1,0:T(8,128)(2,1)S(1)} %collective-permute-done.27.refs_2_, bf16[1024,256]{1,0:T(8,128)(2,1)S(1)} %collective-permute-done.28.refs_3_, ...), custom_call_target="tpu_custom_call" | custom-call | flops 1000 | bytes 1000 | tf_op jit(solution)/shard_map/unpack/pallas_call | solution.py:329
  (57 shorter events, 27.2 us)
Async XLA Ops:
  2.4 23.3 %collective-permute-start.5 = (bf16[128,3072]{1,0:T(8,128)(2,1)}, bf16[128,3072]{1,0:T(8,128)(2,1)S(1)}, u32[]{:S(2)}, u32[]{:S(2)}) collective-permute-start(bf16[128,3072]{1,0:T(8,128)(2,1)} %piece.1), channel_id=1, source_target_pairs={{0,8},{24,16},{1,9},{25,17},{2,10},{26,18},{3,11},{27,19},{4,12},{... | collective-permute-start | bytes 2359304 | tf_op jit(solution)/shard_map/ppermute | solution.py:358
  9.8 21.2 %collective-permute-start.1 = (bf16[1024,512]{1,0:T(8,128)(2,1)S(1)}, bf16[1024,512]{1,0:T(8,128)(2,1)S(1)}, u32[]{:S(2)}, u32[]{:S(2)}) collective-permute-start(bf16[1024,512]{1,0:T(8,128)(2,1)S(1)} %get-tuple-element.64.refs_0_), channel_id=1, source_target_pairs={{8,16},{16,8},{9,17},{17,9},{10,18},{18,10},{11,19},{19,11},{12,20... | collective-permute-start | bytes 3145736 | tf_op jit(solution)/shard_map/ppermute | solution.py:359
  10.5 21.2 %collective-permute-start.2 = (f32[1024,256]{1,0:T(8,128)S(1)}, f32[1024,256]{1,0:T(8,128)S(1)}, u32[]{:S(2)}, u32[]{:S(2)}) collective-permute-start(f32[1024,256]{1,0:T(8,128)S(1)} %get-tuple-element.52), channel_id=1, source_target_pairs={{0,1},{1,2},{2,3},{3,4},{4,5},{5,6},{6,7},{8,9},{9,10},{10,11},{11... | collective-permute-start | bytes 3145736 | tf_op jit(solution)/shard_map/ppermute | solution.py:361
  12.1 19.6 %copy-start.1 = (f32[2,1024]{1,0:T(2,128)S(1)}, f32[2,1024]{1,0:T(2,128)}, u32[]{:S(2)}) copy-start(f32[2,1024]{1,0:T(2,128)} %refs_4_.1) | copy-start | bytes 24580
  12.1 19.6 %collective-permute-start.3 = (f32[1024,256]{1,0:T(8,128)S(1)}, f32[1024,256]{1,0:T(8,128)S(1)}, u32[]{:S(2)}, u32[]{:S(2)}) collective-permute-start(f32[1024,256]{1,0:T(8,128)S(1)} %get-tuple-element.53), channel_id=1, source_target_pairs={{1,0},{2,1},{3,2},{4,3},{5,4},{6,5},{7,6},{9,8},{10,9},{11,10},{12... | collective-permute-start | bytes 3145736 | tf_op jit(solution)/shard_map/ppermute | solution.py:362
  13.5 33.2 %collective-permute-start = (bf16[1024,512]{1,0:T(8,128)(2,1)S(1)}, bf16[1024,512]{1,0:T(8,128)(2,1)S(1)}, u32[]{:S(2)}, u32[]{:S(2)}) collective-permute-start(bf16[1024,512]{1,0:T(8,128)(2,1)S(1)} %get-tuple-element.64.refs_0_), channel_id=1, source_target_pairs={{0,8},{24,16},{1,9},{25,17},{2,10},{26,18},{3,11},{27,19},{4,12},{... | collective-permute-start | bytes 3145736 | tf_op jit(solution)/shard_map/ppermute | solution.py:363
  25.7 22.7 %collective-permute-start.9 = (bf16[128,3072]{1,0:T(8,128)(2,1)S(1)}, bf16[128,3072]{1,0:T(8,128)(2,1)S(1)}, u32[]{:S(2)}, u32[]{:S(2)}) collective-permute-start(bf16[128,3072]{1,0:T(8,128)(2,1)S(1)} %collective-permute-done.5.refs_0_), channel_id=1, source_target_pairs={{0,6},{1,7},{2,4},{3,5},{4,2},{5,3},{6,0},{7,1},{8,14},{9,15},{10,... | collective-permute-start | bytes 2359304 | tf_op jit(solution)/shard_map/ppermute | solution.py:354
  31.0 30.4 %collective-permute-start.6 = (bf16[1024,512]{1,0:T(8,128)(2,1)S(1)}, bf16[1024,512]{1,0:T(8,128)(2,1)S(1)}, u32[]{:S(2)}, u32[]{:S(2)}) collective-permute-start(bf16[1024,512]{1,0:T(8,128)(2,1)S(1)} %get-tuple-element.71.refs_0_), channel_id=1, source_target_pairs={{8,16},{16,8},{9,17},{17,9},{10,18},{18,10},{11,19},{19,11},{12,20... | collective-permute-start | bytes 3145736 | tf_op jit(solution)/shard_map/ppermute | solution.py:360
  46.8 29.9 %collective-permute-start.4 = (bf16[1024,512]{1,0:T(8,128)(2,1)S(1)}, bf16[1024,512]{1,0:T(8,128)(2,1)S(1)}, u32[]{:S(2)}, u32[]{:S(2)}) collective-permute-start(bf16[1024,512]{1,0:T(8,128)(2,1)S(1)} %collective-permute-done.refs_1_), channel_id=1, source_target_pairs={{8,16},{16,8},{9,17},{17,9},{10,18},{18,10},{11,19},{19,11},{12,20... | collective-permute-start | bytes 3145736 | tf_op jit(solution)/shard_map/ppermute | solution.py:369
  48.5 28.9 %collective-permute-start.10 = (bf16[1024,512]{1,0:T(8,128)(2,1)S(1)}, bf16[1024,512]{1,0:T(8,128)(2,1)S(1)}, u32[]{:S(2)}, u32[]{:S(2)}) collective-permute-start(bf16[1024,512]{1,0:T(8,128)(2,1)S(1)} %get-tuple-element.71.refs_0_), channel_id=1, source_target_pairs={{0,8},{24,16},{1,9},{25,17},{2,10},{26,18},{3,11},{27,19},{4,12},{... | collective-permute-start | bytes 3145736 | tf_op jit(solution)/shard_map/ppermute | solution.py:368
  54.7 20.3 %collective-permute-start.7 = (bf16[128,3072]{1,0:T(8,128)(2,1)S(1)}, bf16[128,3072]{1,0:T(8,128)(2,1)S(1)}, u32[]{:S(2)}, u32[]{:S(2)}) collective-permute-start(bf16[128,3072]{1,0:T(8,128)(2,1)S(1)} %collective-permute-done.5.refs_0_), channel_id=1, source_target_pairs={{0,2},{1,3},{2,0},{3,1},{4,6},{5,7},{6,4},{7,5},{8,10},{9,11},{10,... | collective-permute-start | bytes 2359304 | tf_op jit(solution)/shard_map/ppermute | solution.py:354
  61.3 15.1 %collective-permute-start.8 = (bf16[128,3072]{1,0:T(8,128)(2,1)S(1)}, bf16[128,3072]{1,0:T(8,128)(2,1)S(1)}, u32[]{:S(2)}, u32[]{:S(2)}) collective-permute-start(bf16[128,3072]{1,0:T(8,128)(2,1)S(1)} %collective-permute-done.5.refs_0_), channel_id=1, source_target_pairs={{0,4},{1,5},{2,6},{3,7},{4,0},{5,1},{6,2},{7,3},{8,12},{9,13},{10,... | collective-permute-start | bytes 2359304 | tf_op jit(solution)/shard_map/ppermute | solution.py:354
  77.4 5.7 %collective-permute-start.11 = (bf16[512,3072]{1,0:T(8,128)(2,1)S(1)}, bf16[512,3072]{1,0:T(8,128)(2,1)S(1)}, u32[]{:S(2)}, u32[]{:S(2)}) collective-permute-start(bf16[512,3072]{1,0:T(8,128)(2,1)S(1)} %stack.1.this_ref), channel_id=1, source_target_pairs={{0,1},{1,0},{2,3},{3,2},{4,5},{5,4},{6,7},{7,6},{8,9},{9,8},{10,11... | collective-permute-start | bytes 9437192 | tf_op jit(solution)/shard_map/ppermute | solution.py:354
  77.4 11.1 %collective-permute-start.18 = (bf16[1024,512]{1,0:T(8,128)(2,1)S(1)}, bf16[1024,512]{1,0:T(8,128)(2,1)S(1)}, u32[]{:S(2)}, u32[]{:S(2)}) collective-permute-start(bf16[1024,512]{1,0:T(8,128)(2,1)S(1)} %collective-permute-done.10.refs_1_), channel_id=1, source_target_pairs={{8,16},{16,8},{9,17},{17,9},{10,18},{18,10},{11,19},{19,11},{12,20... | collective-permute-start | bytes 3145736 | tf_op jit(solution)/shard_map/ppermute | solution.py:371
  86.5 34.5 %collective-permute-start.12 = (bf16[1024,512]{1,0:T(8,128)(2,1)S(1)}, bf16[1024,512]{1,0:T(8,128)(2,1)S(1)}, u32[]{:S(2)}, u32[]{:S(2)}) collective-permute-start(bf16[1024,512]{1,0:T(8,128)(2,1)S(1)} %sum_kernel.6), channel_id=1, source_target_pairs={{8,0},{16,24},{9,1},{17,25},{10,2},{18,26},{11,3},{19,27},{12,4},{... | collective-permute-start | bytes 3145736 | tf_op jit(solution)/shard_map/ppermute | solution.py:380
  87.8 33.5 %collective-permute-start.13 = (bf16[1024,512]{1,0:T(8,128)(2,1)S(1)}, bf16[1024,512]{1,0:T(8,128)(2,1)S(1)}, u32[]{:S(2)}, u32[]{:S(2)}) collective-permute-start(bf16[1024,512]{1,0:T(8,128)(2,1)S(1)} %get-tuple-element.63), channel_id=1, source_target_pairs={{8,16},{16,8},{9,17},{17,9},{10,18},{18,10},{11,19},{19,11},{12,20... | collective-permute-start | bytes 3145736 | tf_op jit(solution)/shard_map/ppermute | solution.py:378
  91.9 57.7 %collective-permute-start.19 = (bf16[1024,512]{1,0:T(8,128)(2,1)S(1)}, bf16[1024,512]{1,0:T(8,128)(2,1)S(1)}, u32[]{:S(2)}, u32[]{:S(2)}) collective-permute-start(bf16[1024,512]{1,0:T(8,128)(2,1)S(1)} %sum_kernel.7), channel_id=1, source_target_pairs={{8,0},{16,24},{9,1},{17,25},{10,2},{18,26},{11,3},{19,27},{12,4},{... | collective-permute-start | bytes 3145736 | tf_op jit(solution)/shard_map/ppermute | solution.py:383
  97.9 52.1 %collective-permute-start.20 = (bf16[1024,512]{1,0:T(8,128)(2,1)S(1)}, bf16[1024,512]{1,0:T(8,128)(2,1)S(1)}, u32[]{:S(2)}, u32[]{:S(2)}) collective-permute-start(bf16[1024,512]{1,0:T(8,128)(2,1)S(1)} %get-tuple-element.76), channel_id=1, source_target_pairs={{8,16},{16,8},{9,17},{17,9},{10,18},{18,10},{11,19},{19,11},{12,20... | collective-permute-start | bytes 3145736 | tf_op jit(solution)/shard_map/ppermute | solution.py:379
  121.3 27.6 %collective-permute-start.14 = (bf16[1024,256]{1,0:T(8,128)(2,1)S(1)}, bf16[1024,256]{1,0:T(8,128)(2,1)S(1)}, u32[]{:S(2)}, u32[]{:S(2)}) collective-permute-start(bf16[1024,256]{1,0:T(8,128)(2,1)S(1)} %get-tuple-element.67.refs_0_), channel_id=1, source_target_pairs={{0,8},{24,16},{1,9},{25,17},{2,10},{26,18},{3,11},{27,19},{4,12},{... | collective-permute-start | bytes 1572872 | tf_op jit(solution)/shard_map/ppermute | solution.py:381
  136.6 22.5 %collective-permute-start.15 = (bf16[1024,256]{1,0:T(8,128)(2,1)S(1)}, bf16[1024,256]{1,0:T(8,128)(2,1)S(1)}, u32[]{:S(2)}, u32[]{:S(2)}) collective-permute-start(bf16[1024,256]{1,0:T(8,128)(2,1)S(1)} %get-tuple-element.68.refs_1_.refs_0_), channel_id=1, source_target_pairs={{0,8},{24,16},{1,9},{25,17},{2,10},{26,18},{3,11},{27,19},{4,12},{... | collective-permute-start | bytes 1572872 | tf_op jit(solution)/shard_map/ppermute | solution.py:382
  148.9 12.2 %collective-permute-start.16 = (bf16[1024,256]{1,0:T(8,128)(2,1)S(1)}, bf16[1024,256]{1,0:T(8,128)(2,1)S(1)}, u32[]{:S(2)}, u32[]{:S(2)}) collective-permute-start(bf16[1024,256]{1,0:T(8,128)(2,1)S(1)} %collective-permute-done.14.refs_2_), channel_id=1, source_target_pairs={{8,16},{16,8},{9,17},{17,9},{10,18},{18,10},{11,19},{19,11},{12,20... | collective-permute-start | bytes 1572872 | tf_op jit(solution)/shard_map/ppermute | solution.py:386
  150.0 19.7 %collective-permute-start.23 = (bf16[1024,256]{1,0:T(8,128)(2,1)S(1)}, bf16[1024,256]{1,0:T(8,128)(2,1)S(1)}, u32[]{:S(2)}, u32[]{:S(2)}) collective-permute-start(bf16[1024,256]{1,0:T(8,128)(2,1)S(1)} %get-tuple-element.85.refs_0_), channel_id=1, source_target_pairs={{0,8},{24,16},{1,9},{25,17},{2,10},{26,18},{3,11},{27,19},{4,12},{... | collective-permute-start | bytes 1572872 | tf_op jit(solution)/shard_map/ppermute | solution.py:384
  159.1 15.7 %collective-permute-start.17 = (bf16[1024,256]{1,0:T(8,128)(2,1)S(1)}, bf16[1024,256]{1,0:T(8,128)(2,1)S(1)}, u32[]{:S(2)}, u32[]{:S(2)}) collective-permute-start(bf16[1024,256]{1,0:T(8,128)(2,1)S(1)} %collective-permute-done.15.refs_3_), channel_id=1, source_target_pairs={{8,16},{16,8},{9,17},{17,9},{10,18},{18,10},{11,19},{19,11},{12,20... | collective-permute-start | bytes 1572872 | tf_op jit(solution)/shard_map/ppermute | solution.py:387
  159.8 25.4 %collective-permute-start.21 = (f32[1024,256]{1,0:T(8,128)S(1)}, f32[1024,256]{1,0:T(8,128)S(1)}, u32[]{:S(2)}, u32[]{:S(2)}) collective-permute-start(f32[1024,256]{1,0:T(8,128)S(1)} %get-tuple-element.77), channel_id=1, source_target_pairs={{0,1},{1,2},{2,3},{3,4},{4,5},{5,6},{6,7},{8,9},{9,10},{10,11},{11... | collective-permute-start | bytes 3145736 | tf_op jit(solution)/shard_map/ppermute | solution.py:394
  162.9 20.2 %collective-permute-start.27 = (bf16[1024,256]{1,0:T(8,128)(2,1)S(1)}, bf16[1024,256]{1,0:T(8,128)(2,1)S(1)}, u32[]{:S(2)}, u32[]{:S(2)}) collective-permute-start(bf16[1024,256]{1,0:T(8,128)(2,1)S(1)} %sum_kernel.10), channel_id=1, source_target_pairs={{8,0},{16,24},{9,1},{17,25},{10,2},{18,26},{11,3},{19,27},{12,4},{... | collective-permute-start | bytes 1572872 | tf_op jit(solution)/shard_map/ppermute | solution.py:391
  169.7 14.7 %collective-permute-start.25 = (bf16[1024,256]{1,0:T(8,128)(2,1)S(1)}, bf16[1024,256]{1,0:T(8,128)(2,1)S(1)}, u32[]{:S(2)}, u32[]{:S(2)}) collective-permute-start(bf16[1024,256]{1,0:T(8,128)(2,1)S(1)} %get-tuple-element.93.refs_1_.refs_0_), channel_id=1, source_target_pairs={{0,8},{24,16},{1,9},{25,17},{2,10},{26,18},{3,11},{27,19},{4,12},{... | collective-permute-start | bytes 1572872 | tf_op jit(solution)/shard_map/ppermute | solution.py:385
  174.1 10.3 %collective-permute-start.24 = (bf16[1024,256]{1,0:T(8,128)(2,1)S(1)}, bf16[1024,256]{1,0:T(8,128)(2,1)S(1)}, u32[]{:S(2)}, u32[]{:S(2)}) collective-permute-start(bf16[1024,256]{1,0:T(8,128)(2,1)S(1)} %collective-permute-done.23.refs_2_), channel_id=1, source_target_pairs={{8,16},{16,8},{9,17},{17,9},{10,18},{18,10},{11,19},{19,11},{12,20... | collective-permute-start | bytes 1572872 | tf_op jit(solution)/shard_map/ppermute | solution.py:397
  174.8 24.3 %collective-permute-start.22 = (f32[1024,256]{1,0:T(8,128)S(1)}, f32[1024,256]{1,0:T(8,128)S(1)}, u32[]{:S(2)}, u32[]{:S(2)}) collective-permute-start(f32[1024,256]{1,0:T(8,128)S(1)} %get-tuple-element.79), channel_id=1, source_target_pairs={{1,0},{2,1},{3,2},{4,3},{5,4},{6,5},{7,6},{9,8},{10,9},{11,10},{12... | collective-permute-start | bytes 3145736 | tf_op jit(solution)/shard_map/ppermute | solution.py:395
  183.1 14.7 %collective-permute-start.28 = (bf16[1024,256]{1,0:T(8,128)(2,1)S(1)}, bf16[1024,256]{1,0:T(8,128)(2,1)S(1)}, u32[]{:S(2)}, u32[]{:S(2)}) collective-permute-start(bf16[1024,256]{1,0:T(8,128)(2,1)S(1)} %sum_kernel.8), channel_id=1, source_target_pairs={{8,0},{16,24},{9,1},{17,25},{10,2},{18,26},{11,3},{19,27},{12,4},{... | collective-permute-start | bytes 1572872 | tf_op jit(solution)/shard_map/ppermute | solution.py:393
  184.4 21.0 %collective-permute-start.26 = (bf16[1024,256]{1,0:T(8,128)(2,1)S(1)}, bf16[1024,256]{1,0:T(8,128)(2,1)S(1)}, u32[]{:S(2)}, u32[]{:S(2)}) collective-permute-start(bf16[1024,256]{1,0:T(8,128)(2,1)S(1)} %collective-permute-done.25.refs_3_), channel_id=1, source_target_pairs={{8,16},{16,8},{9,17},{17,9},{10,18},{18,10},{11,19},{19,11},{12,20... | collective-permute-start | bytes 1572872 | tf_op jit(solution)/shard_map/ppermute | solution.py:398
  197.8 13.8 %collective-permute-start.29 = (bf16[1024,256]{1,0:T(8,128)(2,1)S(1)}, bf16[1024,256]{1,0:T(8,128)(2,1)S(1)}, u32[]{:S(2)}, u32[]{:S(2)}) collective-permute-start(bf16[1024,256]{1,0:T(8,128)(2,1)S(1)} %sum_kernel.9), channel_id=1, source_target_pairs={{8,0},{16,24},{9,1},{17,25},{10,2},{18,26},{11,3},{19,27},{12,4},{... | collective-permute-start | bytes 1572872 | tf_op jit(solution)/shard_map/ppermute | solution.py:400
  211.6 12.9 %collective-permute-start.30 = (bf16[1024,256]{1,0:T(8,128)(2,1)S(1)}, bf16[1024,256]{1,0:T(8,128)(2,1)S(1)}, u32[]{:S(2)}, u32[]{:S(2)}) collective-permute-start(bf16[1024,256]{1,0:T(8,128)(2,1)S(1)} %sum_kernel.11), channel_id=1, source_target_pairs={{8,0},{16,24},{9,1},{17,25},{10,2},{18,26},{11,3},{19,27},{12,4},{... | collective-permute-start | bytes 1572872 | tf_op jit(solution)/shard_map/ppermute | solution.py:403
  (3 other events, 53.4 us)

commit v3 on v2

--- a/solution.py
+++ b/solution.py
@@ -378,11 +378,11 @@
     b1 = send(own1, perm=across)
     b2 = send(own2, perm=across)
     field1, x1, y1, low = meet(first1, send(sum1, perm=outward), columns, True)
-    a1 = send(after(x1, b1), perm=inward)
+    a1 = send(x1, perm=inward)
     d1 = send(after(y1, b1), perm=inward)
     field2, x2, y2, high = meet(first2, send(sum2, perm=outward), columns, False)
-    a2 = send(after(x2, b2), perm=inward)
-    d2 = send(after(y2, b2, a2), perm=inward)
+    a2 = send(x2, perm=inward)
+    d2 = send(after(y2, a2), perm=inward)
     c1 = send(a1, perm=across)
     e1 = send(d1, perm=across)
     half = b1.shape[1] // 2

time: 228 us -> 227 us (level)
  waiting for transfers between devices: 85.2 us -> 82.9 us
    ppermute x3 -> x2, starting transfers between devices: 28.7 us -> 16 us  [the longest x1 13.2 us: line_of_four(): d2 = send(after(y2, a2), perm=inward)]
    ppermute x3 -> x2, waiting for transfers between devices: 16.4 us -> 4.32 us  [the longest x1 4.32 us: line_of_four(): a2 = send(x2, perm=inward)]
    ppermute x1, starting transfers between devices: 1.32 us -> 9.13 us  [line_of_four(): d1 = send(after(y1, b1), perm=inward)]
    ppermute x1 -> x2, starting transfers between devices: 4.07 us -> 10.2 us  [line_of_four(): a1 = send(x1, perm=inward)]
    ppermute x1, waiting for transfers between devices: 0.01 us -> 4.51 us  [line_of_four(): d1 = send(after(y1, b1), perm=inward)]
    ppermute x1 -> x2, waiting for transfers between devices: 8.28 us -> 11.2 us  [line_of_four(): a1 = send(x1, perm=inward)]
    ppermute x1, waiting for transfers between devices: 0.01 us -> 2.81 us  [line_of_four(): send(sum2, perm=outward)]
  transfers between devices with their start and end apart: 31 -> 31, of which waited for: 13 -> 15; matrix products, arithmetic and copies ran while one was open for 0% -> 0% of each run, Pallas kernels for 26% -> 26%
where the time goes in v3:
time: 227 us; the launch traced here: 226 us
  waiting for transfers between devices  82.9 us (37%)
  starting transfers between devices  79.3 us (35%)
  Pallas kernels  63.5 us (28%)
    pallas_call x10, Pallas kernels, gains(): pl.pallas_call(kernel, in_specs=[vmem] * len(arrays), out_specs=[vmem] *...  33.9 us
    ppermute x1, waiting for transfers between devices, line_of_four(): field1, x1, y1, low = meet(first1, send(sum1, perm=outward), columns, True)  22.3 us
    ppermute x4, waiting for transfers between devices, line_of_four(): lax.ppermute(value, 'tile', [(i, i ^ bits) for i in range(count)])  16.5 us
    ppermute x1, starting transfers between devices, line_of_four(): d2 = send(after(y2, a2), perm=inward)  13.2 us
    pallas_call x2, Pallas kernels, base(): pl.pallas_call(functools.partial(base_kernel, rows, block, strided), grid...  13 us
    ppermute x4, starting transfers between devices, line_of_four(): lax.ppermute(value, 'tile', [(i, i ^ bits) for i in range(count)])  11.9 us
    ppermute x2, waiting for transfers between devices, line_of_four(): a1 = send(x1, perm=inward)  11.2 us
    ppermute x1, waiting for transfers between devices, line_of_four(): rut1 = send(after(rum1, out1), perm=outward)  10.6 us
  transfers between devices with their start and end apart: 31, of which 15 were waited for; matrix products, arithmetic and copies ran while one was open for 0% of the time, Pallas kernels for 26%

profile of v3, /device:TPU:0, one launch (start us, length us, event | category | flops | bytes accessed | tf_op | source)
XLA Modules:
  0.0 226.3 jit_solution(8195259367873107705)
XLA Ops:
  0.0 2.4 %piece.1 = bf16[128,3072]{1,0:T(8,128)(2,1)} custom-call(f32[1024,4096]{1,0:T(8,128)} %w_ref.2), custom_call_target="tpu_custom_call" | custom-call | flops 1000 | bytes 1000 | tf_op jit(solution)/shard_map/piece/pallas_call | solution.py:153
  2.4 5.0 %collective-permute-start.5 = (bf16[128,3072]{1,0:T(8,128)(2,1)}, bf16[128,3072]{1,0:T(8,128)(2,1)S(1)}, u32[]{:S(2)}, u32[]{:S(2)}) collective-permute-start(bf16[128,3072]{1,0:T(8,128)(2,1)} %piece.1), channel_id=1, source_target_pairs={{0,8},{24,16},{1,9},{25,17},{2,10},{26,18},{3,11},{27,19},{4,12},{... | collective-permute-start | bytes 2359304 | tf_op jit(solution)/shard_map/ppermute | solution.py:358
  7.4 2.4 %pack.1 = (bf16[1024,512]{1,0:T(8,128)(2,1)S(1)}, bf16[1024,512]{1,0:T(8,128)(2,1)S(1)}, f32[1024,256]{1,0:T(8,128)S(1)}, f32[1024,256]{1,0:T(8,128)S(1)}) custom-call(f32[8192,128]{1,0:T(8,128)} %bitcast.3), custom_call_target="tpu_custom_call" | custom-call | flops 1000 | bytes 1000 | tf_op jit(solution)/shard_map/pack/pallas_call | solution.py:52
  13.5 4.1 %collective-permute-start = (bf16[1024,512]{1,0:T(8,128)(2,1)S(1)}, bf16[1024,512]{1,0:T(8,128)(2,1)S(1)}, u32[]{:S(2)}, u32[]{:S(2)}) collective-permute-start(bf16[1024,512]{1,0:T(8,128)(2,1)S(1)} %get-tuple-element.62.refs_0_), channel_id=1, source_target_pairs={{0,8},{24,16},{1,9},{25,17},{2,10},{26,18},{3,11},{27,19},{4,12},{... | collective-permute-start | bytes 3145736 | tf_op jit(solution)/shard_map/ppermute | solution.py:363
  17.6 8.1 %cast.1.w_ref = bf16[1024,4096]{1,0:T(8,128)(2,1)S(1)} custom-call(f32[1024,4096]{1,0:T(8,128)} %w_ref.2), custom_call_target="tpu_custom_call" | custom-call | flops 1000 | bytes 1000 | tf_op jit(solution)/shard_map/cast/pallas_call | solution.py:207
  25.7 5.3 %collective-permute-start.9 = (bf16[128,3072]{1,0:T(8,128)(2,1)S(1)}, bf16[128,3072]{1,0:T(8,128)(2,1)S(1)}, u32[]{:S(2)}, u32[]{:S(2)}) collective-permute-start(bf16[128,3072]{1,0:T(8,128)(2,1)S(1)} %collective-permute-done.5.refs_0_), channel_id=1, source_target_pairs={{0,6},{1,7},{2,4},{3,5},{4,2},{5,3},{6,0},{7,1},{8,14},{9,15},{10,... | collective-permute-start | bytes 2359304 | tf_op jit(solution)/shard_map/ppermute | solution.py:354
  31.8 6.7 %base.2 = (f32[1024,512]{1,0:T(8,128)S(1)}, f32[1024,512]{1,0:T(8,128)S(1)}) custom-call(f32[8192,128]{1,0:T(8,128)S(1)} %bitcast.4, f32[1024,256]{1,0:T(8,128)S(1)} %collective-permute-done.2.refs_1_, f32[1024,256]{1,0:T(8,128)S(1)} %collective-permute-done.3.refs_2_, f32[2,1024]{1,0:T(2,128)S(1)} %copy-done.1, f32[1,1024]{1,0:T(1,128)S(1)} %bitcast.5, ...), custom_call_target="tpu_custom_call" | custom-call | flops 1000 | bytes 1000 | tf_op jit(solution)/shard_map/base/pallas_call | solution.py:128
  38.5 8.3 %collective-permute-done.refs_1_ = bf16[1024,512]{1,0:T(8,128)(2,1)S(1)} collective-permute-done((bf16[1024,512]{1,0:T(8,128)(2,1)S(1)}, bf16[1024,512]{1,0:T(8,128)(2,1)S(1)}, u32[]{:S(2)}, u32[]{:S(2)}) %collective-permute-start) | collective-permute-done | bytes 1048608 | tf_op jit(solution)/shard_map/ppermute | solution.py:363
  48.5 6.3 %collective-permute-start.10 = (bf16[1024,512]{1,0:T(8,128)(2,1)S(1)}, bf16[1024,512]{1,0:T(8,128)(2,1)S(1)}, u32[]{:S(2)}, u32[]{:S(2)}) collective-permute-start(bf16[1024,512]{1,0:T(8,128)(2,1)S(1)} %get-tuple-element.68.refs_0_), channel_id=1, source_target_pairs={{0,8},{24,16},{1,9},{25,17},{2,10},{26,18},{3,11},{27,19},{4,12},{... | collective-permute-start | bytes 3145736 | tf_op jit(solution)/shard_map/ppermute | solution.py:368
  54.7 6.6 %collective-permute-start.7 = (bf16[128,3072]{1,0:T(8,128)(2,1)S(1)}, bf16[128,3072]{1,0:T(8,128)(2,1)S(1)}, u32[]{:S(2)}, u32[]{:S(2)}) collective-permute-start(bf16[128,3072]{1,0:T(8,128)(2,1)S(1)} %collective-permute-done.5.refs_0_), channel_id=1, source_target_pairs={{0,2},{1,3},{2,0},{3,1},{4,6},{5,7},{6,4},{7,5},{8,10},{9,11},{10,... | collective-permute-start | bytes 2359304 | tf_op jit(solution)/shard_map/ppermute | solution.py:354
  61.4 13.6 %collective-permute-done.7.refs_1_ = bf16[128,3072]{1,0:T(8,128)(2,1)S(1)} collective-permute-done((bf16[128,3072]{1,0:T(8,128)(2,1)S(1)}, bf16[128,3072]{1,0:T(8,128)(2,1)S(1)}, u32[]{:S(2)}, u32[]{:S(2)}) %collective-permute-start.7) | collective-permute-done | bytes 786464 | tf_op jit(solution)/shard_map/ppermute | solution.py:354
  78.1 4.5 %own_kernel.4 = (f32[1024,512]{1,0:T(8,128)S(1)}, bf16[1024,512]{1,0:T(8,128)(2,1)S(1)}) custom-call(bf16[1024,4096]{1,0:T(8,128)(2,1)S(1)} %cast.1.w_ref, bf16[1024,512]{1,0:T(8,128)(2,1)S(1)} %get-tuple-element.62.refs_0_, bf16[1024,512]{1,0:T(8,128)(2,1)S(1)} %collective-permute-done.refs_1_, ...), custom_call_target="tpu_custom_call" | custom-call | flops 1000 | bytes 1000 | tf_op jit(solution)/shard_map/own_kernel/pallas_call | solution.py:272
  83.0 3.4 %sum_kernel.6 = bf16[1024,512]{1,0:T(8,128)(2,1)S(1)} custom-call(bf16[512,3072]{1,0:T(8,128)(2,1)S(1)} %stack.1.this_ref, bf16[512,3072]{1,0:T(8,128)(2,1)S(1)} %collective-permute-done.11.other_ref, bf16[1024,512]{1,0:T(8,128)(2,1)S(1)} %get-tuple-element.62.refs_0_, bf16[1024,512]{1,0:T(8,128)(2,1)S(1)} %collective-permute-done.1.refs_2_.refs_1_, ...), custom_call_target="tpu_custom_call" | custom-call | flops 1000 | bytes 1000 | tf_op jit(solution)/shard_map/sum_kernel/pallas_call | solution.py:272
  88.5 3.4 %sum_kernel.7 = bf16[1024,512]{1,0:T(8,128)(2,1)S(1)} custom-call(bf16[512,3072]{1,0:T(8,128)(2,1)S(1)} %stack.1.this_ref, bf16[512,3072]{1,0:T(8,128)(2,1)S(1)} %collective-permute-done.11.other_ref, bf16[1024,512]{1,0:T(8,128)(2,1)S(1)} %get-tuple-element.68.refs_0_, bf16[1024,512]{1,0:T(8,128)(2,1)S(1)} %collective-permute-done.6.refs_1_.refs_2_, ...), custom_call_target="tpu_custom_call" | custom-call | flops 1000 | bytes 1000 | tf_op jit(solution)/shard_map/sum_kernel/pallas_call | solution.py:272
  93.4 4.5 %own_kernel.5 = (f32[1024,512]{1,0:T(8,128)S(1)}, bf16[1024,512]{1,0:T(8,128)(2,1)S(1)}) custom-call(bf16[1024,4096]{1,0:T(8,128)(2,1)S(1)} %cast.1.w_ref, bf16[1024,512]{1,0:T(8,128)(2,1)S(1)} %get-tuple-element.68.refs_0_, bf16[1024,512]{1,0:T(8,128)(2,1)S(1)} %collective-permute-done.10.refs_1_, ...), custom_call_target="tpu_custom_call" | custom-call | flops 1000 | bytes 1000 | tf_op jit(solution)/shard_map/own_kernel/pallas_call | solution.py:272
  98.6 22.3 %collective-permute-done.12.sum_ref = bf16[1024,512]{1,0:T(8,128)(2,1)S(1)} collective-permute-done((bf16[1024,512]{1,0:T(8,128)(2,1)S(1)}, bf16[1024,512]{1,0:T(8,128)(2,1)S(1)}, u32[]{:S(2)}, u32[]{:S(2)}) %collective-permute-start.12) | collective-permute-done | bytes 1048608 | tf_op jit(solution)/shard_map/ppermute | solution.py:380
  121.3 6.1 %collective-permute-start.13 = (bf16[1024,256]{1,0:T(8,128)(2,1)S(1)}, bf16[1024,256]{1,0:T(8,128)(2,1)S(1)}, u32[]{:S(2)}, u32[]{:S(2)}) collective-permute-start(bf16[1024,256]{1,0:T(8,128)(2,1)S(1)} %get-tuple-element.63.refs_0_), channel_id=1, source_target_pairs={{0,8},{24,16},{1,9},{25,17},{2,10},{26,18},{3,11},{27,19},{4,12},{... | collective-permute-start | bytes 1572872 | tf_op jit(solution)/shard_map/ppermute | solution.py:381
  127.4 9.1 %collective-permute-start.15 = (bf16[1024,256]{1,0:T(8,128)(2,1)S(1)}, bf16[1024,256]{1,0:T(8,128)(2,1)S(1)}, u32[]{:S(2)}, u32[]{:S(2)}) collective-permute-start(bf16[1024,256]{1,0:T(8,128)(2,1)S(1)} %get-tuple-element.65.refs_1_.refs_0_), channel_id=1, source_target_pairs={{0,8},{24,16},{1,9},{25,17},{2,10},{26,18},{3,11},{27,19},{4,12},{... | collective-permute-start | bytes 1572872 | tf_op jit(solution)/shard_map/ppermute | solution.py:382
  136.6 3.0 %collective-permute-done.13.refs_2_ = bf16[1024,256]{1,0:T(8,128)(2,1)S(1)} collective-permute-done((bf16[1024,256]{1,0:T(8,128)(2,1)S(1)}, bf16[1024,256]{1,0:T(8,128)(2,1)S(1)}, u32[]{:S(2)}, u32[]{:S(2)}) %collective-permute-start.13) | collective-permute-done | bytes 524320 | tf_op jit(solution)/shard_map/ppermute | solution.py:381
  140.2 2.8 %collective-permute-done.19.sum_ref = bf16[1024,512]{1,0:T(8,128)(2,1)S(1)} collective-permute-done((bf16[1024,512]{1,0:T(8,128)(2,1)S(1)}, bf16[1024,512]{1,0:T(8,128)(2,1)S(1)}, u32[]{:S(2)}, u32[]{:S(2)}) %collective-permute-start.19) | collective-permute-done | bytes 1048608 | tf_op jit(solution)/shard_map/ppermute | solution.py:383
  143.4 2.9 %collective-permute-start.23 = (bf16[1024,256]{1,0:T(8,128)(2,1)S(1)}, bf16[1024,256]{1,0:T(8,128)(2,1)S(1)}, u32[]{:S(2)}, u32[]{:S(2)}) collective-permute-start(bf16[1024,256]{1,0:T(8,128)(2,1)S(1)} %get-tuple-element.81.refs_0_), channel_id=1, source_target_pairs={{0,8},{24,16},{1,9},{25,17},{2,10},{26,18},{3,11},{27,19},{4,12},{... | collective-permute-start | bytes 1572872 | tf_op jit(solution)/shard_map/ppermute | solution.py:384
  146.2 4.5 %collective-permute-done.15.refs_3_ = bf16[1024,256]{1,0:T(8,128)(2,1)S(1)} collective-permute-done((bf16[1024,256]{1,0:T(8,128)(2,1)S(1)}, bf16[1024,256]{1,0:T(8,128)(2,1)S(1)}, u32[]{:S(2)}, u32[]{:S(2)}) %collective-permute-start.15) | collective-permute-done | bytes 524320 | tf_op jit(solution)/shard_map/ppermute | solution.py:382
  155.9 4.3 %collective-permute-done.23.refs_2_ = bf16[1024,256]{1,0:T(8,128)(2,1)S(1)} collective-permute-done((bf16[1024,256]{1,0:T(8,128)(2,1)S(1)}, bf16[1024,256]{1,0:T(8,128)(2,1)S(1)}, u32[]{:S(2)}, u32[]{:S(2)}) %collective-permute-start.23) | collective-permute-done | bytes 524320 | tf_op jit(solution)/shard_map/ppermute | solution.py:384
  160.3 13.2 %collective-permute-start.25 = (bf16[1024,256]{1,0:T(8,128)(2,1)S(1)}, bf16[1024,256]{1,0:T(8,128)(2,1)S(1)}, u32[]{:S(2)}, u32[]{:S(2)}) collective-permute-start(bf16[1024,256]{1,0:T(8,128)(2,1)S(1)} %get-tuple-element.89.refs_1_.refs_0_), channel_id=1, source_target_pairs={{0,8},{24,16},{1,9},{25,17},{2,10},{26,18},{3,11},{27,19},{4,12},{... | collective-permute-start | bytes 1572872 | tf_op jit(solution)/shard_map/ppermute | solution.py:385
  177.3 5.6 %collective-permute-done.27.refs_2_ = bf16[1024,256]{1,0:T(8,128)(2,1)S(1)} collective-permute-done((bf16[1024,256]{1,0:T(8,128)(2,1)S(1)}, bf16[1024,256]{1,0:T(8,128)(2,1)S(1)}, u32[]{:S(2)}, u32[]{:S(2)}) %collective-permute-start.27) | collective-permute-done | bytes 524320 | tf_op jit(solution)/shard_map/ppermute | solution.py:391
  184.9 1.8 sum_kernel.9
  186.7 10.6 %collective-permute-done.28.refs_3_ = bf16[1024,256]{1,0:T(8,128)(2,1)S(1)} collective-permute-done((bf16[1024,256]{1,0:T(8,128)(2,1)S(1)}, bf16[1024,256]{1,0:T(8,128)(2,1)S(1)}, u32[]{:S(2)}, u32[]{:S(2)}) %collective-permute-start.28) | collective-permute-done | bytes 524320 | tf_op jit(solution)/shard_map/ppermute | solution.py:393
  198.6 6.2 %base.3 = (f32[1024,512]{1,0:T(8,128)S(1)}, f32[1024,512]{1,0:T(8,128)S(1)}) custom-call(f32[1024,512]{1,0:T(8,128)S(1)} %get-tuple-element.66.refs_0_, f32[1024,512]{1,0:T(8,128)S(1)} %get-tuple-element.71.refs_1_, f32[1024,256]{1,0:T(8,128)S(1)} %collective-permute-done.21.refs_2_, f32[1024,256]{1,0:T(8,128)S(1)} %collective-permute-done.22.refs_3_, ...), custom_call_target="tpu_custom_call" | custom-call | flops 1000 | bytes 1000 | tf_op jit(solution)/shard_map/base/pallas_call | solution.py:128
  206.7 4.1 %collective-permute-done.29.refs_4_ = bf16[1024,256]{1,0:T(8,128)(2,1)S(1)} collective-permute-done((bf16[1024,256]{1,0:T(8,128)(2,1)S(1)}, bf16[1024,256]{1,0:T(8,128)(2,1)S(1)}, u32[]{:S(2)}, u32[]{:S(2)}) %collective-permute-start.29) | collective-permute-done | bytes 524320 | tf_op jit(solution)/shard_map/ppermute | solution.py:400
  212.3 5.5 %own_kernel.6 = (f32[1024,512]{1,0:T(8,128)S(1)}, bf16[1024,512]{1,0:T(8,128)(2,1)}) custom-call(bf16[1024,4096]{1,0:T(8,128)(2,1)S(1)} %cast.1.w_ref, bf16[1024,256]{1,0:T(8,128)(2,1)S(1)} %get-tuple-element.63.refs_0_, bf16[1024,256]{1,0:T(8,128)(2,1)S(1)} %get-tuple-element.65.refs_1_.refs_0_, bf16[1024,256]{1,0:T(8,128)(2,1)S(1)} %collective-permute-done.13.refs_2_, ...), custom_call_target="tpu_custom_call" | custom-call | flops 1000 | bytes 1000 | tf_op jit(solution)/shard_map/own_kernel/pallas_call | solution.py:272
  217.8 5.5 %own_kernel.7 = (f32[1024,512]{1,0:T(8,128)S(1)}, bf16[1024,512]{1,0:T(8,128)(2,1)}) custom-call(bf16[1024,4096]{1,0:T(8,128)(2,1)S(1)} %cast.1.w_ref, bf16[1024,256]{1,0:T(8,128)(2,1)S(1)} %get-tuple-element.81.refs_0_, bf16[1024,256]{1,0:T(8,128)(2,1)S(1)} %get-tuple-element.89.refs_1_.refs_0_, bf16[1024,256]{1,0:T(8,128)(2,1)S(1)} %collective-permute-done.23.refs_2_, ...), custom_call_target="tpu_custom_call" | custom-call | flops 1000 | bytes 1000 | tf_op jit(solution)/shard_map/own_kernel/pallas_call | solution.py:272
  223.4 2.9 %unpack.1 = f32[8192,128]{1,0:T(8,128)} custom-call(f32[1024,512]{1,0:T(8,128)S(1)} %get-tuple-element.78.refs_0_, f32[1024,512]{1,0:T(8,128)S(1)} %get-tuple-element.86.refs_1_, bf16[1024,256]{1,0:T(8,128)(2,1)S(1)} %collective-permute-done.27.refs_2_, bf16[1024,256]{1,0:T(8,128)(2,1)S(1)} %collective-permute-done.28.refs_3_, ...), custom_call_target="tpu_custom_call" | custom-call | flops 1000 | bytes 1000 | tf_op jit(solution)/shard_map/unpack/pallas_call | solution.py:329
  (57 shorter events, 31.0 us)
Async XLA Ops:
  2.4 23.3 %collective-permute-start.5 = (bf16[128,3072]{1,0:T(8,128)(2,1)}, bf16[128,3072]{1,0:T(8,128)(2,1)S(1)}, u32[]{:S(2)}, u32[]{:S(2)}) collective-permute-start(bf16[128,3072]{1,0:T(8,128)(2,1)} %piece.1), channel_id=1, source_target_pairs={{0,8},{24,16},{1,9},{25,17},{2,10},{26,18},{3,11},{27,19},{4,12},{... | collective-permute-start | bytes 2359304 | tf_op jit(solution)/shard_map/ppermute | solution.py:358
  9.8 21.2 %collective-permute-start.1 = (bf16[1024,512]{1,0:T(8,128)(2,1)S(1)}, bf16[1024,512]{1,0:T(8,128)(2,1)S(1)}, u32[]{:S(2)}, u32[]{:S(2)}) collective-permute-start(bf16[1024,512]{1,0:T(8,128)(2,1)S(1)} %get-tuple-element.62.refs_0_), channel_id=1, source_target_pairs={{8,16},{16,8},{9,17},{17,9},{10,18},{18,10},{11,19},{19,11},{12,20... | collective-permute-start | bytes 3145736 | tf_op jit(solution)/shard_map/ppermute | solution.py:359
  10.5 21.2 %collective-permute-start.2 = (f32[1024,256]{1,0:T(8,128)S(1)}, f32[1024,256]{1,0:T(8,128)S(1)}, u32[]{:S(2)}, u32[]{:S(2)}) collective-permute-start(f32[1024,256]{1,0:T(8,128)S(1)} %get-tuple-element.50), channel_id=1, source_target_pairs={{0,1},{1,2},{2,3},{3,4},{4,5},{5,6},{6,7},{8,9},{9,10},{10,11},{11... | collective-permute-start | bytes 3145736 | tf_op jit(solution)/shard_map/ppermute | solution.py:361
  12.1 19.6 %copy-start.1 = (f32[2,1024]{1,0:T(2,128)S(1)}, f32[2,1024]{1,0:T(2,128)}, u32[]{:S(2)}) copy-start(f32[2,1024]{1,0:T(2,128)} %refs_4_.1) | copy-start | bytes 24580
  12.1 19.6 %collective-permute-start.3 = (f32[1024,256]{1,0:T(8,128)S(1)}, f32[1024,256]{1,0:T(8,128)S(1)}, u32[]{:S(2)}, u32[]{:S(2)}) collective-permute-start(f32[1024,256]{1,0:T(8,128)S(1)} %get-tuple-element.51), channel_id=1, source_target_pairs={{1,0},{2,1},{3,2},{4,3},{5,4},{6,5},{7,6},{9,8},{10,9},{11,10},{12... | collective-permute-start | bytes 3145736 | tf_op jit(solution)/shard_map/ppermute | solution.py:362
  13.5 33.2 %collective-permute-start = (bf16[1024,512]{1,0:T(8,128)(2,1)S(1)}, bf16[1024,512]{1,0:T(8,128)(2,1)S(1)}, u32[]{:S(2)}, u32[]{:S(2)}) collective-permute-start(bf16[1024,512]{1,0:T(8,128)(2,1)S(1)} %get-tuple-element.62.refs_0_), channel_id=1, source_target_pairs={{0,8},{24,16},{1,9},{25,17},{2,10},{26,18},{3,11},{27,19},{4,12},{... | collective-permute-start | bytes 3145736 | tf_op jit(solution)/shard_map/ppermute | solution.py:363
  25.7 22.7 %collective-permute-start.9 = (bf16[128,3072]{1,0:T(8,128)(2,1)S(1)}, bf16[128,3072]{1,0:T(8,128)(2,1)S(1)}, u32[]{:S(2)}, u32[]{:S(2)}) collective-permute-start(bf16[128,3072]{1,0:T(8,128)(2,1)S(1)} %collective-permute-done.5.refs_0_), channel_id=1, source_target_pairs={{0,6},{1,7},{2,4},{3,5},{4,2},{5,3},{6,0},{7,1},{8,14},{9,15},{10,... | collective-permute-start | bytes 2359304 | tf_op jit(solution)/shard_map/ppermute | solution.py:354
  31.0 30.4 %collective-permute-start.6 = (bf16[1024,512]{1,0:T(8,128)(2,1)S(1)}, bf16[1024,512]{1,0:T(8,128)(2,1)S(1)}, u32[]{:S(2)}, u32[]{:S(2)}) collective-permute-start(bf16[1024,512]{1,0:T(8,128)(2,1)S(1)} %get-tuple-element.68.refs_0_), channel_id=1, source_target_pairs={{8,16},{16,8},{9,17},{17,9},{10,18},{18,10},{11,19},{19,11},{12,20... | collective-permute-start | bytes 3145736 | tf_op jit(solution)/shard_map/ppermute | solution.py:360
  46.8 29.9 %collective-permute-start.4 = (bf16[1024,512]{1,0:T(8,128)(2,1)S(1)}, bf16[1024,512]{1,0:T(8,128)(2,1)S(1)}, u32[]{:S(2)}, u32[]{:S(2)}) collective-permute-start(bf16[1024,512]{1,0:T(8,128)(2,1)S(1)} %collective-permute-done.refs_1_), channel_id=1, source_target_pairs={{8,16},{16,8},{9,17},{17,9},{10,18},{18,10},{11,19},{19,11},{12,20... | collective-permute-start | bytes 3145736 | tf_op jit(solution)/shard_map/ppermute | solution.py:369
  48.5 28.9 %collective-permute-start.10 = (bf16[1024,512]{1,0:T(8,128)(2,1)S(1)}, bf16[1024,512]{1,0:T(8,128)(2,1)S(1)}, u32[]{:S(2)}, u32[]{:S(2)}) collective-permute-start(bf16[1024,512]{1,0:T(8,128)(2,1)S(1)} %get-tuple-element.68.refs_0_), channel_id=1, source_target_pairs={{0,8},{24,16},{1,9},{25,17},{2,10},{26,18},{3,11},{27,19},{4,12},{... | collective-permute-start | bytes 3145736 | tf_op jit(solution)/shard_map/ppermute | solution.py:368
  54.7 20.3 %collective-permute-start.7 = (bf16[128,3072]{1,0:T(8,128)(2,1)S(1)}, bf16[128,3072]{1,0:T(8,128)(2,1)S(1)}, u32[]{:S(2)}, u32[]{:S(2)}) collective-permute-start(bf16[128,3072]{1,0:T(8,128)(2,1)S(1)} %collective-permute-done.5.refs_0_), channel_id=1, source_target_pairs={{0,2},{1,3},{2,0},{3,1},{4,6},{5,7},{6,4},{7,5},{8,10},{9,11},{10,... | collective-permute-start | bytes 2359304 | tf_op jit(solution)/shard_map/ppermute | solution.py:354
  61.3 15.1 %collective-permute-start.8 = (bf16[128,3072]{1,0:T(8,128)(2,1)S(1)}, bf16[128,3072]{1,0:T(8,128)(2,1)S(1)}, u32[]{:S(2)}, u32[]{:S(2)}) collective-permute-start(bf16[128,3072]{1,0:T(8,128)(2,1)S(1)} %collective-permute-done.5.refs_0_), channel_id=1, source_target_pairs={{0,4},{1,5},{2,6},{3,7},{4,0},{5,1},{6,2},{7,3},{8,12},{9,13},{10,... | collective-permute-start | bytes 2359304 | tf_op jit(solution)/shard_map/ppermute | solution.py:354
  77.4 5.7 %collective-permute-start.11 = (bf16[512,3072]{1,0:T(8,128)(2,1)S(1)}, bf16[512,3072]{1,0:T(8,128)(2,1)S(1)}, u32[]{:S(2)}, u32[]{:S(2)}) collective-permute-start(bf16[512,3072]{1,0:T(8,128)(2,1)S(1)} %stack.1.this_ref), channel_id=1, source_target_pairs={{0,1},{1,0},{2,3},{3,2},{4,5},{5,4},{6,7},{7,6},{8,9},{9,8},{10,11... | collective-permute-start | bytes 9437192 | tf_op jit(solution)/shard_map/ppermute | solution.py:354
  77.4 11.1 %collective-permute-start.18 = (bf16[1024,512]{1,0:T(8,128)(2,1)S(1)}, bf16[1024,512]{1,0:T(8,128)(2,1)S(1)}, u32[]{:S(2)}, u32[]{:S(2)}) collective-permute-start(bf16[1024,512]{1,0:T(8,128)(2,1)S(1)} %collective-permute-done.10.refs_1_), channel_id=1, source_target_pairs={{8,16},{16,8},{9,17},{17,9},{10,18},{18,10},{11,19},{19,11},{12,20... | collective-permute-start | bytes 3145736 | tf_op jit(solution)/shard_map/ppermute | solution.py:371
  86.5 34.5 %collective-permute-start.12 = (bf16[1024,512]{1,0:T(8,128)(2,1)S(1)}, bf16[1024,512]{1,0:T(8,128)(2,1)S(1)}, u32[]{:S(2)}, u32[]{:S(2)}) collective-permute-start(bf16[1024,512]{1,0:T(8,128)(2,1)S(1)} %sum_kernel.6), channel_id=1, source_target_pairs={{8,0},{16,24},{9,1},{17,25},{10,2},{18,26},{11,3},{19,27},{12,4},{... | collective-permute-start | bytes 3145736 | tf_op jit(solution)/shard_map/ppermute | solution.py:380
  87.8 39.7 %collective-permute-start.14 = (bf16[1024,512]{1,0:T(8,128)(2,1)S(1)}, bf16[1024,512]{1,0:T(8,128)(2,1)S(1)}, u32[]{:S(2)}, u32[]{:S(2)}) collective-permute-start(bf16[1024,512]{1,0:T(8,128)(2,1)S(1)} %get-tuple-element.61), channel_id=1, source_target_pairs={{8,16},{16,8},{9,17},{17,9},{10,18},{18,10},{11,19},{19,11},{12,20... | collective-permute-start | bytes 3145736 | tf_op jit(solution)/shard_map/ppermute | solution.py:378
  91.9 51.1 %collective-permute-start.19 = (bf16[1024,512]{1,0:T(8,128)(2,1)S(1)}, bf16[1024,512]{1,0:T(8,128)(2,1)S(1)}, u32[]{:S(2)}, u32[]{:S(2)}) collective-permute-start(bf16[1024,512]{1,0:T(8,128)(2,1)S(1)} %sum_kernel.7), channel_id=1, source_target_pairs={{8,0},{16,24},{9,1},{17,25},{10,2},{18,26},{11,3},{19,27},{12,4},{... | collective-permute-start | bytes 3145736 | tf_op jit(solution)/shard_map/ppermute | solution.py:383
  97.9 48.4 %collective-permute-start.20 = (bf16[1024,512]{1,0:T(8,128)(2,1)S(1)}, bf16[1024,512]{1,0:T(8,128)(2,1)S(1)}, u32[]{:S(2)}, u32[]{:S(2)}) collective-permute-start(bf16[1024,512]{1,0:T(8,128)(2,1)S(1)} %get-tuple-element.73), channel_id=1, source_target_pairs={{8,16},{16,8},{9,17},{17,9},{10,18},{18,10},{11,19},{19,11},{12,20... | collective-permute-start | bytes 3145736 | tf_op jit(solution)/shard_map/ppermute | solution.py:379
  121.3 18.2 %collective-permute-start.13 = (bf16[1024,256]{1,0:T(8,128)(2,1)S(1)}, bf16[1024,256]{1,0:T(8,128)(2,1)S(1)}, u32[]{:S(2)}, u32[]{:S(2)}) collective-permute-start(bf16[1024,256]{1,0:T(8,128)(2,1)S(1)} %get-tuple-element.63.refs_0_), channel_id=1, source_target_pairs={{0,8},{24,16},{1,9},{25,17},{2,10},{26,18},{3,11},{27,19},{4,12},{... | collective-permute-start | bytes 1572872 | tf_op jit(solution)/shard_map/ppermute | solution.py:381
  127.4 23.3 %collective-permute-start.15 = (bf16[1024,256]{1,0:T(8,128)(2,1)S(1)}, bf16[1024,256]{1,0:T(8,128)(2,1)S(1)}, u32[]{:S(2)}, u32[]{:S(2)}) collective-permute-start(bf16[1024,256]{1,0:T(8,128)(2,1)S(1)} %get-tuple-element.65.refs_1_.refs_0_), channel_id=1, source_target_pairs={{0,8},{24,16},{1,9},{25,17},{2,10},{26,18},{3,11},{27,19},{4,12},{... | collective-permute-start | bytes 1572872 | tf_op jit(solution)/shard_map/ppermute | solution.py:382
  139.5 13.3 %collective-permute-start.16 = (bf16[1024,256]{1,0:T(8,128)(2,1)S(1)}, bf16[1024,256]{1,0:T(8,128)(2,1)S(1)}, u32[]{:S(2)}, u32[]{:S(2)}) collective-permute-start(bf16[1024,256]{1,0:T(8,128)(2,1)S(1)} %collective-permute-done.13.refs_2_), channel_id=1, source_target_pairs={{8,16},{16,8},{9,17},{17,9},{10,18},{18,10},{11,19},{19,11},{12,20... | collective-permute-start | bytes 1572872 | tf_op jit(solution)/shard_map/ppermute | solution.py:386
  143.4 16.9 %collective-permute-start.23 = (bf16[1024,256]{1,0:T(8,128)(2,1)S(1)}, bf16[1024,256]{1,0:T(8,128)(2,1)S(1)}, u32[]{:S(2)}, u32[]{:S(2)}) collective-permute-start(bf16[1024,256]{1,0:T(8,128)(2,1)S(1)} %get-tuple-element.81.refs_0_), channel_id=1, source_target_pairs={{0,8},{24,16},{1,9},{25,17},{2,10},{26,18},{3,11},{27,19},{4,12},{... | collective-permute-start | bytes 1572872 | tf_op jit(solution)/shard_map/ppermute | solution.py:384
  150.8 23.4 %collective-permute-start.17 = (bf16[1024,256]{1,0:T(8,128)(2,1)S(1)}, bf16[1024,256]{1,0:T(8,128)(2,1)S(1)}, u32[]{:S(2)}, u32[]{:S(2)}) collective-permute-start(bf16[1024,256]{1,0:T(8,128)(2,1)S(1)} %collective-permute-done.15.refs_3_), channel_id=1, source_target_pairs={{8,16},{16,8},{9,17},{17,9},{10,18},{18,10},{11,19},{19,11},{12,20... | collective-permute-start | bytes 1572872 | tf_op jit(solution)/shard_map/ppermute | solution.py:387
  151.4 33.4 %collective-permute-start.21 = (f32[1024,256]{1,0:T(8,128)S(1)}, f32[1024,256]{1,0:T(8,128)S(1)}, u32[]{:S(2)}, u32[]{:S(2)}) collective-permute-start(f32[1024,256]{1,0:T(8,128)S(1)} %get-tuple-element.74), channel_id=1, source_target_pairs={{0,1},{1,2},{2,3},{3,4},{4,5},{5,6},{6,7},{8,9},{9,10},{10,11},{11... | collective-permute-start | bytes 3145736 | tf_op jit(solution)/shard_map/ppermute | solution.py:394
  154.6 28.2 %collective-permute-start.27 = (bf16[1024,256]{1,0:T(8,128)(2,1)S(1)}, bf16[1024,256]{1,0:T(8,128)(2,1)S(1)}, u32[]{:S(2)}, u32[]{:S(2)}) collective-permute-start(bf16[1024,256]{1,0:T(8,128)(2,1)S(1)} %sum_kernel.10), channel_id=1, source_target_pairs={{8,0},{16,24},{9,1},{17,25},{10,2},{18,26},{11,3},{19,27},{12,4},{... | collective-permute-start | bytes 1572872 | tf_op jit(solution)/shard_map/ppermute | solution.py:391
  160.3 23.9 %collective-permute-start.25 = (bf16[1024,256]{1,0:T(8,128)(2,1)S(1)}, bf16[1024,256]{1,0:T(8,128)(2,1)S(1)}, u32[]{:S(2)}, u32[]{:S(2)}) collective-permute-start(bf16[1024,256]{1,0:T(8,128)(2,1)S(1)} %get-tuple-element.89.refs_1_.refs_0_), channel_id=1, source_target_pairs={{0,8},{24,16},{1,9},{25,17},{2,10},{26,18},{3,11},{27,19},{4,12},{... | collective-permute-start | bytes 1572872 | tf_op jit(solution)/shard_map/ppermute | solution.py:385
  173.4 10.7 %collective-permute-start.24 = (bf16[1024,256]{1,0:T(8,128)(2,1)S(1)}, bf16[1024,256]{1,0:T(8,128)(2,1)S(1)}, u32[]{:S(2)}, u32[]{:S(2)}) collective-permute-start(bf16[1024,256]{1,0:T(8,128)(2,1)S(1)} %collective-permute-done.23.refs_2_), channel_id=1, source_target_pairs={{8,16},{16,8},{9,17},{17,9},{10,18},{18,10},{11,19},{19,11},{12,20... | collective-permute-start | bytes 1572872 | tf_op jit(solution)/shard_map/ppermute | solution.py:397
  174.1 24.4 %collective-permute-start.22 = (f32[1024,256]{1,0:T(8,128)S(1)}, f32[1024,256]{1,0:T(8,128)S(1)}, u32[]{:S(2)}, u32[]{:S(2)}) collective-permute-start(f32[1024,256]{1,0:T(8,128)S(1)} %get-tuple-element.76), channel_id=1, source_target_pairs={{1,0},{2,1},{3,2},{4,3},{5,4},{6,5},{7,6},{9,8},{10,9},{11,10},{12... | collective-permute-start | bytes 3145736 | tf_op jit(solution)/shard_map/ppermute | solution.py:395
  182.9 14.4 %collective-permute-start.28 = (bf16[1024,256]{1,0:T(8,128)(2,1)S(1)}, bf16[1024,256]{1,0:T(8,128)(2,1)S(1)}, u32[]{:S(2)}, u32[]{:S(2)}) collective-permute-start(bf16[1024,256]{1,0:T(8,128)(2,1)S(1)} %sum_kernel.8), channel_id=1, source_target_pairs={{8,0},{16,24},{9,1},{17,25},{10,2},{18,26},{11,3},{19,27},{12,4},{... | collective-permute-start | bytes 1572872 | tf_op jit(solution)/shard_map/ppermute | solution.py:393
  184.2 20.7 %collective-permute-start.26 = (bf16[1024,256]{1,0:T(8,128)(2,1)S(1)}, bf16[1024,256]{1,0:T(8,128)(2,1)S(1)}, u32[]{:S(2)}, u32[]{:S(2)}) collective-permute-start(bf16[1024,256]{1,0:T(8,128)(2,1)S(1)} %collective-permute-done.25.refs_3_), channel_id=1, source_target_pairs={{8,16},{16,8},{9,17},{17,9},{10,18},{18,10},{11,19},{19,11},{12,20... | collective-permute-start | bytes 1572872 | tf_op jit(solution)/shard_map/ppermute | solution.py:398
  197.3 13.5 %collective-permute-start.29 = (bf16[1024,256]{1,0:T(8,128)(2,1)S(1)}, bf16[1024,256]{1,0:T(8,128)(2,1)S(1)}, u32[]{:S(2)}, u32[]{:S(2)}) collective-permute-start(bf16[1024,256]{1,0:T(8,128)(2,1)S(1)} %sum_kernel.9), channel_id=1, source_target_pairs={{8,0},{16,24},{9,1},{17,25},{10,2},{18,26},{11,3},{19,27},{12,4},{... | collective-permute-start | bytes 1572872 | tf_op jit(solution)/shard_map/ppermute | solution.py:400
  210.8 12.6 %collective-permute-start.30 = (bf16[1024,256]{1,0:T(8,128)(2,1)S(1)}, bf16[1024,256]{1,0:T(8,128)(2,1)S(1)}, u32[]{:S(2)}, u32[]{:S(2)}) collective-permute-start(bf16[1024,256]{1,0:T(8,128)(2,1)S(1)} %sum_kernel.11), channel_id=1, source_target_pairs={{8,0},{16,24},{9,1},{17,25},{10,2},{18,26},{11,3},{19,27},{12,4},{... | collective-permute-start | bytes 1572872 | tf_op jit(solution)/shard_map/ppermute | solution.py:403
  (3 other events, 53.4 us)

commit v4 on v3

--- a/solution.py
+++ b/solution.py
@@ -248,6 +248,17 @@
         rounded_ref[span, :] = line.astype(bf16)
 
 
+def early_kernel(counts, w_ref, *refs):
+    *part_refs, out_ref = refs
+    out_ref[...] = time_step * product(w_ref, slice(None), parts_of(counts, part_refs), True)
+
+
+def late_kernel(counts, w_ref, *refs):
+    *part_refs, base_ref, early_ref, out_ref = refs
+    total = product(w_ref, slice(None), parts_of(counts, part_refs), True)
+    out_ref[...] = base_ref[...] + early_ref[...] + time_step * total
+
+
 def sum_kernel(counts, cut, this_ref, other_ref, *refs):
     *part_refs, sum_ref = refs
     parts = parts_of(counts, part_refs)
@@ -285,6 +296,16 @@
     return gains(kernel, (weights, *x, *a, *b, *c, based), based.shape, (f32, bf16))
 
 
+def early_rows(weights, x, b):
+    kernel = functools.partial(early_kernel, {0: len(x), 2: 1})
+    return gains(kernel, (weights, *x, b), b.shape, (f32,))[0]
+
+
+def late_rows(weights, a, c, based, early):
+    kernel = functools.partial(late_kernel, {1: len(a), 3: len(c)})
+    return gains(kernel, (weights, *a, *c, based, early), based.shape, (f32,))[0]
+
+
 def end_sum(weights, x, b, c, cut=None):
     kernel = functools.partial(sum_kernel, {0: 1, 2: 1, 3: 1}, cut)
     return gains(kernel, (*weights, x, b, c), x.shape, (bf16,))[0]
@@ -324,7 +345,7 @@
 def unpack(firsts, sums, rows):
     modes, cells = firsts[0].shape
     columns = 2 * cells // rows
-    block = 256
+    block = 128
     spec = lambda count: pl.BlockSpec((block, count), lambda i: (i, 0))
     flat = pl.pallas_call(
         functools.partial(unpack_kernel, rows, block),
@@ -380,10 +401,12 @@
     field1, x1, y1, low = meet(first1, send(sum1, perm=outward), columns, True)
     a1 = send(x1, perm=inward)
     d1 = send(after(y1, b1), perm=inward)
+    early1 = early_rows(own_w, [x1, y1], b1)
     field2, x2, y2, high = meet(first2, send(sum2, perm=outward), columns, False)
     a2 = send(x2, perm=inward)
     d2 = send(after(y2, a2), perm=inward)
-    c1 = send(a1, perm=across)
+    early2 = early_rows(own_w, [x2, y2], b2)
+    c1 = send(after(a1, early1), perm=across)
     e1 = send(d1, perm=across)
     half = b1.shape[1] // 2
     left, right = slice(0, half), slice(half, 2 * half)
@@ -396,12 +419,12 @@
     base1, base2 = local([field1, field2], before, behind)
     c2 = send(a2, perm=across)
     e2 = send(after(d2, c2), perm=across)
-    sum2 = end_sum(edge_w, after(x2, rum1, before), b2, c2, left)
+    sum2 = end_sum(edge_w, after(x2, rum1, before, early2), b2, c2, left)
     out2 = send(after(sum2, rut1, out1), perm=outward)
     rum2 = end_sum(edge_w, after(y2, sum2, base1), b2, e2, right)
-    first1, _ = own_rows(own_w, [x1, y1], [a1, d1], [b1], [c1, e1], base1)
+    first1 = late_rows(own_w, [a1, d1], [c1, e1], base1, early1)
     rut2 = send(after(rum2, out2), perm=outward)
-    first2, _ = own_rows(own_w, [after(x2, sum2), y2], [a2, d2], [b2], [c2, e2], base2)
+    first2 = late_rows(own_w, [after(a2, sum2), d2], [c2, e2], base2, early2)
     return unpack([first1, first2], [out1, rut1, out2, rut2], rows)
 
 

time: 227 us -> 228 us (level)
    ppermute x1, waiting for transfers between devices: 0.16 us -> 6.64 us  [line_of_four(): rut2 = send(after(rum2, out2), perm=outward)]
    ppermute x1, waiting for transfers between devices: 10.6 us -> 8.27 us  [line_of_four(): rut1 = send(after(rum1, out1), perm=outward)]
    ppermute x2, waiting for transfers between devices: 11.2 us -> 8.9 us  [line_of_four(): a1 = send(x1, perm=inward)]
    pallas_call x10 -> x12, Pallas kernels: 33.9 us -> 32.3 us  [gains(): pl.pallas_call(kernel, in_specs=[vmem] * len(arrays), out_specs=[vmem] *...]
  transfers between devices with their start and end apart: 31 -> 31, of which waited for: 15 -> 14; matrix products, arithmetic and copies ran while one was open for 0% -> 0% of each run, Pallas kernels for 26% -> 25%
where the time goes in v4:
time: 228 us; the launch traced here: 227 us
  waiting for transfers between devices  84.4 us (37%)
  starting transfers between devices  79.4 us (35%)
  Pallas kernels  62.9 us (28%)
    pallas_call x12, Pallas kernels, gains(): pl.pallas_call(kernel, in_specs=[vmem] * len(arrays), out_specs=[vmem] *...  32.3 us
    ppermute x1, waiting for transfers between devices, line_of_four(): field1, x1, y1, low = meet(first1, send(sum1, perm=outward), columns, True)  22.1 us
    ppermute x4, waiting for transfers between devices, line_of_four(): lax.ppermute(value, 'tile', [(i, i ^ bits) for i in range(count)])  17.3 us
    ppermute x1, starting transfers between devices, line_of_four(): d2 = send(after(y2, a2), perm=inward)  13.2 us
    pallas_call x2, Pallas kernels, base(): pl.pallas_call(functools.partial(base_kernel, rows, block, strided), grid...  13 us
    ppermute x4, starting transfers between devices, line_of_four(): lax.ppermute(value, 'tile', [(i, i ^ bits) for i in range(count)])  12 us
    ppermute x2, starting transfers between devices, line_of_four(): a1 = send(x1, perm=inward)  10.2 us
    ppermute x1, starting transfers between devices, line_of_four(): d1 = send(after(y1, b1), perm=inward)  9.13 us
  transfers between devices with their start and end apart: 31, of which 14 were waited for; matrix products, arithmetic and copies ran while one was open for 0% of the time, Pallas kernels for 25%

profile of v4, /device:TPU:0, one launch (start us, length us, event | category | flops | bytes accessed | tf_op | source)
XLA Modules:
  0.0 227.3 jit_solution(3257297843036230599)
XLA Ops:
  0.0 2.4 %piece.1 = bf16[128,3072]{1,0:T(8,128)(2,1)} custom-call(f32[1024,4096]{1,0:T(8,128)} %w_ref.2), custom_call_target="tpu_custom_call" | custom-call | flops 1000 | bytes 1000 | tf_op jit(solution)/shard_map/piece/pallas_call | solution.py:153
  2.4 5.0 %collective-permute-start.5 = (bf16[128,3072]{1,0:T(8,128)(2,1)}, bf16[128,3072]{1,0:T(8,128)(2,1)S(1)}, u32[]{:S(2)}, u32[]{:S(2)}) collective-permute-start(bf16[128,3072]{1,0:T(8,128)(2,1)} %piece.1), channel_id=1, source_target_pairs={{0,8},{24,16},{1,9},{25,17},{2,10},{26,18},{3,11},{27,19},{4,12},{... | collective-permute-start | bytes 2359304 | tf_op jit(solution)/shard_map/ppermute | solution.py:379
  7.4 2.4 %pack.1 = (bf16[1024,512]{1,0:T(8,128)(2,1)S(1)}, bf16[1024,512]{1,0:T(8,128)(2,1)S(1)}, f32[1024,256]{1,0:T(8,128)S(1)}, f32[1024,256]{1,0:T(8,128)S(1)}) custom-call(f32[8192,128]{1,0:T(8,128)} %bitcast.3), custom_call_target="tpu_custom_call" | custom-call | flops 1000 | bytes 1000 | tf_op jit(solution)/shard_map/pack/pallas_call | solution.py:52
  13.5 4.1 %collective-permute-start = (bf16[1024,512]{1,0:T(8,128)(2,1)S(1)}, bf16[1024,512]{1,0:T(8,128)(2,1)S(1)}, u32[]{:S(2)}, u32[]{:S(2)}) collective-permute-start(bf16[1024,512]{1,0:T(8,128)(2,1)S(1)} %get-tuple-element.61.refs_0_), channel_id=1, source_target_pairs={{0,8},{24,16},{1,9},{25,17},{2,10},{26,18},{3,11},{27,19},{4,12},{... | collective-permute-start | bytes 3145736 | tf_op jit(solution)/shard_map/ppermute | solution.py:384
  17.6 8.1 %cast.1.w_ref = bf16[1024,4096]{1,0:T(8,128)(2,1)S(1)} custom-call(f32[1024,4096]{1,0:T(8,128)} %w_ref.2), custom_call_target="tpu_custom_call" | custom-call | flops 1000 | bytes 1000 | tf_op jit(solution)/shard_map/cast/pallas_call | solution.py:207
  25.7 5.3 %collective-permute-start.9 = (bf16[128,3072]{1,0:T(8,128)(2,1)S(1)}, bf16[128,3072]{1,0:T(8,128)(2,1)S(1)}, u32[]{:S(2)}, u32[]{:S(2)}) collective-permute-start(bf16[128,3072]{1,0:T(8,128)(2,1)S(1)} %collective-permute-done.5.refs_0_), channel_id=1, source_target_pairs={{0,6},{1,7},{2,4},{3,5},{4,2},{5,3},{6,0},{7,1},{8,14},{9,15},{10,... | collective-permute-start | bytes 2359304 | tf_op jit(solution)/shard_map/ppermute | solution.py:375
  31.8 6.7 %base.2 = (f32[1024,512]{1,0:T(8,128)S(1)}, f32[1024,512]{1,0:T(8,128)S(1)}) custom-call(f32[8192,128]{1,0:T(8,128)S(1)} %bitcast.4, f32[1024,256]{1,0:T(8,128)S(1)} %collective-permute-done.2.refs_1_, f32[1024,256]{1,0:T(8,128)S(1)} %collective-permute-done.3.refs_2_, f32[2,1024]{1,0:T(2,128)S(1)} %copy-done.1, f32[1,1024]{1,0:T(1,128)S(1)} %bitcast.5, ...), custom_call_target="tpu_custom_call" | custom-call | flops 1000 | bytes 1000 | tf_op jit(solution)/shard_map/base/pallas_call | solution.py:128
  38.5 8.3 %collective-permute-done.refs_1_ = bf16[1024,512]{1,0:T(8,128)(2,1)S(1)} collective-permute-done((bf16[1024,512]{1,0:T(8,128)(2,1)S(1)}, bf16[1024,512]{1,0:T(8,128)(2,1)S(1)}, u32[]{:S(2)}, u32[]{:S(2)}) %collective-permute-start) | collective-permute-done | bytes 1048608 | tf_op jit(solution)/shard_map/ppermute | solution.py:384
  48.5 6.3 %collective-permute-start.10 = (bf16[1024,512]{1,0:T(8,128)(2,1)S(1)}, bf16[1024,512]{1,0:T(8,128)(2,1)S(1)}, u32[]{:S(2)}, u32[]{:S(2)}) collective-permute-start(bf16[1024,512]{1,0:T(8,128)(2,1)S(1)} %get-tuple-element.68.refs_0_), channel_id=1, source_target_pairs={{0,8},{24,16},{1,9},{25,17},{2,10},{26,18},{3,11},{27,19},{4,12},{... | collective-permute-start | bytes 3145736 | tf_op jit(solution)/shard_map/ppermute | solution.py:389
  54.7 6.6 %collective-permute-start.8 = (bf16[128,3072]{1,0:T(8,128)(2,1)S(1)}, bf16[128,3072]{1,0:T(8,128)(2,1)S(1)}, u32[]{:S(2)}, u32[]{:S(2)}) collective-permute-start(bf16[128,3072]{1,0:T(8,128)(2,1)S(1)} %collective-permute-done.5.refs_0_), channel_id=1, source_target_pairs={{0,4},{1,5},{2,6},{3,7},{4,0},{5,1},{6,2},{7,3},{8,12},{9,13},{10,... | collective-permute-start | bytes 2359304 | tf_op jit(solution)/shard_map/ppermute | solution.py:375
  61.4 14.4 %collective-permute-done.8.refs_2_ = bf16[128,3072]{1,0:T(8,128)(2,1)S(1)} collective-permute-done((bf16[128,3072]{1,0:T(8,128)(2,1)S(1)}, bf16[128,3072]{1,0:T(8,128)(2,1)S(1)}, u32[]{:S(2)}, u32[]{:S(2)}) %collective-permute-start.8) | collective-permute-done | bytes 786464 | tf_op jit(solution)/shard_map/ppermute | solution.py:375
  78.4 4.5 %own_kernel.2 = (f32[1024,512]{1,0:T(8,128)S(1)}, bf16[1024,512]{1,0:T(8,128)(2,1)S(1)}) custom-call(bf16[1024,4096]{1,0:T(8,128)(2,1)S(1)} %cast.1.w_ref, bf16[1024,512]{1,0:T(8,128)(2,1)S(1)} %get-tuple-element.61.refs_0_, bf16[1024,512]{1,0:T(8,128)(2,1)S(1)} %collective-permute-done.refs_1_, ...), custom_call_target="tpu_custom_call" | custom-call | flops 1000 | bytes 1000 | tf_op jit(solution)/shard_map/own_kernel/pallas_call | solution.py:283
  83.3 3.4 %sum_kernel.6 = bf16[1024,512]{1,0:T(8,128)(2,1)S(1)} custom-call(bf16[512,3072]{1,0:T(8,128)(2,1)S(1)} %stack.1.this_ref, bf16[512,3072]{1,0:T(8,128)(2,1)S(1)} %collective-permute-done.11.other_ref, bf16[1024,512]{1,0:T(8,128)(2,1)S(1)} %get-tuple-element.61.refs_0_, bf16[1024,512]{1,0:T(8,128)(2,1)S(1)} %collective-permute-done.1.refs_2_.refs_1_, ...), custom_call_target="tpu_custom_call" | custom-call | flops 1000 | bytes 1000 | tf_op jit(solution)/shard_map/sum_kernel/pallas_call | solution.py:283
  88.7 3.4 %sum_kernel.7 = bf16[1024,512]{1,0:T(8,128)(2,1)S(1)} custom-call(bf16[512,3072]{1,0:T(8,128)(2,1)S(1)} %stack.1.this_ref, bf16[512,3072]{1,0:T(8,128)(2,1)S(1)} %collective-permute-done.11.other_ref, bf16[1024,512]{1,0:T(8,128)(2,1)S(1)} %get-tuple-element.68.refs_0_, bf16[1024,512]{1,0:T(8,128)(2,1)S(1)} %collective-permute-done.6.refs_1_.refs_2_, ...), custom_call_target="tpu_custom_call" | custom-call | flops 1000 | bytes 1000 | tf_op jit(solution)/shard_map/sum_kernel/pallas_call | solution.py:283
  93.6 4.5 %own_kernel.3 = (f32[1024,512]{1,0:T(8,128)S(1)}, bf16[1024,512]{1,0:T(8,128)(2,1)S(1)}) custom-call(bf16[1024,4096]{1,0:T(8,128)(2,1)S(1)} %cast.1.w_ref, bf16[1024,512]{1,0:T(8,128)(2,1)S(1)} %get-tuple-element.68.refs_0_, bf16[1024,512]{1,0:T(8,128)(2,1)S(1)} %collective-permute-done.10.refs_1_, ...), custom_call_target="tpu_custom_call" | custom-call | flops 1000 | bytes 1000 | tf_op jit(solution)/shard_map/own_kernel/pallas_call | solution.py:283
  98.8 22.1 %collective-permute-done.12.sum_ref = bf16[1024,512]{1,0:T(8,128)(2,1)S(1)} collective-permute-done((bf16[1024,512]{1,0:T(8,128)(2,1)S(1)}, bf16[1024,512]{1,0:T(8,128)(2,1)S(1)}, u32[]{:S(2)}, u32[]{:S(2)}) %collective-permute-start.12) | collective-permute-done | bytes 1048608 | tf_op jit(solution)/shard_map/ppermute | solution.py:401
  121.3 6.1 %collective-permute-start.13 = (bf16[1024,256]{1,0:T(8,128)(2,1)S(1)}, bf16[1024,256]{1,0:T(8,128)(2,1)S(1)}, u32[]{:S(2)}, u32[]{:S(2)}) collective-permute-start(bf16[1024,256]{1,0:T(8,128)(2,1)S(1)} %get-tuple-element.62.refs_0_), channel_id=1, source_target_pairs={{0,8},{24,16},{1,9},{25,17},{2,10},{26,18},{3,11},{27,19},{4,12},{... | collective-permute-start | bytes 1572872 | tf_op jit(solution)/shard_map/ppermute | solution.py:402
  127.4 9.1 %collective-permute-start.15 = (bf16[1024,256]{1,0:T(8,128)(2,1)S(1)}, bf16[1024,256]{1,0:T(8,128)(2,1)S(1)}, u32[]{:S(2)}, u32[]{:S(2)}) collective-permute-start(bf16[1024,256]{1,0:T(8,128)(2,1)S(1)} %get-tuple-element.64.refs_1_.refs_0_), channel_id=1, source_target_pairs={{0,8},{24,16},{1,9},{25,17},{2,10},{26,18},{3,11},{27,19},{4,12},{... | collective-permute-start | bytes 1572872 | tf_op jit(solution)/shard_map/ppermute | solution.py:403
  140.2 2.8 %collective-permute-done.19.sum_ref = bf16[1024,512]{1,0:T(8,128)(2,1)S(1)} collective-permute-done((bf16[1024,512]{1,0:T(8,128)(2,1)S(1)}, bf16[1024,512]{1,0:T(8,128)(2,1)S(1)}, u32[]{:S(2)}, u32[]{:S(2)}) %collective-permute-start.19) | collective-permute-done | bytes 1048608 | tf_op jit(solution)/shard_map/ppermute | solution.py:405
  143.4 2.9 %collective-permute-start.23 = (bf16[1024,256]{1,0:T(8,128)(2,1)S(1)}, bf16[1024,256]{1,0:T(8,128)(2,1)S(1)}, u32[]{:S(2)}, u32[]{:S(2)}) collective-permute-start(bf16[1024,256]{1,0:T(8,128)(2,1)S(1)} %get-tuple-element.80.refs_0_), channel_id=1, source_target_pairs={{0,8},{24,16},{1,9},{25,17},{2,10},{26,18},{3,11},{27,19},{4,12},{... | collective-permute-start | bytes 1572872 | tf_op jit(solution)/shard_map/ppermute | solution.py:406
  146.2 4.5 %collective-permute-done.15.refs_1_ = bf16[1024,256]{1,0:T(8,128)(2,1)S(1)} collective-permute-done((bf16[1024,256]{1,0:T(8,128)(2,1)S(1)}, bf16[1024,256]{1,0:T(8,128)(2,1)S(1)}, u32[]{:S(2)}, u32[]{:S(2)}) %collective-permute-start.15) | collective-permute-done | bytes 524320 | tf_op jit(solution)/shard_map/ppermute | solution.py:403
  155.9 4.3 %collective-permute-done.23.refs_0_ = bf16[1024,256]{1,0:T(8,128)(2,1)S(1)} collective-permute-done((bf16[1024,256]{1,0:T(8,128)(2,1)S(1)}, bf16[1024,256]{1,0:T(8,128)(2,1)S(1)}, u32[]{:S(2)}, u32[]{:S(2)}) %collective-permute-start.23) | collective-permute-done | bytes 524320 | tf_op jit(solution)/shard_map/ppermute | solution.py:406
  160.3 13.2 %collective-permute-start.25 = (bf16[1024,256]{1,0:T(8,128)(2,1)S(1)}, bf16[1024,256]{1,0:T(8,128)(2,1)S(1)}, u32[]{:S(2)}, u32[]{:S(2)}) collective-permute-start(bf16[1024,256]{1,0:T(8,128)(2,1)S(1)} %get-tuple-element.87.refs_1_.refs_0_), channel_id=1, source_target_pairs={{0,8},{24,16},{1,9},{25,17},{2,10},{26,18},{3,11},{27,19},{4,12},{... | collective-permute-start | bytes 1572872 | tf_op jit(solution)/shard_map/ppermute | solution.py:407
  177.3 5.6 %collective-permute-done.27.refs_2_ = bf16[1024,256]{1,0:T(8,128)(2,1)S(1)} collective-permute-done((bf16[1024,256]{1,0:T(8,128)(2,1)S(1)}, bf16[1024,256]{1,0:T(8,128)(2,1)S(1)}, u32[]{:S(2)}, u32[]{:S(2)}) %collective-permute-start.27) | collective-permute-done | bytes 524320 | tf_op jit(solution)/shard_map/ppermute | solution.py:414
  184.1 2.3 %early_kernel.3.refs_5_ = f32[1024,512]{1,0:T(8,128)S(1)} custom-call(bf16[1024,4096]{1,0:T(8,128)(2,1)S(1)} %cast.1.w_ref, bf16[1024,256]{1,0:T(8,128)(2,1)S(1)} %get-tuple-element.80.refs_0_, bf16[1024,256]{1,0:T(8,128)(2,1)S(1)} %get-tuple-element.87.refs_1_.refs_0_, bf16[1024,512]{1,0:T(8,128)(2,1)S(1)} %collective-permute-done.20.refs_2_.refs_1_), custom_call_target="tpu_custom_call" | custom-call | flops 1000 | bytes 1000 | tf_op jit(solution)/shard_map/early_kernel/pallas_call | solution.py:283
  189.0 8.3 %collective-permute-done.28.refs_3_ = bf16[1024,256]{1,0:T(8,128)(2,1)S(1)} collective-permute-done((bf16[1024,256]{1,0:T(8,128)(2,1)S(1)}, bf16[1024,256]{1,0:T(8,128)(2,1)S(1)}, u32[]{:S(2)}, u32[]{:S(2)}) %collective-permute-start.28) | collective-permute-done | bytes 524320 | tf_op jit(solution)/shard_map/ppermute | solution.py:416
  198.8 6.2 %base.3 = (f32[1024,512]{1,0:T(8,128)S(1)}, f32[1024,512]{1,0:T(8,128)S(1)}) custom-call(f32[1024,512]{1,0:T(8,128)S(1)} %get-tuple-element.66.refs_0_, f32[1024,512]{1,0:T(8,128)S(1)} %get-tuple-element.71.refs_1_, f32[1024,256]{1,0:T(8,128)S(1)} %collective-permute-done.21.refs_2_, f32[1024,256]{1,0:T(8,128)S(1)} %collective-permute-done.22.refs_3_, ...), custom_call_target="tpu_custom_call" | custom-call | flops 1000 | bytes 1000 | tf_op jit(solution)/shard_map/base/pallas_call | solution.py:128
  206.9 3.9 %collective-permute-done.29.refs_4_ = bf16[1024,256]{1,0:T(8,128)(2,1)S(1)} collective-permute-done((bf16[1024,256]{1,0:T(8,128)(2,1)S(1)}, bf16[1024,256]{1,0:T(8,128)(2,1)S(1)}, u32[]{:S(2)}, u32[]{:S(2)}) %collective-permute-start.29) | collective-permute-done | bytes 524320 | tf_op jit(solution)/shard_map/ppermute | solution.py:423
  212.1 2.3 %late_kernel.2.refs_0_ = f32[1024,512]{1,0:T(8,128)S(1)} custom-call(bf16[1024,4096]{1,0:T(8,128)(2,1)S(1)} %cast.1.w_ref, bf16[1024,256]{1,0:T(8,128)(2,1)S(1)} %collective-permute-done.13.refs_0_, bf16[1024,256]{1,0:T(8,128)(2,1)S(1)} %collective-permute-done.15.refs_1_, bf16[1024,256]{1,0:T(8,128)(2,1)S(1)} %collective-permute-done.16.refs_2_, ...), custom_call_target="tpu_custom_call" | custom-call | flops 1000 | bytes 1000 | tf_op jit(solution)/shard_map/late_kernel/pallas_call | solution.py:283
  214.4 2.3 %late_kernel.3.refs_1_ = f32[1024,512]{1,0:T(8,128)S(1)} custom-call(bf16[1024,4096]{1,0:T(8,128)(2,1)S(1)} %cast.1.w_ref, bf16[1024,256]{1,0:T(8,128)(2,1)S(1)} %collective-permute-done.23.refs_0_, bf16[1024,256]{1,0:T(8,128)(2,1)S(1)} %collective-permute-done.25.refs_1_, bf16[1024,256]{1,0:T(8,128)(2,1)S(1)} %collective-permute-done.24.refs_2_, ...), custom_call_target="tpu_custom_call" | custom-call | flops 1000 | bytes 1000 | tf_op jit(solution)/shard_map/late_kernel/pallas_call | solution.py:283
  216.8 6.6 %collective-permute-done.30.refs_5_ = bf16[1024,256]{1,0:T(8,128)(2,1)S(1)} collective-permute-done((bf16[1024,256]{1,0:T(8,128)(2,1)S(1)}, bf16[1024,256]{1,0:T(8,128)(2,1)S(1)}, u32[]{:S(2)}, u32[]{:S(2)}) %collective-permute-start.30) | collective-permute-done | bytes 524320 | tf_op jit(solution)/shard_map/ppermute | solution.py:426
  223.4 3.9 %unpack.1 = f32[8192,128]{1,0:T(8,128)} custom-call(f32[1024,512]{1,0:T(8,128)S(1)} %late_kernel.2.refs_0_, f32[1024,512]{1,0:T(8,128)S(1)} %late_kernel.3.refs_1_, bf16[1024,256]{1,0:T(8,128)(2,1)S(1)} %collective-permute-done.27.refs_2_, bf16[1024,256]{1,0:T(8,128)(2,1)S(1)} %collective-permute-done.28.refs_3_, ...), custom_call_target="tpu_custom_call" | custom-call | flops 1000 | bytes 1000 | tf_op jit(solution)/shard_map/unpack/pallas_call | solution.py:350
  (59 shorter events, 34.9 us)
Async XLA Ops:
  2.4 23.3 %collective-permute-start.5 = (bf16[128,3072]{1,0:T(8,128)(2,1)}, bf16[128,3072]{1,0:T(8,128)(2,1)S(1)}, u32[]{:S(2)}, u32[]{:S(2)}) collective-permute-start(bf16[128,3072]{1,0:T(8,128)(2,1)} %piece.1), channel_id=1, source_target_pairs={{0,8},{24,16},{1,9},{25,17},{2,10},{26,18},{3,11},{27,19},{4,12},{... | collective-permute-start | bytes 2359304 | tf_op jit(solution)/shard_map/ppermute | solution.py:379
  9.8 21.2 %collective-permute-start.1 = (bf16[1024,512]{1,0:T(8,128)(2,1)S(1)}, bf16[1024,512]{1,0:T(8,128)(2,1)S(1)}, u32[]{:S(2)}, u32[]{:S(2)}) collective-permute-start(bf16[1024,512]{1,0:T(8,128)(2,1)S(1)} %get-tuple-element.61.refs_0_), channel_id=1, source_target_pairs={{8,16},{16,8},{9,17},{17,9},{10,18},{18,10},{11,19},{19,11},{12,20... | collective-permute-start | bytes 3145736 | tf_op jit(solution)/shard_map/ppermute | solution.py:380
  10.5 21.2 %collective-permute-start.2 = (f32[1024,256]{1,0:T(8,128)S(1)}, f32[1024,256]{1,0:T(8,128)S(1)}, u32[]{:S(2)}, u32[]{:S(2)}) collective-permute-start(f32[1024,256]{1,0:T(8,128)S(1)} %get-tuple-element.49), channel_id=1, source_target_pairs={{0,1},{1,2},{2,3},{3,4},{4,5},{5,6},{6,7},{8,9},{9,10},{10,11},{11... | collective-permute-start | bytes 3145736 | tf_op jit(solution)/shard_map/ppermute | solution.py:382
  12.1 19.6 %copy-start.1 = (f32[2,1024]{1,0:T(2,128)S(1)}, f32[2,1024]{1,0:T(2,128)}, u32[]{:S(2)}) copy-start(f32[2,1024]{1,0:T(2,128)} %refs_4_.1) | copy-start | bytes 24580
  12.1 19.6 %collective-permute-start.3 = (f32[1024,256]{1,0:T(8,128)S(1)}, f32[1024,256]{1,0:T(8,128)S(1)}, u32[]{:S(2)}, u32[]{:S(2)}) collective-permute-start(f32[1024,256]{1,0:T(8,128)S(1)} %get-tuple-element.50), channel_id=1, source_target_pairs={{1,0},{2,1},{3,2},{4,3},{5,4},{6,5},{7,6},{9,8},{10,9},{11,10},{12... | collective-permute-start | bytes 3145736 | tf_op jit(solution)/shard_map/ppermute | solution.py:383
  13.5 33.2 %collective-permute-start = (bf16[1024,512]{1,0:T(8,128)(2,1)S(1)}, bf16[1024,512]{1,0:T(8,128)(2,1)S(1)}, u32[]{:S(2)}, u32[]{:S(2)}) collective-permute-start(bf16[1024,512]{1,0:T(8,128)(2,1)S(1)} %get-tuple-element.61.refs_0_), channel_id=1, source_target_pairs={{0,8},{24,16},{1,9},{25,17},{2,10},{26,18},{3,11},{27,19},{4,12},{... | collective-permute-start | bytes 3145736 | tf_op jit(solution)/shard_map/ppermute | solution.py:384
  25.7 22.7 %collective-permute-start.9 = (bf16[128,3072]{1,0:T(8,128)(2,1)S(1)}, bf16[128,3072]{1,0:T(8,128)(2,1)S(1)}, u32[]{:S(2)}, u32[]{:S(2)}) collective-permute-start(bf16[128,3072]{1,0:T(8,128)(2,1)S(1)} %collective-permute-done.5.refs_0_), channel_id=1, source_target_pairs={{0,6},{1,7},{2,4},{3,5},{4,2},{5,3},{6,0},{7,1},{8,14},{9,15},{10,... | collective-permute-start | bytes 2359304 | tf_op jit(solution)/shard_map/ppermute | solution.py:375
  31.0 30.4 %collective-permute-start.6 = (bf16[1024,512]{1,0:T(8,128)(2,1)S(1)}, bf16[1024,512]{1,0:T(8,128)(2,1)S(1)}, u32[]{:S(2)}, u32[]{:S(2)}) collective-permute-start(bf16[1024,512]{1,0:T(8,128)(2,1)S(1)} %get-tuple-element.68.refs_0_), channel_id=1, source_target_pairs={{8,16},{16,8},{9,17},{17,9},{10,18},{18,10},{11,19},{19,11},{12,20... | collective-permute-start | bytes 3145736 | tf_op jit(solution)/shard_map/ppermute | solution.py:381
  46.8 30.7 %collective-permute-start.4 = (bf16[1024,512]{1,0:T(8,128)(2,1)S(1)}, bf16[1024,512]{1,0:T(8,128)(2,1)S(1)}, u32[]{:S(2)}, u32[]{:S(2)}) collective-permute-start(bf16[1024,512]{1,0:T(8,128)(2,1)S(1)} %collective-permute-done.refs_1_), channel_id=1, source_target_pairs={{8,16},{16,8},{9,17},{17,9},{10,18},{18,10},{11,19},{19,11},{12,20... | collective-permute-start | bytes 3145736 | tf_op jit(solution)/shard_map/ppermute | solution.py:390
  48.5 29.1 %collective-permute-start.10 = (bf16[1024,512]{1,0:T(8,128)(2,1)S(1)}, bf16[1024,512]{1,0:T(8,128)(2,1)S(1)}, u32[]{:S(2)}, u32[]{:S(2)}) collective-permute-start(bf16[1024,512]{1,0:T(8,128)(2,1)S(1)} %get-tuple-element.68.refs_0_), channel_id=1, source_target_pairs={{0,8},{24,16},{1,9},{25,17},{2,10},{26,18},{3,11},{27,19},{4,12},{... | collective-permute-start | bytes 3145736 | tf_op jit(solution)/shard_map/ppermute | solution.py:389
  54.7 21.1 %collective-permute-start.8 = (bf16[128,3072]{1,0:T(8,128)(2,1)S(1)}, bf16[128,3072]{1,0:T(8,128)(2,1)S(1)}, u32[]{:S(2)}, u32[]{:S(2)}) collective-permute-start(bf16[128,3072]{1,0:T(8,128)(2,1)S(1)} %collective-permute-done.5.refs_0_), channel_id=1, source_target_pairs={{0,4},{1,5},{2,6},{3,7},{4,0},{5,1},{6,2},{7,3},{8,12},{9,13},{10,... | collective-permute-start | bytes 2359304 | tf_op jit(solution)/shard_map/ppermute | solution.py:375
  61.3 16.0 %collective-permute-start.7 = (bf16[128,3072]{1,0:T(8,128)(2,1)S(1)}, bf16[128,3072]{1,0:T(8,128)(2,1)S(1)}, u32[]{:S(2)}, u32[]{:S(2)}) collective-permute-start(bf16[128,3072]{1,0:T(8,128)(2,1)S(1)} %collective-permute-done.5.refs_0_), channel_id=1, source_target_pairs={{0,2},{1,3},{2,0},{3,1},{4,6},{5,7},{6,4},{7,5},{8,10},{9,11},{10,... | collective-permute-start | bytes 2359304 | tf_op jit(solution)/shard_map/ppermute | solution.py:375
  77.5 5.7 %collective-permute-start.11 = (bf16[512,3072]{1,0:T(8,128)(2,1)S(1)}, bf16[512,3072]{1,0:T(8,128)(2,1)S(1)}, u32[]{:S(2)}, u32[]{:S(2)}) collective-permute-start(bf16[512,3072]{1,0:T(8,128)(2,1)S(1)} %stack.1.this_ref), channel_id=1, source_target_pairs={{0,1},{1,0},{2,3},{3,2},{4,5},{5,4},{6,7},{7,6},{8,9},{9,8},{10,11... | collective-permute-start | bytes 9437192 | tf_op jit(solution)/shard_map/ppermute | solution.py:375
  77.6 11.1 %collective-permute-start.18 = (bf16[1024,512]{1,0:T(8,128)(2,1)S(1)}, bf16[1024,512]{1,0:T(8,128)(2,1)S(1)}, u32[]{:S(2)}, u32[]{:S(2)}) collective-permute-start(bf16[1024,512]{1,0:T(8,128)(2,1)S(1)} %collective-permute-done.10.refs_1_), channel_id=1, source_target_pairs={{8,16},{16,8},{9,17},{17,9},{10,18},{18,10},{11,19},{19,11},{12,20... | collective-permute-start | bytes 3145736 | tf_op jit(solution)/shard_map/ppermute | solution.py:392
  86.7 34.3 %collective-permute-start.12 = (bf16[1024,512]{1,0:T(8,128)(2,1)S(1)}, bf16[1024,512]{1,0:T(8,128)(2,1)S(1)}, u32[]{:S(2)}, u32[]{:S(2)}) collective-permute-start(bf16[1024,512]{1,0:T(8,128)(2,1)S(1)} %sum_kernel.6), channel_id=1, source_target_pairs={{8,0},{16,24},{9,1},{17,25},{10,2},{18,26},{11,3},{19,27},{12,4},{... | collective-permute-start | bytes 3145736 | tf_op jit(solution)/shard_map/ppermute | solution.py:401
  88.0 39.5 %collective-permute-start.14 = (bf16[1024,512]{1,0:T(8,128)(2,1)S(1)}, bf16[1024,512]{1,0:T(8,128)(2,1)S(1)}, u32[]{:S(2)}, u32[]{:S(2)}) collective-permute-start(bf16[1024,512]{1,0:T(8,128)(2,1)S(1)} %get-tuple-element.60), channel_id=1, source_target_pairs={{8,16},{16,8},{9,17},{17,9},{10,18},{18,10},{11,19},{19,11},{12,20... | collective-permute-start | bytes 3145736 | tf_op jit(solution)/shard_map/ppermute | solution.py:399
  92.1 50.9 %collective-permute-start.19 = (bf16[1024,512]{1,0:T(8,128)(2,1)S(1)}, bf16[1024,512]{1,0:T(8,128)(2,1)S(1)}, u32[]{:S(2)}, u32[]{:S(2)}) collective-permute-start(bf16[1024,512]{1,0:T(8,128)(2,1)S(1)} %sum_kernel.7), channel_id=1, source_target_pairs={{8,0},{16,24},{9,1},{17,25},{10,2},{18,26},{11,3},{19,27},{12,4},{... | collective-permute-start | bytes 3145736 | tf_op jit(solution)/shard_map/ppermute | solution.py:405
  98.1 48.1 %collective-permute-start.20 = (bf16[1024,512]{1,0:T(8,128)(2,1)S(1)}, bf16[1024,512]{1,0:T(8,128)(2,1)S(1)}, u32[]{:S(2)}, u32[]{:S(2)}) collective-permute-start(bf16[1024,512]{1,0:T(8,128)(2,1)S(1)} %get-tuple-element.73), channel_id=1, source_target_pairs={{8,16},{16,8},{9,17},{17,9},{10,18},{18,10},{11,19},{19,11},{12,20... | collective-permute-start | bytes 3145736 | tf_op jit(solution)/shard_map/ppermute | solution.py:400
  121.3 18.2 %collective-permute-start.13 = (bf16[1024,256]{1,0:T(8,128)(2,1)S(1)}, bf16[1024,256]{1,0:T(8,128)(2,1)S(1)}, u32[]{:S(2)}, u32[]{:S(2)}) collective-permute-start(bf16[1024,256]{1,0:T(8,128)(2,1)S(1)} %get-tuple-element.62.refs_0_), channel_id=1, source_target_pairs={{0,8},{24,16},{1,9},{25,17},{2,10},{26,18},{3,11},{27,19},{4,12},{... | collective-permute-start | bytes 1572872 | tf_op jit(solution)/shard_map/ppermute | solution.py:402
  127.4 23.3 %collective-permute-start.15 = (bf16[1024,256]{1,0:T(8,128)(2,1)S(1)}, bf16[1024,256]{1,0:T(8,128)(2,1)S(1)}, u32[]{:S(2)}, u32[]{:S(2)}) collective-permute-start(bf16[1024,256]{1,0:T(8,128)(2,1)S(1)} %get-tuple-element.64.refs_1_.refs_0_), channel_id=1, source_target_pairs={{0,8},{24,16},{1,9},{25,17},{2,10},{26,18},{3,11},{27,19},{4,12},{... | collective-permute-start | bytes 1572872 | tf_op jit(solution)/shard_map/ppermute | solution.py:403
  139.5 13.3 %collective-permute-start.16 = (bf16[1024,256]{1,0:T(8,128)(2,1)S(1)}, bf16[1024,256]{1,0:T(8,128)(2,1)S(1)}, u32[]{:S(2)}, u32[]{:S(2)}) collective-permute-start(bf16[1024,256]{1,0:T(8,128)(2,1)S(1)} %collective-permute-done.13.refs_0_), channel_id=1, source_target_pairs={{8,16},{16,8},{9,17},{17,9},{10,18},{18,10},{11,19},{19,11},{12,20... | collective-permute-start | bytes 1572872 | tf_op jit(solution)/shard_map/ppermute | solution.py:409
  143.4 16.9 %collective-permute-start.23 = (bf16[1024,256]{1,0:T(8,128)(2,1)S(1)}, bf16[1024,256]{1,0:T(8,128)(2,1)S(1)}, u32[]{:S(2)}, u32[]{:S(2)}) collective-permute-start(bf16[1024,256]{1,0:T(8,128)(2,1)S(1)} %get-tuple-element.80.refs_0_), channel_id=1, source_target_pairs={{0,8},{24,16},{1,9},{25,17},{2,10},{26,18},{3,11},{27,19},{4,12},{... | collective-permute-start | bytes 1572872 | tf_op jit(solution)/shard_map/ppermute | solution.py:406
  150.8 23.4 %collective-permute-start.17 = (bf16[1024,256]{1,0:T(8,128)(2,1)S(1)}, bf16[1024,256]{1,0:T(8,128)(2,1)S(1)}, u32[]{:S(2)}, u32[]{:S(2)}) collective-permute-start(bf16[1024,256]{1,0:T(8,128)(2,1)S(1)} %collective-permute-done.15.refs_1_), channel_id=1, source_target_pairs={{8,16},{16,8},{9,17},{17,9},{10,18},{18,10},{11,19},{19,11},{12,20... | collective-permute-start | bytes 1572872 | tf_op jit(solution)/shard_map/ppermute | solution.py:410
  151.4 35.8 %collective-permute-start.21 = (f32[1024,256]{1,0:T(8,128)S(1)}, f32[1024,256]{1,0:T(8,128)S(1)}, u32[]{:S(2)}, u32[]{:S(2)}) collective-permute-start(f32[1024,256]{1,0:T(8,128)S(1)} %get-tuple-element.74), channel_id=1, source_target_pairs={{0,1},{1,2},{2,3},{3,4},{4,5},{5,6},{6,7},{8,9},{9,10},{10,11},{11... | collective-permute-start | bytes 3145736 | tf_op jit(solution)/shard_map/ppermute | solution.py:417
  154.6 28.2 %collective-permute-start.27 = (bf16[1024,256]{1,0:T(8,128)(2,1)S(1)}, bf16[1024,256]{1,0:T(8,128)(2,1)S(1)}, u32[]{:S(2)}, u32[]{:S(2)}) collective-permute-start(bf16[1024,256]{1,0:T(8,128)(2,1)S(1)} %sum_kernel.10), channel_id=1, source_target_pairs={{8,0},{16,24},{9,1},{17,25},{10,2},{18,26},{11,3},{19,27},{12,4},{... | collective-permute-start | bytes 1572872 | tf_op jit(solution)/shard_map/ppermute | solution.py:414
  160.3 26.2 %collective-permute-start.25 = (bf16[1024,256]{1,0:T(8,128)(2,1)S(1)}, bf16[1024,256]{1,0:T(8,128)(2,1)S(1)}, u32[]{:S(2)}, u32[]{:S(2)}) collective-permute-start(bf16[1024,256]{1,0:T(8,128)(2,1)S(1)} %get-tuple-element.87.refs_1_.refs_0_), channel_id=1, source_target_pairs={{0,8},{24,16},{1,9},{25,17},{2,10},{26,18},{3,11},{27,19},{4,12},{... | collective-permute-start | bytes 1572872 | tf_op jit(solution)/shard_map/ppermute | solution.py:407
  173.4 13.1 %collective-permute-start.24 = (bf16[1024,256]{1,0:T(8,128)(2,1)S(1)}, bf16[1024,256]{1,0:T(8,128)(2,1)S(1)}, u32[]{:S(2)}, u32[]{:S(2)}) collective-permute-start(bf16[1024,256]{1,0:T(8,128)(2,1)S(1)} %collective-permute-done.23.refs_0_), channel_id=1, source_target_pairs={{8,16},{16,8},{9,17},{17,9},{10,18},{18,10},{11,19},{19,11},{12,20... | collective-permute-start | bytes 1572872 | tf_op jit(solution)/shard_map/ppermute | solution.py:420
  174.1 24.7 %collective-permute-start.22 = (f32[1024,256]{1,0:T(8,128)S(1)}, f32[1024,256]{1,0:T(8,128)S(1)}, u32[]{:S(2)}, u32[]{:S(2)}) collective-permute-start(f32[1024,256]{1,0:T(8,128)S(1)} %get-tuple-element.76), channel_id=1, source_target_pairs={{1,0},{2,1},{3,2},{4,3},{5,4},{6,5},{7,6},{9,8},{10,9},{11,10},{12... | collective-permute-start | bytes 3145736 | tf_op jit(solution)/shard_map/ppermute | solution.py:418
  182.9 14.4 %collective-permute-start.28 = (bf16[1024,256]{1,0:T(8,128)(2,1)S(1)}, bf16[1024,256]{1,0:T(8,128)(2,1)S(1)}, u32[]{:S(2)}, u32[]{:S(2)}) collective-permute-start(bf16[1024,256]{1,0:T(8,128)(2,1)S(1)} %sum_kernel.8), channel_id=1, source_target_pairs={{8,0},{16,24},{9,1},{17,25},{10,2},{18,26},{11,3},{19,27},{12,4},{... | collective-permute-start | bytes 1572872 | tf_op jit(solution)/shard_map/ppermute | solution.py:416
  186.5 18.6 %collective-permute-start.26 = (bf16[1024,256]{1,0:T(8,128)(2,1)S(1)}, bf16[1024,256]{1,0:T(8,128)(2,1)S(1)}, u32[]{:S(2)}, u32[]{:S(2)}) collective-permute-start(bf16[1024,256]{1,0:T(8,128)(2,1)S(1)} %collective-permute-done.25.refs_1_), channel_id=1, source_target_pairs={{8,16},{16,8},{9,17},{17,9},{10,18},{18,10},{11,19},{19,11},{12,20... | collective-permute-start | bytes 1572872 | tf_op jit(solution)/shard_map/ppermute | solution.py:421
  197.3 13.5 %collective-permute-start.29 = (bf16[1024,256]{1,0:T(8,128)(2,1)S(1)}, bf16[1024,256]{1,0:T(8,128)(2,1)S(1)}, u32[]{:S(2)}, u32[]{:S(2)}) collective-permute-start(bf16[1024,256]{1,0:T(8,128)(2,1)S(1)} %sum_kernel.9), channel_id=1, source_target_pairs={{8,0},{16,24},{9,1},{17,25},{10,2},{18,26},{11,3},{19,27},{12,4},{... | collective-permute-start | bytes 1572872 | tf_op jit(solution)/shard_map/ppermute | solution.py:423
  210.8 12.6 %collective-permute-start.30 = (bf16[1024,256]{1,0:T(8,128)(2,1)S(1)}, bf16[1024,256]{1,0:T(8,128)(2,1)S(1)}, u32[]{:S(2)}, u32[]{:S(2)}) collective-permute-start(bf16[1024,256]{1,0:T(8,128)(2,1)S(1)} %sum_kernel.11), channel_id=1, source_target_pairs={{8,0},{16,24},{9,1},{17,25},{10,2},{18,26},{11,3},{19,27},{12,4},{... | collective-permute-start | bytes 1572872 | tf_op jit(solution)/shard_map/ppermute | solution.py:426
  (3 other events, 53.4 us)

commit v5 on v3

--- a/solution.py
+++ b/solution.py
@@ -47,7 +47,7 @@
 
 def pack(field):
     modes, rows, columns = field.shape
-    blocks = 4
+    blocks = 8
     shape = lambda count, kind: jax.ShapeDtypeStruct((modes, count * columns), kind)
     return pl.pallas_call(
         functools.partial(pack_kernel, blocks),
@@ -141,10 +141,18 @@
     at = pl.multiple_of(lax.axis_index("tile") * share, share)
     skipped = w_ref.shape[1] - kept
     left = pl.multiple_of(jnp.where(lax.axis_index("mode") == 0, skipped, 0), skipped)
-    copy = pltpu.make_async_copy(w_ref.at[pl.ds(at, share), pl.ds(left, kept)], held_ref, done_ref)
-    copy.start()
-    copy.wait()
-    out_ref[...] = held_ref[...].astype(bf16)
+    count = done_ref.shape[0]
+    rows = share // count
+    spans = [pl.ds(i * rows, rows) for i in range(count)]
+    copies = [
+        pltpu.make_async_copy(w_ref.at[pl.ds(at + i * rows, rows), pl.ds(left, kept)], held_ref.at[span], done_ref.at[i])
+        for i, span in enumerate(spans)
+    ]
+    for copy in copies:
+        copy.start()
+    for copy, span in zip(copies, spans):
+        copy.wait()
+        out_ref[span, :] = held_ref[span, :].astype(bf16)
 
 
 def piece_of(weights, count):
@@ -155,7 +163,7 @@
         in_specs=[pl.BlockSpec(memory_space=pl.ANY)],
         out_specs=pl.BlockSpec(memory_space=pltpu.VMEM),
         out_shape=jax.ShapeDtypeStruct(shape, bf16),
-        scratch_shapes=[pltpu.VMEM(shape, f32), pltpu.SemaphoreType.DMA],
+        scratch_shapes=[pltpu.VMEM(shape, f32), pltpu.SemaphoreType.DMA((4,))],
         name="piece",
         **small(56),
     )(weights)

time: 227 us -> 227 us (level)
  no operation moved by 1% of the time
where the time goes in v5:
time: 227 us; the launch traced here: 226 us
  waiting for transfers between devices  82.9 us (37%)
  starting transfers between devices  79.3 us (35%)
  Pallas kernels  63.3 us (28%)
    pallas_call x10, Pallas kernels, gains(): pl.pallas_call(kernel, in_specs=[vmem] * len(arrays), out_specs=[vmem] *...  33.9 us
    ppermute x1, waiting for transfers between devices, line_of_four(): field1, x1, y1, low = meet(first1, send(sum1, perm=outward), columns, True)  22.3 us
    ppermute x4, waiting for transfers between devices, line_of_four(): lax.ppermute(value, 'tile', [(i, i ^ bits) for i in range(count)])  16.4 us
    ppermute x1, starting transfers between devices, line_of_four(): d2 = send(after(y2, a2), perm=inward)  13.2 us
    pallas_call x2, Pallas kernels, base(): pl.pallas_call(functools.partial(base_kernel, rows, block, strided), grid...  13 us
    ppermute x4, starting transfers between devices, line_of_four(): lax.ppermute(value, 'tile', [(i, i ^ bits) for i in range(count)])  11.8 us
    ppermute x2, waiting for transfers between devices, line_of_four(): a1 = send(x1, perm=inward)  11.3 us
    ppermute x1, waiting for transfers between devices, line_of_four(): rut1 = send(after(rum1, out1), perm=outward)  10.6 us
  transfers between devices with their start and end apart: 31, of which 15 were waited for; matrix products, arithmetic and copies ran while one was open for 0% of the time, Pallas kernels for 26%

profile of v5, /device:TPU:0, one launch (start us, length us, event | category | flops | bytes accessed | tf_op | source)
XLA Modules:
  0.0 226.0 jit_solution(15205018923494842373)
XLA Ops:
  0.0 2.3 %piece.1 = bf16[128,3072]{1,0:T(8,128)(2,1)} custom-call(f32[1024,4096]{1,0:T(8,128)} %w_ref.2), custom_call_target="tpu_custom_call" | custom-call | flops 1000 | bytes 1000 | tf_op jit(solution)/shard_map/piece/pallas_call | solution.py:161
  2.3 5.0 %collective-permute-start.5 = (bf16[128,3072]{1,0:T(8,128)(2,1)}, bf16[128,3072]{1,0:T(8,128)(2,1)S(1)}, u32[]{:S(2)}, u32[]{:S(2)}) collective-permute-start(bf16[128,3072]{1,0:T(8,128)(2,1)} %piece.1), channel_id=1, source_target_pairs={{0,8},{24,16},{1,9},{25,17},{2,10},{26,18},{3,11},{27,19},{4,12},{... | collective-permute-start | bytes 2359304 | tf_op jit(solution)/shard_map/ppermute | solution.py:366
  7.3 2.3 %pack.1 = (bf16[1024,512]{1,0:T(8,128)(2,1)S(1)}, bf16[1024,512]{1,0:T(8,128)(2,1)S(1)}, f32[1024,256]{1,0:T(8,128)S(1)}, f32[1024,256]{1,0:T(8,128)S(1)}) custom-call(f32[8192,128]{1,0:T(8,128)} %bitcast.3), custom_call_target="tpu_custom_call" | custom-call | flops 1000 | bytes 1000 | tf_op jit(solution)/shard_map/pack/pallas_call | solution.py:52
  13.3 4.1 %collective-permute-start = (bf16[1024,512]{1,0:T(8,128)(2,1)S(1)}, bf16[1024,512]{1,0:T(8,128)(2,1)S(1)}, u32[]{:S(2)}, u32[]{:S(2)}) collective-permute-start(bf16[1024,512]{1,0:T(8,128)(2,1)S(1)} %get-tuple-element.62.refs_0_), channel_id=1, source_target_pairs={{0,8},{24,16},{1,9},{25,17},{2,10},{26,18},{3,11},{27,19},{4,12},{... | collective-permute-start | bytes 3145736 | tf_op jit(solution)/shard_map/ppermute | solution.py:371
  17.4 8.1 %cast.1.w_ref = bf16[1024,4096]{1,0:T(8,128)(2,1)S(1)} custom-call(f32[1024,4096]{1,0:T(8,128)} %w_ref.2), custom_call_target="tpu_custom_call" | custom-call | flops 1000 | bytes 1000 | tf_op jit(solution)/shard_map/cast/pallas_call | solution.py:215
  25.5 5.3 %collective-permute-start.9 = (bf16[128,3072]{1,0:T(8,128)(2,1)S(1)}, bf16[128,3072]{1,0:T(8,128)(2,1)S(1)}, u32[]{:S(2)}, u32[]{:S(2)}) collective-permute-start(bf16[128,3072]{1,0:T(8,128)(2,1)S(1)} %collective-permute-done.5.refs_0_), channel_id=1, source_target_pairs={{0,6},{1,7},{2,4},{3,5},{4,2},{5,3},{6,0},{7,1},{8,14},{9,15},{10,... | collective-permute-start | bytes 2359304 | tf_op jit(solution)/shard_map/ppermute | solution.py:362
  31.6 6.7 %base.2 = (f32[1024,512]{1,0:T(8,128)S(1)}, f32[1024,512]{1,0:T(8,128)S(1)}) custom-call(f32[8192,128]{1,0:T(8,128)S(1)} %bitcast.4, f32[1024,256]{1,0:T(8,128)S(1)} %collective-permute-done.2.refs_1_, f32[1024,256]{1,0:T(8,128)S(1)} %collective-permute-done.3.refs_2_, f32[2,1024]{1,0:T(2,128)S(1)} %copy-done.1, f32[1,1024]{1,0:T(1,128)S(1)} %bitcast.5, ...), custom_call_target="tpu_custom_call" | custom-call | flops 1000 | bytes 1000 | tf_op jit(solution)/shard_map/base/pallas_call | solution.py:128
  38.3 8.4 %collective-permute-done.refs_1_ = bf16[1024,512]{1,0:T(8,128)(2,1)S(1)} collective-permute-done((bf16[1024,512]{1,0:T(8,128)(2,1)S(1)}, bf16[1024,512]{1,0:T(8,128)(2,1)S(1)}, u32[]{:S(2)}, u32[]{:S(2)}) %collective-permute-start) | collective-permute-done | bytes 1048608 | tf_op jit(solution)/shard_map/ppermute | solution.py:371
  48.3 6.4 %collective-permute-start.10 = (bf16[1024,512]{1,0:T(8,128)(2,1)S(1)}, bf16[1024,512]{1,0:T(8,128)(2,1)S(1)}, u32[]{:S(2)}, u32[]{:S(2)}) collective-permute-start(bf16[1024,512]{1,0:T(8,128)(2,1)S(1)} %get-tuple-element.68.refs_0_), channel_id=1, source_target_pairs={{0,8},{24,16},{1,9},{25,17},{2,10},{26,18},{3,11},{27,19},{4,12},{... | collective-permute-start | bytes 3145736 | tf_op jit(solution)/shard_map/ppermute | solution.py:376
  54.6 6.5 %collective-permute-start.7 = (bf16[128,3072]{1,0:T(8,128)(2,1)S(1)}, bf16[128,3072]{1,0:T(8,128)(2,1)S(1)}, u32[]{:S(2)}, u32[]{:S(2)}) collective-permute-start(bf16[128,3072]{1,0:T(8,128)(2,1)S(1)} %collective-permute-done.5.refs_0_), channel_id=1, source_target_pairs={{0,2},{1,3},{2,0},{3,1},{4,6},{5,7},{6,4},{7,5},{8,10},{9,11},{10,... | collective-permute-start | bytes 2359304 | tf_op jit(solution)/shard_map/ppermute | solution.py:362
  61.2 13.6 %collective-permute-done.7.refs_1_ = bf16[128,3072]{1,0:T(8,128)(2,1)S(1)} collective-permute-done((bf16[128,3072]{1,0:T(8,128)(2,1)S(1)}, bf16[128,3072]{1,0:T(8,128)(2,1)S(1)}, u32[]{:S(2)}, u32[]{:S(2)}) %collective-permute-start.7) | collective-permute-done | bytes 786464 | tf_op jit(solution)/shard_map/ppermute | solution.py:362
  77.9 4.5 %own_kernel.4 = (f32[1024,512]{1,0:T(8,128)S(1)}, bf16[1024,512]{1,0:T(8,128)(2,1)S(1)}) custom-call(bf16[1024,4096]{1,0:T(8,128)(2,1)S(1)} %cast.1.w_ref, bf16[1024,512]{1,0:T(8,128)(2,1)S(1)} %get-tuple-element.62.refs_0_, bf16[1024,512]{1,0:T(8,128)(2,1)S(1)} %collective-permute-done.refs_1_, ...), custom_call_target="tpu_custom_call" | custom-call | flops 1000 | bytes 1000 | tf_op jit(solution)/shard_map/own_kernel/pallas_call | solution.py:280
  82.8 3.4 %sum_kernel.6 = bf16[1024,512]{1,0:T(8,128)(2,1)S(1)} custom-call(bf16[512,3072]{1,0:T(8,128)(2,1)S(1)} %stack.1.this_ref, bf16[512,3072]{1,0:T(8,128)(2,1)S(1)} %collective-permute-done.11.other_ref, bf16[1024,512]{1,0:T(8,128)(2,1)S(1)} %get-tuple-element.62.refs_0_, bf16[1024,512]{1,0:T(8,128)(2,1)S(1)} %collective-permute-done.1.refs_2_.refs_1_, ...), custom_call_target="tpu_custom_call" | custom-call | flops 1000 | bytes 1000 | tf_op jit(solution)/shard_map/sum_kernel/pallas_call | solution.py:280
  88.3 3.4 %sum_kernel.7 = bf16[1024,512]{1,0:T(8,128)(2,1)S(1)} custom-call(bf16[512,3072]{1,0:T(8,128)(2,1)S(1)} %stack.1.this_ref, bf16[512,3072]{1,0:T(8,128)(2,1)S(1)} %collective-permute-done.11.other_ref, bf16[1024,512]{1,0:T(8,128)(2,1)S(1)} %get-tuple-element.68.refs_0_, bf16[1024,512]{1,0:T(8,128)(2,1)S(1)} %collective-permute-done.6.refs_1_.refs_2_, ...), custom_call_target="tpu_custom_call" | custom-call | flops 1000 | bytes 1000 | tf_op jit(solution)/shard_map/sum_kernel/pallas_call | solution.py:280
  93.2 4.5 %own_kernel.5 = (f32[1024,512]{1,0:T(8,128)S(1)}, bf16[1024,512]{1,0:T(8,128)(2,1)S(1)}) custom-call(bf16[1024,4096]{1,0:T(8,128)(2,1)S(1)} %cast.1.w_ref, bf16[1024,512]{1,0:T(8,128)(2,1)S(1)} %get-tuple-element.68.refs_0_, bf16[1024,512]{1,0:T(8,128)(2,1)S(1)} %collective-permute-done.10.refs_1_, ...), custom_call_target="tpu_custom_call" | custom-call | flops 1000 | bytes 1000 | tf_op jit(solution)/shard_map/own_kernel/pallas_call | solution.py:280
  98.4 22.3 %collective-permute-done.12.sum_ref = bf16[1024,512]{1,0:T(8,128)(2,1)S(1)} collective-permute-done((bf16[1024,512]{1,0:T(8,128)(2,1)S(1)}, bf16[1024,512]{1,0:T(8,128)(2,1)S(1)}, u32[]{:S(2)}, u32[]{:S(2)}) %collective-permute-start.12) | collective-permute-done | bytes 1048608 | tf_op jit(solution)/shard_map/ppermute | solution.py:388
  121.1 6.1 %collective-permute-start.13 = (bf16[1024,256]{1,0:T(8,128)(2,1)S(1)}, bf16[1024,256]{1,0:T(8,128)(2,1)S(1)}, u32[]{:S(2)}, u32[]{:S(2)}) collective-permute-start(bf16[1024,256]{1,0:T(8,128)(2,1)S(1)} %get-tuple-element.63.refs_0_), channel_id=1, source_target_pairs={{0,8},{24,16},{1,9},{25,17},{2,10},{26,18},{3,11},{27,19},{4,12},{... | collective-permute-start | bytes 1572872 | tf_op jit(solution)/shard_map/ppermute | solution.py:389
  127.2 9.1 %collective-permute-start.15 = (bf16[1024,256]{1,0:T(8,128)(2,1)S(1)}, bf16[1024,256]{1,0:T(8,128)(2,1)S(1)}, u32[]{:S(2)}, u32[]{:S(2)}) collective-permute-start(bf16[1024,256]{1,0:T(8,128)(2,1)S(1)} %get-tuple-element.65.refs_1_.refs_0_), channel_id=1, source_target_pairs={{0,8},{24,16},{1,9},{25,17},{2,10},{26,18},{3,11},{27,19},{4,12},{... | collective-permute-start | bytes 1572872 | tf_op jit(solution)/shard_map/ppermute | solution.py:390
  136.4 3.0 %collective-permute-done.13.refs_2_ = bf16[1024,256]{1,0:T(8,128)(2,1)S(1)} collective-permute-done((bf16[1024,256]{1,0:T(8,128)(2,1)S(1)}, bf16[1024,256]{1,0:T(8,128)(2,1)S(1)}, u32[]{:S(2)}, u32[]{:S(2)}) %collective-permute-start.13) | collective-permute-done | bytes 524320 | tf_op jit(solution)/shard_map/ppermute | solution.py:389
  140.0 2.8 %collective-permute-done.19.sum_ref = bf16[1024,512]{1,0:T(8,128)(2,1)S(1)} collective-permute-done((bf16[1024,512]{1,0:T(8,128)(2,1)S(1)}, bf16[1024,512]{1,0:T(8,128)(2,1)S(1)}, u32[]{:S(2)}, u32[]{:S(2)}) %collective-permute-start.19) | collective-permute-done | bytes 1048608 | tf_op jit(solution)/shard_map/ppermute | solution.py:391
  143.2 2.9 %collective-permute-start.23 = (bf16[1024,256]{1,0:T(8,128)(2,1)S(1)}, bf16[1024,256]{1,0:T(8,128)(2,1)S(1)}, u32[]{:S(2)}, u32[]{:S(2)}) collective-permute-start(bf16[1024,256]{1,0:T(8,128)(2,1)S(1)} %get-tuple-element.81.refs_0_), channel_id=1, source_target_pairs={{0,8},{24,16},{1,9},{25,17},{2,10},{26,18},{3,11},{27,19},{4,12},{... | collective-permute-start | bytes 1572872 | tf_op jit(solution)/shard_map/ppermute | solution.py:392
  146.0 4.5 %collective-permute-done.15.refs_3_ = bf16[1024,256]{1,0:T(8,128)(2,1)S(1)} collective-permute-done((bf16[1024,256]{1,0:T(8,128)(2,1)S(1)}, bf16[1024,256]{1,0:T(8,128)(2,1)S(1)}, u32[]{:S(2)}, u32[]{:S(2)}) %collective-permute-start.15) | collective-permute-done | bytes 524320 | tf_op jit(solution)/shard_map/ppermute | solution.py:390
  155.7 4.3 %collective-permute-done.23.refs_2_ = bf16[1024,256]{1,0:T(8,128)(2,1)S(1)} collective-permute-done((bf16[1024,256]{1,0:T(8,128)(2,1)S(1)}, bf16[1024,256]{1,0:T(8,128)(2,1)S(1)}, u32[]{:S(2)}, u32[]{:S(2)}) %collective-permute-start.23) | collective-permute-done | bytes 524320 | tf_op jit(solution)/shard_map/ppermute | solution.py:392
  160.1 13.2 %collective-permute-start.25 = (bf16[1024,256]{1,0:T(8,128)(2,1)S(1)}, bf16[1024,256]{1,0:T(8,128)(2,1)S(1)}, u32[]{:S(2)}, u32[]{:S(2)}) collective-permute-start(bf16[1024,256]{1,0:T(8,128)(2,1)S(1)} %get-tuple-element.89.refs_1_.refs_0_), channel_id=1, source_target_pairs={{0,8},{24,16},{1,9},{25,17},{2,10},{26,18},{3,11},{27,19},{4,12},{... | collective-permute-start | bytes 1572872 | tf_op jit(solution)/shard_map/ppermute | solution.py:393
  175.3 1.8 sum_kernel.8
  177.1 5.6 %collective-permute-done.27.refs_2_ = bf16[1024,256]{1,0:T(8,128)(2,1)S(1)} collective-permute-done((bf16[1024,256]{1,0:T(8,128)(2,1)S(1)}, bf16[1024,256]{1,0:T(8,128)(2,1)S(1)}, u32[]{:S(2)}, u32[]{:S(2)}) %collective-permute-start.27) | collective-permute-done | bytes 524320 | tf_op jit(solution)/shard_map/ppermute | solution.py:399
  186.5 10.6 %collective-permute-done.28.refs_3_ = bf16[1024,256]{1,0:T(8,128)(2,1)S(1)} collective-permute-done((bf16[1024,256]{1,0:T(8,128)(2,1)S(1)}, bf16[1024,256]{1,0:T(8,128)(2,1)S(1)}, u32[]{:S(2)}, u32[]{:S(2)}) %collective-permute-start.28) | collective-permute-done | bytes 524320 | tf_op jit(solution)/shard_map/ppermute | solution.py:401
  198.4 6.2 %base.3 = (f32[1024,512]{1,0:T(8,128)S(1)}, f32[1024,512]{1,0:T(8,128)S(1)}) custom-call(f32[1024,512]{1,0:T(8,128)S(1)} %get-tuple-element.66.refs_0_, f32[1024,512]{1,0:T(8,128)S(1)} %get-tuple-element.71.refs_1_, f32[1024,256]{1,0:T(8,128)S(1)} %collective-permute-done.21.refs_2_, f32[1024,256]{1,0:T(8,128)S(1)} %collective-permute-done.22.refs_3_, ...), custom_call_target="tpu_custom_call" | custom-call | flops 1000 | bytes 1000 | tf_op jit(solution)/shard_map/base/pallas_call | solution.py:128
  206.4 4.1 %collective-permute-done.29.refs_4_ = bf16[1024,256]{1,0:T(8,128)(2,1)S(1)} collective-permute-done((bf16[1024,256]{1,0:T(8,128)(2,1)S(1)}, bf16[1024,256]{1,0:T(8,128)(2,1)S(1)}, u32[]{:S(2)}, u32[]{:S(2)}) %collective-permute-start.29) | collective-permute-done | bytes 524320 | tf_op jit(solution)/shard_map/ppermute | solution.py:408
  212.1 5.5 %own_kernel.6 = (f32[1024,512]{1,0:T(8,128)S(1)}, bf16[1024,512]{1,0:T(8,128)(2,1)}) custom-call(bf16[1024,4096]{1,0:T(8,128)(2,1)S(1)} %cast.1.w_ref, bf16[1024,256]{1,0:T(8,128)(2,1)S(1)} %get-tuple-element.63.refs_0_, bf16[1024,256]{1,0:T(8,128)(2,1)S(1)} %get-tuple-element.65.refs_1_.refs_0_, bf16[1024,256]{1,0:T(8,128)(2,1)S(1)} %collective-permute-done.13.refs_2_, ...), custom_call_target="tpu_custom_call" | custom-call | flops 1000 | bytes 1000 | tf_op jit(solution)/shard_map/own_kernel/pallas_call | solution.py:280
  217.6 5.5 %own_kernel.7 = (f32[1024,512]{1,0:T(8,128)S(1)}, bf16[1024,512]{1,0:T(8,128)(2,1)}) custom-call(bf16[1024,4096]{1,0:T(8,128)(2,1)S(1)} %cast.1.w_ref, bf16[1024,256]{1,0:T(8,128)(2,1)S(1)} %get-tuple-element.81.refs_0_, bf16[1024,256]{1,0:T(8,128)(2,1)S(1)} %get-tuple-element.89.refs_1_.refs_0_, bf16[1024,256]{1,0:T(8,128)(2,1)S(1)} %collective-permute-done.23.refs_2_, ...), custom_call_target="tpu_custom_call" | custom-call | flops 1000 | bytes 1000 | tf_op jit(solution)/shard_map/own_kernel/pallas_call | solution.py:280
  223.2 2.9 %unpack.1 = f32[8192,128]{1,0:T(8,128)} custom-call(f32[1024,512]{1,0:T(8,128)S(1)} %get-tuple-element.78.refs_0_, f32[1024,512]{1,0:T(8,128)S(1)} %get-tuple-element.86.refs_1_, bf16[1024,256]{1,0:T(8,128)(2,1)S(1)} %collective-permute-done.27.refs_2_, bf16[1024,256]{1,0:T(8,128)(2,1)S(1)} %collective-permute-done.28.refs_3_, ...), custom_call_target="tpu_custom_call" | custom-call | flops 1000 | bytes 1000 | tf_op jit(solution)/shard_map/unpack/pallas_call | solution.py:337
  (57 shorter events, 30.8 us)
Async XLA Ops:
  2.3 23.2 %collective-permute-start.5 = (bf16[128,3072]{1,0:T(8,128)(2,1)}, bf16[128,3072]{1,0:T(8,128)(2,1)S(1)}, u32[]{:S(2)}, u32[]{:S(2)}) collective-permute-start(bf16[128,3072]{1,0:T(8,128)(2,1)} %piece.1), channel_id=1, source_target_pairs={{0,8},{24,16},{1,9},{25,17},{2,10},{26,18},{3,11},{27,19},{4,12},{... | collective-permute-start | bytes 2359304 | tf_op jit(solution)/shard_map/ppermute | solution.py:366
  9.6 21.2 %collective-permute-start.1 = (bf16[1024,512]{1,0:T(8,128)(2,1)S(1)}, bf16[1024,512]{1,0:T(8,128)(2,1)S(1)}, u32[]{:S(2)}, u32[]{:S(2)}) collective-permute-start(bf16[1024,512]{1,0:T(8,128)(2,1)S(1)} %get-tuple-element.62.refs_0_), channel_id=1, source_target_pairs={{8,16},{16,8},{9,17},{17,9},{10,18},{18,10},{11,19},{19,11},{12,20... | collective-permute-start | bytes 3145736 | tf_op jit(solution)/shard_map/ppermute | solution.py:367
  10.3 21.2 %collective-permute-start.2 = (f32[1024,256]{1,0:T(8,128)S(1)}, f32[1024,256]{1,0:T(8,128)S(1)}, u32[]{:S(2)}, u32[]{:S(2)}) collective-permute-start(f32[1024,256]{1,0:T(8,128)S(1)} %get-tuple-element.50), channel_id=1, source_target_pairs={{0,1},{1,2},{2,3},{3,4},{4,5},{5,6},{6,7},{8,9},{9,10},{10,11},{11... | collective-permute-start | bytes 3145736 | tf_op jit(solution)/shard_map/ppermute | solution.py:369
  11.9 19.6 %copy-start.1 = (f32[2,1024]{1,0:T(2,128)S(1)}, f32[2,1024]{1,0:T(2,128)}, u32[]{:S(2)}) copy-start(f32[2,1024]{1,0:T(2,128)} %refs_4_.1) | copy-start | bytes 24580
  11.9 19.6 %collective-permute-start.3 = (f32[1024,256]{1,0:T(8,128)S(1)}, f32[1024,256]{1,0:T(8,128)S(1)}, u32[]{:S(2)}, u32[]{:S(2)}) collective-permute-start(f32[1024,256]{1,0:T(8,128)S(1)} %get-tuple-element.51), channel_id=1, source_target_pairs={{1,0},{2,1},{3,2},{4,3},{5,4},{6,5},{7,6},{9,8},{10,9},{11,10},{12... | collective-permute-start | bytes 3145736 | tf_op jit(solution)/shard_map/ppermute | solution.py:370
  13.3 33.3 %collective-permute-start = (bf16[1024,512]{1,0:T(8,128)(2,1)S(1)}, bf16[1024,512]{1,0:T(8,128)(2,1)S(1)}, u32[]{:S(2)}, u32[]{:S(2)}) collective-permute-start(bf16[1024,512]{1,0:T(8,128)(2,1)S(1)} %get-tuple-element.62.refs_0_), channel_id=1, source_target_pairs={{0,8},{24,16},{1,9},{25,17},{2,10},{26,18},{3,11},{27,19},{4,12},{... | collective-permute-start | bytes 3145736 | tf_op jit(solution)/shard_map/ppermute | solution.py:371
  25.5 22.7 %collective-permute-start.9 = (bf16[128,3072]{1,0:T(8,128)(2,1)S(1)}, bf16[128,3072]{1,0:T(8,128)(2,1)S(1)}, u32[]{:S(2)}, u32[]{:S(2)}) collective-permute-start(bf16[128,3072]{1,0:T(8,128)(2,1)S(1)} %collective-permute-done.5.refs_0_), channel_id=1, source_target_pairs={{0,6},{1,7},{2,4},{3,5},{4,2},{5,3},{6,0},{7,1},{8,14},{9,15},{10,... | collective-permute-start | bytes 2359304 | tf_op jit(solution)/shard_map/ppermute | solution.py:362
  30.8 30.4 %collective-permute-start.6 = (bf16[1024,512]{1,0:T(8,128)(2,1)S(1)}, bf16[1024,512]{1,0:T(8,128)(2,1)S(1)}, u32[]{:S(2)}, u32[]{:S(2)}) collective-permute-start(bf16[1024,512]{1,0:T(8,128)(2,1)S(1)} %get-tuple-element.68.refs_0_), channel_id=1, source_target_pairs={{8,16},{16,8},{9,17},{17,9},{10,18},{18,10},{11,19},{19,11},{12,20... | collective-permute-start | bytes 3145736 | tf_op jit(solution)/shard_map/ppermute | solution.py:368
  46.7 29.8 %collective-permute-start.4 = (bf16[1024,512]{1,0:T(8,128)(2,1)S(1)}, bf16[1024,512]{1,0:T(8,128)(2,1)S(1)}, u32[]{:S(2)}, u32[]{:S(2)}) collective-permute-start(bf16[1024,512]{1,0:T(8,128)(2,1)S(1)} %collective-permute-done.refs_1_), channel_id=1, source_target_pairs={{8,16},{16,8},{9,17},{17,9},{10,18},{18,10},{11,19},{19,11},{12,20... | collective-permute-start | bytes 3145736 | tf_op jit(solution)/shard_map/ppermute | solution.py:377
  48.3 28.9 %collective-permute-start.10 = (bf16[1024,512]{1,0:T(8,128)(2,1)S(1)}, bf16[1024,512]{1,0:T(8,128)(2,1)S(1)}, u32[]{:S(2)}, u32[]{:S(2)}) collective-permute-start(bf16[1024,512]{1,0:T(8,128)(2,1)S(1)} %get-tuple-element.68.refs_0_), channel_id=1, source_target_pairs={{0,8},{24,16},{1,9},{25,17},{2,10},{26,18},{3,11},{27,19},{4,12},{... | collective-permute-start | bytes 3145736 | tf_op jit(solution)/shard_map/ppermute | solution.py:376
  54.6 20.1 %collective-permute-start.7 = (bf16[128,3072]{1,0:T(8,128)(2,1)S(1)}, bf16[128,3072]{1,0:T(8,128)(2,1)S(1)}, u32[]{:S(2)}, u32[]{:S(2)}) collective-permute-start(bf16[128,3072]{1,0:T(8,128)(2,1)S(1)} %collective-permute-done.5.refs_0_), channel_id=1, source_target_pairs={{0,2},{1,3},{2,0},{3,1},{4,6},{5,7},{6,4},{7,5},{8,10},{9,11},{10,... | collective-permute-start | bytes 2359304 | tf_op jit(solution)/shard_map/ppermute | solution.py:362
  61.1 15.1 %collective-permute-start.8 = (bf16[128,3072]{1,0:T(8,128)(2,1)S(1)}, bf16[128,3072]{1,0:T(8,128)(2,1)S(1)}, u32[]{:S(2)}, u32[]{:S(2)}) collective-permute-start(bf16[128,3072]{1,0:T(8,128)(2,1)S(1)} %collective-permute-done.5.refs_0_), channel_id=1, source_target_pairs={{0,4},{1,5},{2,6},{3,7},{4,0},{5,1},{6,2},{7,3},{8,12},{9,13},{10,... | collective-permute-start | bytes 2359304 | tf_op jit(solution)/shard_map/ppermute | solution.py:362
  77.2 5.7 %collective-permute-start.11 = (bf16[512,3072]{1,0:T(8,128)(2,1)S(1)}, bf16[512,3072]{1,0:T(8,128)(2,1)S(1)}, u32[]{:S(2)}, u32[]{:S(2)}) collective-permute-start(bf16[512,3072]{1,0:T(8,128)(2,1)S(1)} %stack.1.this_ref), channel_id=1, source_target_pairs={{0,1},{1,0},{2,3},{3,2},{4,5},{5,4},{6,7},{7,6},{8,9},{9,8},{10,11... | collective-permute-start | bytes 9437192 | tf_op jit(solution)/shard_map/ppermute | solution.py:362
  77.2 11.1 %collective-permute-start.18 = (bf16[1024,512]{1,0:T(8,128)(2,1)S(1)}, bf16[1024,512]{1,0:T(8,128)(2,1)S(1)}, u32[]{:S(2)}, u32[]{:S(2)}) collective-permute-start(bf16[1024,512]{1,0:T(8,128)(2,1)S(1)} %collective-permute-done.10.refs_1_), channel_id=1, source_target_pairs={{8,16},{16,8},{9,17},{17,9},{10,18},{18,10},{11,19},{19,11},{12,20... | collective-permute-start | bytes 3145736 | tf_op jit(solution)/shard_map/ppermute | solution.py:379
  86.3 34.5 %collective-permute-start.12 = (bf16[1024,512]{1,0:T(8,128)(2,1)S(1)}, bf16[1024,512]{1,0:T(8,128)(2,1)S(1)}, u32[]{:S(2)}, u32[]{:S(2)}) collective-permute-start(bf16[1024,512]{1,0:T(8,128)(2,1)S(1)} %sum_kernel.6), channel_id=1, source_target_pairs={{8,0},{16,24},{9,1},{17,25},{10,2},{18,26},{11,3},{19,27},{12,4},{... | collective-permute-start | bytes 3145736 | tf_op jit(solution)/shard_map/ppermute | solution.py:388
  87.6 39.7 %collective-permute-start.14 = (bf16[1024,512]{1,0:T(8,128)(2,1)S(1)}, bf16[1024,512]{1,0:T(8,128)(2,1)S(1)}, u32[]{:S(2)}, u32[]{:S(2)}) collective-permute-start(bf16[1024,512]{1,0:T(8,128)(2,1)S(1)} %get-tuple-element.61), channel_id=1, source_target_pairs={{8,16},{16,8},{9,17},{17,9},{10,18},{18,10},{11,19},{19,11},{12,20... | collective-permute-start | bytes 3145736 | tf_op jit(solution)/shard_map/ppermute | solution.py:386
  91.7 51.1 %collective-permute-start.19 = (bf16[1024,512]{1,0:T(8,128)(2,1)S(1)}, bf16[1024,512]{1,0:T(8,128)(2,1)S(1)}, u32[]{:S(2)}, u32[]{:S(2)}) collective-permute-start(bf16[1024,512]{1,0:T(8,128)(2,1)S(1)} %sum_kernel.7), channel_id=1, source_target_pairs={{8,0},{16,24},{9,1},{17,25},{10,2},{18,26},{11,3},{19,27},{12,4},{... | collective-permute-start | bytes 3145736 | tf_op jit(solution)/shard_map/ppermute | solution.py:391
  97.7 48.4 %collective-permute-start.20 = (bf16[1024,512]{1,0:T(8,128)(2,1)S(1)}, bf16[1024,512]{1,0:T(8,128)(2,1)S(1)}, u32[]{:S(2)}, u32[]{:S(2)}) collective-permute-start(bf16[1024,512]{1,0:T(8,128)(2,1)S(1)} %get-tuple-element.73), channel_id=1, source_target_pairs={{8,16},{16,8},{9,17},{17,9},{10,18},{18,10},{11,19},{19,11},{12,20... | collective-permute-start | bytes 3145736 | tf_op jit(solution)/shard_map/ppermute | solution.py:387
  121.1 18.2 %collective-permute-start.13 = (bf16[1024,256]{1,0:T(8,128)(2,1)S(1)}, bf16[1024,256]{1,0:T(8,128)(2,1)S(1)}, u32[]{:S(2)}, u32[]{:S(2)}) collective-permute-start(bf16[1024,256]{1,0:T(8,128)(2,1)S(1)} %get-tuple-element.63.refs_0_), channel_id=1, source_target_pairs={{0,8},{24,16},{1,9},{25,17},{2,10},{26,18},{3,11},{27,19},{4,12},{... | collective-permute-start | bytes 1572872 | tf_op jit(solution)/shard_map/ppermute | solution.py:389
  127.2 23.3 %collective-permute-start.15 = (bf16[1024,256]{1,0:T(8,128)(2,1)S(1)}, bf16[1024,256]{1,0:T(8,128)(2,1)S(1)}, u32[]{:S(2)}, u32[]{:S(2)}) collective-permute-start(bf16[1024,256]{1,0:T(8,128)(2,1)S(1)} %get-tuple-element.65.refs_1_.refs_0_), channel_id=1, source_target_pairs={{0,8},{24,16},{1,9},{25,17},{2,10},{26,18},{3,11},{27,19},{4,12},{... | collective-permute-start | bytes 1572872 | tf_op jit(solution)/shard_map/ppermute | solution.py:390
  139.3 13.3 %collective-permute-start.16 = (bf16[1024,256]{1,0:T(8,128)(2,1)S(1)}, bf16[1024,256]{1,0:T(8,128)(2,1)S(1)}, u32[]{:S(2)}, u32[]{:S(2)}) collective-permute-start(bf16[1024,256]{1,0:T(8,128)(2,1)S(1)} %collective-permute-done.13.refs_2_), channel_id=1, source_target_pairs={{8,16},{16,8},{9,17},{17,9},{10,18},{18,10},{11,19},{19,11},{12,20... | collective-permute-start | bytes 1572872 | tf_op jit(solution)/shard_map/ppermute | solution.py:394
  143.2 16.9 %collective-permute-start.23 = (bf16[1024,256]{1,0:T(8,128)(2,1)S(1)}, bf16[1024,256]{1,0:T(8,128)(2,1)S(1)}, u32[]{:S(2)}, u32[]{:S(2)}) collective-permute-start(bf16[1024,256]{1,0:T(8,128)(2,1)S(1)} %get-tuple-element.81.refs_0_), channel_id=1, source_target_pairs={{0,8},{24,16},{1,9},{25,17},{2,10},{26,18},{3,11},{27,19},{4,12},{... | collective-permute-start | bytes 1572872 | tf_op jit(solution)/shard_map/ppermute | solution.py:392
  150.6 23.4 %collective-permute-start.17 = (bf16[1024,256]{1,0:T(8,128)(2,1)S(1)}, bf16[1024,256]{1,0:T(8,128)(2,1)S(1)}, u32[]{:S(2)}, u32[]{:S(2)}) collective-permute-start(bf16[1024,256]{1,0:T(8,128)(2,1)S(1)} %collective-permute-done.15.refs_3_), channel_id=1, source_target_pairs={{8,16},{16,8},{9,17},{17,9},{10,18},{18,10},{11,19},{19,11},{12,20... | collective-permute-start | bytes 1572872 | tf_op jit(solution)/shard_map/ppermute | solution.py:395
  151.2 33.4 %collective-permute-start.21 = (f32[1024,256]{1,0:T(8,128)S(1)}, f32[1024,256]{1,0:T(8,128)S(1)}, u32[]{:S(2)}, u32[]{:S(2)}) collective-permute-start(f32[1024,256]{1,0:T(8,128)S(1)} %get-tuple-element.74), channel_id=1, source_target_pairs={{0,1},{1,2},{2,3},{3,4},{4,5},{5,6},{6,7},{8,9},{9,10},{10,11},{11... | collective-permute-start | bytes 3145736 | tf_op jit(solution)/shard_map/ppermute | solution.py:402
  154.4 28.2 %collective-permute-start.27 = (bf16[1024,256]{1,0:T(8,128)(2,1)S(1)}, bf16[1024,256]{1,0:T(8,128)(2,1)S(1)}, u32[]{:S(2)}, u32[]{:S(2)}) collective-permute-start(bf16[1024,256]{1,0:T(8,128)(2,1)S(1)} %sum_kernel.10), channel_id=1, source_target_pairs={{8,0},{16,24},{9,1},{17,25},{10,2},{18,26},{11,3},{19,27},{12,4},{... | collective-permute-start | bytes 1572872 | tf_op jit(solution)/shard_map/ppermute | solution.py:399
  160.1 23.9 %collective-permute-start.25 = (bf16[1024,256]{1,0:T(8,128)(2,1)S(1)}, bf16[1024,256]{1,0:T(8,128)(2,1)S(1)}, u32[]{:S(2)}, u32[]{:S(2)}) collective-permute-start(bf16[1024,256]{1,0:T(8,128)(2,1)S(1)} %get-tuple-element.89.refs_1_.refs_0_), channel_id=1, source_target_pairs={{0,8},{24,16},{1,9},{25,17},{2,10},{26,18},{3,11},{27,19},{4,12},{... | collective-permute-start | bytes 1572872 | tf_op jit(solution)/shard_map/ppermute | solution.py:393
  173.2 10.7 %collective-permute-start.24 = (bf16[1024,256]{1,0:T(8,128)(2,1)S(1)}, bf16[1024,256]{1,0:T(8,128)(2,1)S(1)}, u32[]{:S(2)}, u32[]{:S(2)}) collective-permute-start(bf16[1024,256]{1,0:T(8,128)(2,1)S(1)} %collective-permute-done.23.refs_2_), channel_id=1, source_target_pairs={{8,16},{16,8},{9,17},{17,9},{10,18},{18,10},{11,19},{19,11},{12,20... | collective-permute-start | bytes 1572872 | tf_op jit(solution)/shard_map/ppermute | solution.py:405
  174.0 24.4 %collective-permute-start.22 = (f32[1024,256]{1,0:T(8,128)S(1)}, f32[1024,256]{1,0:T(8,128)S(1)}, u32[]{:S(2)}, u32[]{:S(2)}) collective-permute-start(f32[1024,256]{1,0:T(8,128)S(1)} %get-tuple-element.76), channel_id=1, source_target_pairs={{1,0},{2,1},{3,2},{4,3},{5,4},{6,5},{7,6},{9,8},{10,9},{11,10},{12... | collective-permute-start | bytes 3145736 | tf_op jit(solution)/shard_map/ppermute | solution.py:403
  182.7 14.4 %collective-permute-start.28 = (bf16[1024,256]{1,0:T(8,128)(2,1)S(1)}, bf16[1024,256]{1,0:T(8,128)(2,1)S(1)}, u32[]{:S(2)}, u32[]{:S(2)}) collective-permute-start(bf16[1024,256]{1,0:T(8,128)(2,1)S(1)} %sum_kernel.8), channel_id=1, source_target_pairs={{8,0},{16,24},{9,1},{17,25},{10,2},{18,26},{11,3},{19,27},{12,4},{... | collective-permute-start | bytes 1572872 | tf_op jit(solution)/shard_map/ppermute | solution.py:401
  184.0 20.7 %collective-permute-start.26 = (bf16[1024,256]{1,0:T(8,128)(2,1)S(1)}, bf16[1024,256]{1,0:T(8,128)(2,1)S(1)}, u32[]{:S(2)}, u32[]{:S(2)}) collective-permute-start(bf16[1024,256]{1,0:T(8,128)(2,1)S(1)} %collective-permute-done.25.refs_3_), channel_id=1, source_target_pairs={{8,16},{16,8},{9,17},{17,9},{10,18},{18,10},{11,19},{19,11},{12,20... | collective-permute-start | bytes 1572872 | tf_op jit(solution)/shard_map/ppermute | solution.py:406
  197.1 13.5 %collective-permute-start.29 = (bf16[1024,256]{1,0:T(8,128)(2,1)S(1)}, bf16[1024,256]{1,0:T(8,128)(2,1)S(1)}, u32[]{:S(2)}, u32[]{:S(2)}) collective-permute-start(bf16[1024,256]{1,0:T(8,128)(2,1)S(1)} %sum_kernel.9), channel_id=1, source_target_pairs={{8,0},{16,24},{9,1},{17,25},{10,2},{18,26},{11,3},{19,27},{12,4},{... | collective-permute-start | bytes 1572872 | tf_op jit(solution)/shard_map/ppermute | solution.py:408
  210.6 12.6 %collective-permute-start.30 = (bf16[1024,256]{1,0:T(8,128)(2,1)S(1)}, bf16[1024,256]{1,0:T(8,128)(2,1)S(1)}, u32[]{:S(2)}, u32[]{:S(2)}) collective-permute-start(bf16[1024,256]{1,0:T(8,128)(2,1)S(1)} %sum_kernel.11), channel_id=1, source_target_pairs={{8,0},{16,24},{9,1},{17,25},{10,2},{18,26},{11,3},{19,27},{12,4},{... | collective-permute-start | bytes 1572872 | tf_op jit(solution)/shard_map/ppermute | solution.py:411
  (3 other events, 53.4 us)
